TPU v7x, 32 devices: a whole 2x2x4 slice. The times are simulated.
32 devices in a mesh: dp: 8 (over y, x, core), tp: 4 (over z).
Axes of the slice: x: 2, y: 2, z: 4, core: 2. Of those that a mesh axis runs over, the one named last changes fastest.
Arguments:
- tokens: bfloat16 [8, 1024, 768], P('dp', 'tp')
- w_qkv: bfloat16 [768, 2304], replicated, may hold values from -0.21875 to 0.21875
- bias_query: bfloat16 [768], replicated, may hold values from -1.5 to 1.5
- bias_value: bfloat16 [768], replicated, may hold values from -1.5 to 1.5
- w_out: bfloat16 [768, 768], replicated, may hold values from -1.25 to 1.25
- bias_out: bfloat16 [768], replicated, may hold values from -1.5 to 1.5
- gain_attn: bfloat16 [768], replicated, may hold values from 0.25 to 1.75
- shift_attn: bfloat16 [768], replicated, may hold values from -1.5 to 1.5
- w_in: bfloat16 [768, 3072], P(None, 'tp'), may hold values from -0.21875 to 0.21875
- bias_in: bfloat16 [3072], P('tp'), may hold values from -1.5 to 1.5
- w_back: bfloat16 [3072, 768], P('tp'), may hold values from -0.109375 to 0.109375
- bias_back: bfloat16 [768], replicated, may hold values from -1.5 to 1.5
- gain_ffn: bfloat16 [768], replicated, may hold values from 0.25 to 1.75
- shift_ffn: bfloat16 [768], replicated, may hold values from -1.5 to 1.5
- random_blocks: int32 [8, 12, 16, 3], P('dp'), may hold values from 1 to 14, as said below
- cotangent: bfloat16 [8, 1024, 768], P('dp', 'tp'), may hold values from -6 to 6
Outputs:
- layer_out: bfloat16 [8, 1024, 768], P('dp', 'tp')
- grad_tokens: bfloat16 [8, 1024, 768], P('dp', 'tp')
- grad_w_qkv: float32 [768, 2304], replicated
- grad_bias_query: float32 [768], replicated
- grad_bias_value: float32 [768], replicated
- grad_w_out: float32 [768, 768], replicated
- grad_bias_out: float32 [768], replicated
- grad_gain_attn: float32 [768], replicated
- grad_shift_attn: float32 [768], replicated
- grad_w_in: float32 [768, 3072], P(None, 'tp')
- grad_bias_in: float32 [3072], P('tp')
- grad_w_back: float32 [3072, 768], P('tp')
- grad_bias_back: float32 [768], replicated
- grad_gain_ffn: float32 [768], replicated
- grad_shift_ffn: float32 [768], replicated
Inputs may be any that keep to these rules, and one draw needn't show every extreme that they name: `random_blocks`: for each sequence, head and query block i, the 3 entries are different block numbers, none of them 0, 15, i - 1, i or i + 1.
All inputs are finite; a program needn't handle non-finite values.
Results may differ from a plain program's by a relative error of at most 0.017.
Values may be sent and summed in bfloat16 or wider, within the bound.
No kernel may reach another device: no remote copies, remote signals or barrier semaphores. Data moves between devices by JAX's collectives and lax.ppermute only.
A program may use at most 192 MiB of HBM per device.

v0:
```python
import jax
import jax.numpy as jnp
from jax import lax
from jax.sharding import PartitionSpec as P

HEADS = 12
BLOCK = 64


epsilon = 1e-05
masked_score = -1e30


def normalize(hidden_in, gain_vec, shift_vec):
    row_mean = jnp.mean(hidden_in, axis=-1, keepdims=True)
    centred = hidden_in - row_mean
    variance = jnp.mean(centred * centred, axis=-1, keepdims=True)
    return centred * lax.rsqrt(variance + epsilon) * gain_vec + shift_vec


def contract_rows(left, right):
    return lax.dot_general(
        left, right, (((0,), (0,)), ((), ())), preferred_element_type=jnp.float32
    )


def times_transposed(left, right):
    return lax.dot_general(
        left, right, (((1,), (1,)), ((), ())), preferred_element_type=jnp.float32
    )


def to_heads(flat_rows):
    rows_count, model_width = flat_rows.shape
    shaped = flat_rows.reshape(rows_count // BLOCK, BLOCK, HEADS, model_width // HEADS)
    return shaped.transpose(2, 0, 1, 3)


def from_heads(blocked):
    heads_count, blocks_count, block_rows, head_dim = blocked.shape
    return blocked.transpose(1, 2, 0, 3).reshape(blocks_count * block_rows, heads_count * head_dim)


def block_lists(random_rows, first_block, local_blocks, total_blocks):
    block_ids = first_block + jnp.arange(local_blocks, dtype=jnp.int32)
    before_ids = block_ids - 1
    after_ids = block_ids + 1
    fixed_ids = jnp.stack(
        [
            jnp.zeros_like(block_ids),
            jnp.full_like(block_ids, total_blocks - 1),
            before_ids,
            block_ids,
            after_ids,
        ],
        axis=-1,
    )
    fixed_ok = jnp.stack(
        [
            block_ids >= 0,
            block_ids >= 0,
            before_ids >= 1,
            (block_ids >= 1) & (block_ids <= total_blocks - 2),
            after_ids <= total_blocks - 2,
        ],
        axis=-1,
    )
    fixed_ids = jnp.clip(fixed_ids, 0, total_blocks - 1)
    heads_count = random_rows.shape[0]
    key_lists = jnp.concatenate(
        [jnp.broadcast_to(fixed_ids[None], (heads_count,) + fixed_ids.shape), random_rows], axis=-1
    )
    key_valid = jnp.concatenate([fixed_ok, jnp.ones(random_rows.shape[1:], jnp.bool_)], axis=-1)
    return (key_lists, key_valid)


def flat_pick(blocks, key_lists):
    picked = jax.vmap(lambda block_set, index_set: block_set[index_set])(blocks, key_lists)
    heads_count, local_blocks, picks_count, block_rows, head_dim = picked.shape
    return picked.reshape(heads_count, local_blocks, picks_count * block_rows, head_dim)


def add_to_blocks(picked_rows, block_index, total_blocks):
    start_rows = jnp.zeros((total_blocks, picked_rows.shape[-1]), jnp.float32)
    return start_rows.at[block_index].add(picked_rows)


def log_total(scores):
    row_max = jnp.max(scores, axis=-1, keepdims=True)
    return row_max + jnp.log(jnp.sum(jnp.exp(scores - row_max), axis=-1, keepdims=True))


def per_device(
    tokens,
    w_qkv,
    bias_query,
    bias_value,
    w_out,
    bias_out,
    gain_attn,
    shift_attn,
    w_in,
    bias_in,
    w_back,
    bias_back,
    gain_ffn,
    shift_ffn,
    random_blocks,
    cotangent,
):
    token_rows = tokens[0]
    rows_here, model_width = token_rows.shape
    head_dim = model_width // HEADS
    score_scale = head_dim ** (-0.5)
    tp_count = lax.axis_size("tp")
    tp_rank = lax.axis_index("tp")
    local_blocks = rows_here // BLOCK
    total_blocks = local_blocks * tp_count
    first_block = tp_rank * local_blocks
    is_global = (tp_rank == 0) | (tp_rank == tp_count - 1)
    chosen = jnp.where(tp_rank == 0, 0, local_blocks - 1).astype(jnp.int32)
    selected = (jnp.arange(local_blocks, dtype=jnp.int32) == chosen) & is_global
    select_mask = selected[None, :, None, None]
    gain_one = gain_attn.astype(jnp.float32)
    shift_one = shift_attn.astype(jnp.float32)
    gain_two = gain_ffn.astype(jnp.float32)
    shift_two = shift_ffn.astype(jnp.float32)
    projected = jnp.dot(token_rows, w_qkv, preferred_element_type=jnp.float32)
    queries = (projected[:, :model_width] + bias_query.astype(jnp.float32)).astype(jnp.bfloat16)
    keys_here = projected[:, model_width : 2 * model_width].astype(jnp.bfloat16)
    values_here = (projected[:, 2 * model_width :] + bias_value.astype(jnp.float32)).astype(
        jnp.bfloat16
    )
    keys_all, values_all = (
        lax.all_gather(keys_here, "tp", axis=0, tiled=True),
        lax.all_gather(values_here, "tp", axis=0, tiled=True),
    )
    query_blocks = to_heads(queries)
    key_heads = to_heads(keys_all)
    value_heads = to_heads(values_all)
    full_keys = key_heads.reshape(HEADS, total_blocks * BLOCK, head_dim)
    full_values = value_heads.reshape(HEADS, total_blocks * BLOCK, head_dim)
    random_rows = lax.dynamic_slice_in_dim(random_blocks[0], first_block, local_blocks, 1)
    key_lists, key_valid = block_lists(random_rows, first_block, local_blocks, total_blocks)
    picks_count = key_lists.shape[-1]
    keep_mask = jnp.repeat(key_valid, BLOCK, axis=-1)[None, :, None, :]
    picked_keys = flat_pick(key_heads, key_lists)
    picked_values = flat_pick(value_heads, key_lists)
    global_query = lax.dynamic_index_in_dim(query_blocks, chosen, 1, keepdims=False)

    def sparse_scores():
        raw_scores = jnp.einsum(
            "hqbe,hqje->hqbj", query_blocks, picked_keys, preferred_element_type=jnp.float32
        )
        return jnp.where(keep_mask, score_scale * raw_scores, masked_score)

    def global_scores():
        return score_scale * jnp.einsum(
            "hbe,hje->hbj", global_query, full_keys, preferred_element_type=jnp.float32
        )

    scores = sparse_scores()
    sparse_total = log_total(scores)
    sparse_low = jnp.exp(scores - sparse_total).astype(jnp.bfloat16)
    sparse_out = jnp.einsum(
        "hqbj,hqje->hqbe", sparse_low, picked_values, preferred_element_type=jnp.float32
    )
    wide_scores = global_scores()
    global_total = log_total(wide_scores)
    global_low = jnp.exp(wide_scores - global_total).astype(jnp.bfloat16)
    global_out = jnp.einsum(
        "hbj,hje->hbe", global_low, full_values, preferred_element_type=jnp.float32
    )
    attended = jnp.where(select_mask, global_out[:, None], sparse_out)
    attended_low = from_heads(attended).astype(jnp.bfloat16)
    mixed_out = jnp.dot(attended_low, w_out, preferred_element_type=jnp.float32) + bias_out.astype(
        jnp.float32
    )
    first_in = token_rows.astype(jnp.float32) + mixed_out
    first_norm, first_back = jax.vjp(normalize, first_in, gain_one, shift_one)
    ffn_input = first_norm.astype(jnp.bfloat16)
    ffn_rows = lax.all_gather(ffn_input, "tp", axis=0, tiled=True)
    pre_act = jnp.dot(ffn_rows, w_in, preferred_element_type=jnp.float32) + bias_in.astype(
        jnp.float32
    )
    activated, gelu_back = jax.vjp(jax.nn.gelu, pre_act)
    activated_low = activated.astype(jnp.bfloat16)
    branch = lax.psum_scatter(
        jnp.dot(activated_low, w_back, preferred_element_type=jnp.float32).astype(jnp.bfloat16),
        "tp",
        scatter_dimension=0,
        tiled=True,
    ).astype(jnp.float32)
    second_in = first_norm + branch + bias_back.astype(jnp.float32)
    second_out, second_back = jax.vjp(normalize, second_in, gain_two, shift_two)
    layer_out = second_out.astype(jnp.bfloat16)[None]
    grad_out = cotangent[0].astype(jnp.float32)
    grad_second, grad_gain_two, grad_shift_two = second_back(grad_out)
    grad_branch = grad_second.astype(jnp.bfloat16)
    grad_bias_two = jnp.sum(grad_branch.astype(jnp.float32), axis=0)
    branch_rows = lax.all_gather(grad_branch, "tp", axis=0, tiled=True)
    grad_act = times_transposed(branch_rows, w_back)
    grad_w_back = contract_rows(activated_low, branch_rows)
    grad_pre = gelu_back(grad_act)[0].astype(jnp.bfloat16)
    grad_bias_in = jnp.sum(grad_pre.astype(jnp.float32), axis=0)
    grad_w_in = contract_rows(ffn_rows, grad_pre)
    grad_ffn_input = lax.psum_scatter(
        times_transposed(grad_pre, w_in), "tp", scatter_dimension=0, tiled=True
    )
    grad_first = grad_second + grad_ffn_input
    grad_first_in, grad_gain_one, grad_shift_one = first_back(grad_first)
    grad_mixed = grad_first_in.astype(jnp.bfloat16)
    grad_bias_out = jnp.sum(grad_mixed.astype(jnp.float32), axis=0)
    grad_w_out = contract_rows(attended_low, grad_mixed)
    grad_attended = times_transposed(grad_mixed, w_out).astype(jnp.bfloat16)
    grad_blocks = to_heads(grad_attended)
    grad_sparse = jnp.where(select_mask, jnp.zeros_like(grad_blocks), grad_blocks)
    again_scores = sparse_scores()
    sparse_probs = jnp.exp(again_scores - sparse_total)
    sparse_again = sparse_probs.astype(jnp.bfloat16)
    grad_probs = jnp.einsum(
        "hqbe,hqje->hqbj", grad_sparse, picked_values, preferred_element_type=jnp.float32
    )
    grad_scores = (
        sparse_probs * (grad_probs - jnp.sum(grad_probs * sparse_probs, axis=-1, keepdims=True))
    ).astype(jnp.bfloat16)
    grad_query_sparse = score_scale * jnp.einsum(
        "hqbj,hqje->hqbe", grad_scores, picked_keys, preferred_element_type=jnp.float32
    )
    grad_keys_picked = score_scale * jnp.einsum(
        "hqbj,hqbe->hqje", grad_scores, query_blocks, preferred_element_type=jnp.float32
    )
    grad_values_picked = jnp.einsum(
        "hqbj,hqbe->hqje", sparse_again, grad_sparse, preferred_element_type=jnp.float32
    )
    both_picked = jnp.concatenate(
        [
            grad_keys_picked.reshape(HEADS, local_blocks * picks_count, BLOCK * head_dim),
            grad_values_picked.reshape(HEADS, local_blocks * picks_count, BLOCK * head_dim),
        ],
        axis=-1,
    )
    flat_lists = key_lists.reshape(HEADS, local_blocks * picks_count)
    both_blocks = jax.vmap(
        lambda rows_one, index_one: add_to_blocks(rows_one, index_one, total_blocks)
    )(both_picked, flat_lists)
    keys_from_blocks = both_blocks[:, :, : BLOCK * head_dim].reshape(
        HEADS, total_blocks * BLOCK, head_dim
    )
    values_from_blocks = both_blocks[:, :, BLOCK * head_dim :].reshape(
        HEADS, total_blocks * BLOCK, head_dim
    )
    grad_global = lax.dynamic_index_in_dim(grad_blocks, chosen, 1, keepdims=False)
    grad_global = jnp.where(is_global, grad_global, jnp.zeros_like(grad_global))
    wide_again = global_scores()
    global_probs = jnp.exp(wide_again - global_total)
    grad_wide = jnp.einsum(
        "hbe,hje->hbj", grad_global, full_values, preferred_element_type=jnp.float32
    )
    grad_wide_scores = (
        global_probs * (grad_wide - jnp.sum(grad_wide * global_probs, axis=-1, keepdims=True))
    ).astype(jnp.bfloat16)
    grad_query_global = score_scale * jnp.einsum(
        "hbj,hje->hbe", grad_wide_scores, full_keys, preferred_element_type=jnp.float32
    )
    grad_keys_full = keys_from_blocks + score_scale * jnp.einsum(
        "hbj,hbe->hje", grad_wide_scores, global_query, preferred_element_type=jnp.float32
    )
    grad_values_full = values_from_blocks + jnp.einsum(
        "hbj,hbe->hje",
        global_probs.astype(jnp.bfloat16),
        grad_global,
        preferred_element_type=jnp.float32,
    )
    grad_query_blocks = grad_query_sparse + jnp.where(select_mask, grad_query_global[:, None], 0.0)
    keys_rows = from_heads(grad_keys_full.reshape(HEADS, total_blocks, BLOCK, head_dim))
    values_rows = from_heads(grad_values_full.reshape(HEADS, total_blocks, BLOCK, head_dim))
    key_grads, value_grads = (
        lax.psum_scatter(
            keys_rows.astype(jnp.bfloat16), "tp", scatter_dimension=0, tiled=True
        ).astype(jnp.float32),
        lax.psum_scatter(
            values_rows.astype(jnp.bfloat16), "tp", scatter_dimension=0, tiled=True
        ).astype(jnp.float32),
    )
    query_low = from_heads(grad_query_blocks).astype(jnp.bfloat16)
    key_low = key_grads.astype(jnp.bfloat16)
    value_low = value_grads.astype(jnp.bfloat16)
    grad_qkv = jnp.concatenate([query_low, key_low, value_low], axis=1)
    grad_w_qkv = contract_rows(token_rows, grad_qkv)
    grad_bias_query = jnp.sum(query_low.astype(jnp.float32), axis=0)
    grad_bias_value = jnp.sum(value_low.astype(jnp.float32), axis=0)
    grad_tokens = (grad_first_in + times_transposed(grad_qkv, w_qkv)).astype(jnp.bfloat16)[None]
    (
        sum_w_qkv,
        sum_bias_query,
        sum_bias_value,
        sum_w_out,
        sum_bias_out,
        sum_gain_one,
        sum_shift_one,
        sum_gain_two,
        sum_shift_two,
        sum_bias_two,
    ) = lax.psum(
        (
            grad_w_qkv,
            grad_bias_query,
            grad_bias_value,
            grad_w_out,
            grad_bias_out,
            grad_gain_one,
            grad_shift_one,
            grad_gain_two,
            grad_shift_two,
            grad_bias_two,
        ),
        ("dp", "tp"),
    )
    sum_w_in, sum_bias_in, sum_w_back = lax.psum((grad_w_in, grad_bias_in, grad_w_back), "dp")
    return (
        layer_out,
        grad_tokens,
        sum_w_qkv,
        sum_bias_query,
        sum_bias_value,
        sum_w_out,
        sum_bias_out,
        sum_gain_one,
        sum_shift_one,
        sum_w_in,
        sum_bias_in,
        sum_w_back,
        sum_bias_two,
        sum_gain_two,
        sum_shift_two,
    )


def solution(mesh):
    in_specs = (
        P("dp", "tp", None),
        P(),
        P(),
        P(),
        P(),
        P(),
        P(),
        P(),
        P(None, "tp"),
        P("tp"),
        P("tp", None),
        P(),
        P(),
        P(),
        P("dp", None, None, None),
        P("dp", "tp", None),
    )
    out_specs = (
        P("dp", "tp", None),
        P("dp", "tp", None),
        P(),
        P(),
        P(),
        P(),
        P(),
        P(),
        P(),
        P(None, "tp"),
        P("tp"),
        P("tp", None),
        P(),
        P(),
        P(),
    )
    return jax.shard_map(
        per_device, mesh=mesh, in_specs=in_specs, out_specs=out_specs, check_vma=False
    )
```

profile of v0, /device:TPU:1, one launch (start us, length us, event | category | flops | bytes accessed | tf_op | source)
XLA Modules:
  0.0 1042.9 jit_solution(3385208644554820574)
XLA Ops:
  38.8 13.9 %all-gather.5.cloned.1.call-done = bf16[1024,768]{1,0:T(8,128)(2,1)} async-done(((bf16[256,768]{1,0:T(8,128)(2,1)}), bf16[1024,768]{1,0:T(8,128)(2,1)}) %all-gather.5.cloned.1.call-update) | async-done | bytes 1572880 | tf_op jit(solution)/shard_map/all_gather | solution.py:135
  52.7 5.9 reshape.375
  58.6 4.7 copy.104
  63.3 5.3 copy.81
  68.5 22.3 %all-gather.7.cloned.1.call-done = bf16[1024,768]{1,0:T(8,128)(2,1)} async-done(((bf16[256,768]{1,0:T(8,128)(2,1)}), bf16[1024,768]{1,0:T(8,128)(2,1)}) %all-gather.7.cloned.1.call-update) | async-done | bytes 1572880 | tf_op jit(solution)/shard_map/all_gather | solution.py:136
  90.8 5.9 reshape.376
  96.7 4.7 copy.103
  101.4 5.4 copy.85
  106.9 6.4 gather_fusion.1
  113.3 6.3 gather_fusion
  144.6 34.4 %all-gather.9.cloned.1.call-done = bf16[1024,768]{1,0:T(8,128)(2,1)} async-done(((bf16[256,768]{1,0:T(8,128)(2,1)}), bf16[1024,768]{1,0:T(8,128)(2,1)}) %all-gather.9.cloned.1.call-update) | async-done | bytes 1572880 | tf_op jit(solution)/shard_map/all_gather | solution.py:182
  191.0 30.4 %reduce-scatter.5.cloned.1.call-done = bf16[256,768]{1,0:T(8,128)(2,1)} async-done(((bf16[1024,768]{1,0:T(8,128)(2,1)}), bf16[256,768]{1,0:T(8,128)(2,1)}) %reduce-scatter.5.cloned.1.call-update) | async-done | bytes 393232 | tf_op jit(solution)/shard_map/reduce_scatter | solution.py:188
  228.9 36.2 %all-gather.11.cloned.1.call-done = bf16[1024,768]{1,0:T(8,128)(2,1)} async-done(((bf16[256,768]{1,0:T(8,128)(2,1)}), bf16[1024,768]{1,0:T(8,128)(2,1)}) %all-gather.11.cloned.1.call-update) | async-done | bytes 1572880 | tf_op jit(solution)/shard_map/all_gather | solution.py:201
  265.1 6.4 convert_reduce_fusion
  280.9 54.2 %reduce-scatter.7.cloned.1.call-done = f32[256,768]{1,0:T(8,128)} async-done(((f32[1024,768]{1,0:T(8,128)}), f32[256,768]{1,0:T(8,128)}) %reduce-scatter.7.cloned.1.call-update) | async-done | bytes 786448 | tf_op jit(solution)/shard_map/reduce_scatter | solution.py:207
  352.4 11.0 %multiply_reduce_fusion = (f32[12,4,64]{2,1,0:T(4,128)}, f32[12,4,64,512]{3,2,1,0:T(8,128)}) fusion(f32[12,4,64,512]{3,2,1,0:T(8,128)} %copy-done.1, f32[12,4,64]{2,1,0:T(4,128)} %bitcast.174, pred[4,512]{1,0:T(4,128)(4,1)S(1)} %copy-done.28, bf16[12,4,512,64]{3,2,1,0:T(8,128)(2,1)} %bitcast.165, bf16[4,64,12,64]{3,1,0,2:T(8,128)(2,1)} %copy.57, ...), kind=kOutput, calls=%fused_computation.5 | convolution fusion | flops 209384448 | bytes 16148484 | tf_op jit(solution)/shard_map/hqbe,hqje->hqbj/dot_general | solution.py:221
  363.4 10.0 fusion.24
  375.2 5.6 multiply_reduce_fusion.1
  380.8 3.8 multiply_convert_fusion
  386.4 3.6 broadcast_multiply_fusion
  390.0 10.8 %reshape.352 = f32[12,32,4096]{2,1,0:T(8,128)} reshape(f32[12,4,512,64]{3,2,1,0:T(8,128)} %fusion.24) | data formatting | bytes 12582912 | tf_op jit(solution)/shard_map/reshape | solution.py:239
  400.8 9.6 copy.66
  410.3 10.9 %reshape.351 = f32[12,32,4096]{2,1,0:T(8,128)} reshape(f32[12,4,512,64]{3,2,1,0:T(8,128)} %copy.66) | data formatting | bytes 12582912 | tf_op jit(solution)/shard_map/reshape | solution.py:238
  421.2 10.6 %pad_maximum_fusion = f32[12,32,8192]{2,1,0:T(8,128)} fusion(f32[12,32,4096]{2,1,0:T(8,128)} %reshape.352, f32[12,32,4096]{2,1,0:T(8,128)} %reshape.351), kind=kLoop, calls=%fused_computation.3 | loop fusion | flops 3145728 | bytes 25165824 | tf_op jit(solution)/shard_map/concatenate | solution.py:236
  431.8 3.4 broadcast_in_dim.140
  435.2 196.5 %scatter_fusion = f32[12,16,8192]{2,1,0:T(8,128)} fusion(f32[12,16,8192]{2,1,0:T(8,128)} %broadcast_in_dim.140, s32[384]{0:T(512)S(1)} %reshape.367, f32[384,8192]{1,0:T(8,128)} %bitcast.160), kind=kCustom, calls=%fused_computation.2 | custom fusion | flops 3145728 | bytes 37751808 | tf_op jit(solution)/shard_map/vmap()/scatter-add | solution.py:85
  631.7 6.2 fusion.78
  637.9 6.1 reshape.353
  643.9 6.1 copy.70
  650.1 3.7 multiply_convert_fusion.1
  656.7 5.2 convert_element_type.176
  662.0 5.4 convert_element_type.178
  667.4 6.1 reshape.354
  673.5 6.1 copy.72
  679.6 5.0 add_convert_fusion
  684.7 5.3 convert_element_type.180
  689.9 5.4 convert_element_type.182
  698.3 4.7 convert_reduce_fusion.1
  714.6 23.0 %reduce-scatter.11.cloned.1.call-done = bf16[256,768]{0,1:T(8,128)(2,1)} async-done(((bf16[1024,768]{0,1:T(8,128)(2,1)}), bf16[256,768]{0,1:T(8,128)(2,1)}) %reduce-scatter.11.cloned.1.call-update) | async-done | bytes 393232 | tf_op jit(solution)/shard_map/reduce_scatter | solution.py:282
  739.3 5.4 convolution_bitcast_fusion
  744.8 4.9 fusion.83
  754.7 13.3 %psum.99 = f32[768]{0:T(1024)} all-reduce(f32[768]{0:T(1024)} %get-tuple-element.62), channel_id=1, replica_groups=mesh['dp'=8,'tp'=4] {'dp'}, use_global_device_ids=true, to_apply=%region_33.34 | all-reduce | flops 768 | bytes 6144 | tf_op jit(solution)/shard_map/psum | solution.py:320
  769.9 42.2 %all-reduce = (f32[768]{0:T(1024)}, f32[768]{0:T(1024)}, f32[768]{0:T(1024)}, f32[768]{0:T(1024)}, f32[768]{0:T(1024)}, /*index=5*/f32[768]{0:T(1024)}, f32[768]{0:T(1024)}, f32[768]{0:T(1024)}) all-reduce(f32[768]{0:T(1024)} %reduce_sum.236, f32[768]{0:T(1024)S(1)} %convert_reduce_fusion.5, ...), channel_id=1, replica_groups=mesh['dp'=8,'tp'=4] {'dp','tp'}, use_global_device_ids=true, to_apply=%region_21.22 | all-reduce | flops 6144 | bytes 49152 | tf_op jit(solution)/shard_map/psum | solution.py:305
  812.1 3.4 fusion.14
  815.5 121.1 %all-reduce.6.cloned.1.call-done = (f32[768,2304]{0,1:T(8,128)}, f32[768,768]{1,0:T(8,128)}) async-done(((f32[768,2304]{0,1:T(8,128)}, f32[768,768]{1,0:T(8,128)}), (f32[768,2304]{0,1:T(8,128)}, f32[768,768]{1,0:T(8,128)})) %all-reduce.6.cloned.1.call-update) | async-done | bytes 9437200 | tf_op jit(solution)/shard_map/psum | solution.py:305
  936.6 8.0 copy.73
  944.5 83.8 %all-reduce.8.cloned.1.call-done = (f32[768,768]{1,0:T(8,128)}, f32[768,768]{1,0:T(8,128)}) async-done(((f32[768,768]{1,0:T(8,128)}, f32[768,768]{1,0:T(8,128)}), (f32[768,768]{1,0:T(8,128)}, f32[768,768]{1,0:T(8,128)})) %all-reduce.8.cloned.1.call-update) | async-done | bytes 4718608 | tf_op jit(solution)/shard_map/psum | solution.py:320
  1028.3 3.4 copy.112
  (235 shorter events, 136.0 us)
Async XLA Ops:
  7.2 6.4 copy-start.47
  7.2 6.4 copy-start.48
  7.2 45.5 %all-gather.5.cloned.1.call-start = ((), (), s32[]{:S(2)}) async-start(), calls=%async_computation.4 | async-start | bytes 1966080 | tf_op jit(solution)/shard_map/all_gather | solution.py:135
  12.7 5.9 copy-start.49
  13.5 77.3 %all-gather.7.cloned.1.call-start = ((), (), s32[]{:S(2)}) async-start(), calls=%async_computation.5 | async-start | bytes 1966080 | tf_op jit(solution)/shard_map/all_gather | solution.py:136
  16.0 163.0 %all-gather.9.cloned.1.call-start = ((), (), s32[]{:S(2)}) async-start(), calls=%async_computation.6 | async-start | bytes 1966080 | tf_op jit(solution)/shard_map/all_gather | solution.py:182
  119.6 3.1 copy-start.9
  119.6 4.0 slice-start
  121.9 3.0 slice-start.1
  122.7 7.2 slice-start.2
  124.9 5.0 slice-start.3
  127.3 2.6 copy-start.40
  129.9 7.7 copy-start.34
  139.7 81.6 %copy-start.29 = (f32[256]{0:T(256)}, f32[256]{0:T(256)S(1)}, u32[]{:S(2)}) copy-start(f32[256]{0:T(256)S(1)} %broadcast_multiply_fusion.2) | copy-start | bytes 3076
  142.8 78.5 %reduce-scatter.5.cloned.1.call-start = ((), (), s32[]{:S(2)}) async-start(), calls=%async_computation.7 | async-start | bytes 1966080 | tf_op jit(solution)/shard_map/reduce_scatter | solution.py:188
  179.0 4.9 copy-start.43
  179.0 4.9 copy-start.51
  187.1 78.0 %all-gather.11.cloned.1.call-start = ((), (), s32[]{:S(2)}) async-start(), calls=%async_computation.8 | async-start | bytes 1966080 | tf_op jit(solution)/shard_map/all_gather | solution.py:201
  221.4 4.0 copy-start.17
  221.4 4.0 copy-start.30
  221.4 4.0 copy-start.35
  223.1 42.0 %copy-start.44 = (f32[768]{0:T(1024)S(1)}, f32[768]{0:T(1024)}, u32[]{:S(2)}) copy-start(f32[768]{0:T(1024)} %convert_element_type.157) | copy-start | bytes 9220
  228.9 106.2 %reduce-scatter.7.cloned.1.call-start = ((), (), s32[]{:S(2)}) async-start(), calls=%async_computation.9 | async-start | bytes 3932160 | tf_op jit(solution)/shard_map/reduce_scatter | solution.py:207
  265.1 7.6 copy-start.52
  275.9 436.9 %reduce-scatter.9.cloned.1.call-start = ((), (), s32[]{:S(2)}) async-start(), calls=%async_computation.10 | async-start | bytes 1966080 | tf_op jit(solution)/shard_map/reduce_scatter | solution.py:279
  335.1 3.5 copy-start.6
  335.1 6.9 copy-start.16
  342.0 10.4 copy-start.28
  352.4 11.0 %copy-start.14 = (bf16[4,64,12,64]{3,1,0,2:T(8,128)(2,1)S(1)}, bf16[4,64,12,64]{3,1,0,2:T(8,128)(2,1)}, u32[]{:S(2)}) copy-start(bf16[4,64,12,64]{3,1,0,2:T(8,128)(2,1)} %copy.57) | copy-start | bytes 1179652
  352.4 11.0 %copy-start.24 = (f32[6,8,64]{2,1,0:T(8,128)S(1)}, f32[6,8,64]{2,1,0:T(8,128)}, u32[]{:S(2)}) copy-start(f32[6,8,64]{2,1,0:T(8,128)} %copy-done.23) | copy-start | bytes 36868
  352.4 11.0 %copy-start.41 = (pred[4]{0:T(512)(128)(4,1)S(1)}, pred[4]{0:T(512)(128)(4,1)}, u32[]{:S(2)}) copy-start(pred[4]{0:T(512)(128)(4,1)} %compare_and_fusion) | copy-start | bytes 16
  375.2 5.6 copy-start.7
  375.2 5.6 copy-start.25
  375.2 5.6 copy-start.26
  380.8 5.6 copy-start.12
  650.1 4.9 copy-start.10
  650.1 4.9 copy-start.22
  667.4 70.2 %reduce-scatter.11.cloned.1.call-start = ((), (), s32[]{:S(2)}) async-start(), calls=%async_computation.11 | async-start | bytes 1966080 | tf_op jit(solution)/shard_map/reduce_scatter | solution.py:282
  695.3 2.7 copy-start.42
  695.4 241.2 %all-reduce.6.cloned.1.call-start = ((), (), s32[]{:S(2)}) async-start(), calls=%async_computation.12 | async-start | bytes 18874368 | tf_op jit(solution)/shard_map/psum | solution.py:305
  695.4 2.9 copy-start.4
  744.7 5.0 copy-start.45
  744.7 283.6 %all-reduce.8.cloned.1.call-start = ((), (), s32[]{:S(2)}) async-start(), calls=%async_computation.13 | async-start | bytes 9437184 | tf_op jit(solution)/shard_map/psum | solution.py:320
  744.8 4.9 copy-start.50
  744.8 4.9 copy-start.54
  753.0 16.8 %copy-start.36 = (f32[768]{0:T(1024)S(1)}, f32[768]{0:T(1024)}, u32[]{:S(2)}) copy-start(f32[768]{0:T(1024)} %get-tuple-element.47) | copy-start | bytes 9220
  753.0 16.8 %copy-start.37 = (f32[768]{0:T(1024)S(1)}, f32[768]{0:T(1024)}, u32[]{:S(2)}) copy-start(f32[768]{0:T(1024)} %get-tuple-element.64) | copy-start | bytes 9220
  1028.3 3.4 copy-start.21
  (22 other events, 32.0 us)
Sparse Core Ops, SparseCore 0:
  13.6 39.0 all-gather.4
  54.8 35.9 all-gather.6
  143.0 35.9 all-gather.8
  187.2 34.0 reduce-scatter.4
  229.0 36.0 all-gather.10
  276.0 59.0 reduce-scatter.6
  667.5 33.4 reduce-scatter.8
  703.2 34.2 reduce-scatter.10
  744.8 191.6 all-reduce.5
  941.3 87.0 all-reduce.7
where the time goes:
time: 1050 us; the launch traced here: 1040 us
  waiting for transfers between devices  419 us (40%)
  other arithmetic  249 us (24%)
  local copies, waits for them, and re-layouts  209 us (20%)
  matrix products  94.2 us (9%)
  blocking collectives  55.5 us (5%)
  between operations  15.2 us (1%)
    scatter-add x2, other arithmetic, add_to_blocks(): return start_rows.at[block_index].add(picked_rows)  198 us
    psum x1, waiting for transfers between devices, per_device(): lax.psum((grad_w_qkv, grad_bias_query, grad_bias_value, grad_w_out, grad_...  121 us
    psum x1, waiting for transfers between devices, per_device(): lax.psum((grad_w_in, grad_bias_in, grad_w_back), 'dp')  83.8 us
    reduce_scatter x1, waiting for transfers between devices, per_device(): lax.psum_scatter(times_transposed(grad_pre, w_in), 'tp', scatter_dimensio...  54.2 us
    psum x1, blocking collectives, per_device(): lax.psum((grad_w_qkv, grad_bias_query, grad_bias_value, grad_w_out, grad_...  42.2 us
    unnamed x128, local copies, waits for them, and re-layouts  38.4 us
    all_gather x1, waiting for transfers between devices, per_device(): branch_rows = lax.all_gather(grad_branch, 'tp', axis=0, tiled=True)  36.2 us
    all_gather x1, waiting for transfers between devices, per_device(): ffn_rows = lax.all_gather(ffn_input, 'tp', axis=0, tiled=True)  34.4 us
  transfers between devices with their start and end apart: 10, of which 9 were waited for; matrix products, arithmetic and copies ran while one was open for 12% of the time, Pallas kernels for 0%

commit v1 on v0

v1 whole, which is shorter than its diff:
```python
import functools

import jax
import jax.numpy as jnp
from jax import lax
from jax.experimental import pallas as pl
from jax.experimental.pallas import tpu as pltpu
from jax.sharding import PartitionSpec as P

HEADS = 12
BLOCK = 64
HEAD_DIM = 64
TP = 4
GROUP = HEADS // TP
QUARTER = 256
LENGTH = TP * QUARTER
WIDTH = HEADS * HEAD_DIM
GROUP_WIDTH = GROUP * HEAD_DIM
SLOTS = 8
SLICE = WIDTH // SLOTS
CORE, X_BIT, Y_BIT = 1, 2, 4
PLANE_MASKS = (0, X_BIT, Y_BIT, X_BIT | Y_BIT)

epsilon = 1e-05
masked_score = -1e30
score_scale = HEAD_DIM ** (-0.5)
f32 = jnp.float32
bf16 = jnp.bfloat16

VMEM_LIMIT = 56 * 1024 * 1024


def mm(left, right):
    return jnp.dot(left, right, preferred_element_type=f32)


def mm_nt(left, right):
    return lax.dot_general(left, right, (((1,), (1,)), ((), ())), preferred_element_type=f32)


def total(*terms):
    acc = terms[0].astype(f32)
    for term in terms[1:]:
        acc = acc + term.astype(f32)
    return acc


def add_low(*terms):
    return total(*terms).astype(bf16)


def hop(array, dp_mask, z_mask):
    dp_count = lax.axis_size("dp")
    pairs = [
        (d * TP + z, (d ^ dp_mask) * TP + (z ^ z_mask)) for d in range(dp_count) for z in range(TP)
    ]
    return lax.ppermute(array, ("dp", "tp"), pairs)


def after(array, *others):
    return lax.optimization_barrier((array, *others))[0]


def place(array):
    dp_count = lax.axis_size("dp")
    pairs = []
    for d in range(dp_count):
        for z in range(TP):
            here = d * TP + z
            away = (d ^ CORE) * TP + (z ^ 2)
            pairs.append((here, here if (d & 1) == z // 2 else away))
    return lax.ppermute(array, ("dp", "tp"), pairs)


def block_bias(quarter, random_ref, head, chunk):
    shape = (LENGTH // BLOCK, QUARTER)
    row = lax.broadcasted_iota(jnp.int32, shape, 0)
    lane_block = lax.broadcasted_iota(jnp.int32, shape, 1) // BLOCK
    key_block = ((row // TP) ^ quarter) * TP + (row % TP)
    base = TP * (quarter ^ chunk)
    query_block = base + lane_block
    last = LENGTH // BLOCK - 1
    allowed = (key_block == 0) | (key_block == last)
    allowed |= (query_block == 0) | (query_block == last)
    allowed |= jnp.abs(key_block - query_block) <= 1
    for pick in range(3):
        chosen = jnp.zeros(shape, jnp.int32)
        for b in range(TP):
            value = random_ref[(head * (LENGTH // BLOCK) + base + b) * 3 + pick]
            chosen = jnp.where(lane_block == b, value, chosen)
        allowed |= key_block == chosen
    return jnp.where(allowed, 0.0, masked_score).astype(f32)


def biased(scores, bias):
    blocks = LENGTH // BLOCK
    spread = scores.reshape(blocks, BLOCK, QUARTER) + bias.reshape(blocks, 1, QUARTER)
    return spread.reshape(LENGTH, QUARTER)


def pack_heads(ref, pieces):
    ref[0:QUARTER, 0:64] = pieces[0]
    ref[0:QUARTER, 64:128] = pieces[1]
    ref[QUARTER:, 0:64] = pieces[2][: QUARTER // 2]
    ref[QUARTER:, 64:128] = pieces[2][QUARTER // 2 :]


def unpack_heads(ref):
    third = jnp.concatenate([ref[QUARTER:, 0:64], ref[QUARTER:, 64:128]], axis=0)
    return [ref[0:QUARTER, 0:64], ref[0:QUARTER, 64:128], third]


def attention_kernel(
    info, random_ref, t0, t1, t2, t3, w_ref, b_ref, a0, a1, a2, a3, q_ref, k_ref, v_ref, lse_ref, out_scr
):
    quarter = info[0]
    for slot, t_ref in enumerate((t0, t1, t2, t3)):
        rows = pl.ds(slot * QUARTER, QUARTER)
        proj = mm(t_ref[...], w_ref[...]) + b_ref[...]
        for h in range(GROUP):
            cols = slice(h * HEAD_DIM, (h + 1) * HEAD_DIM)
            q_ref[h, rows, :] = (proj[:, cols].astype(bf16).astype(f32) * score_scale).astype(bf16)
            k_ref[h, rows, :] = proj[:, GROUP_WIDTH:][:, cols].astype(bf16)
            v_ref[h, rows, :] = proj[:, 2 * GROUP_WIDTH :][:, cols].astype(bf16)
    for h in range(GROUP):
        keys = k_ref[h]
        values_t = v_ref[h].T

        def chunk_step(chunk, carry, h=h, keys=keys, values_t=values_t):
            rows = pl.ds(pl.multiple_of(chunk * QUARTER, QUARTER), QUARTER)
            scores = mm_nt(keys, q_ref[h, rows, :])
            scores = biased(scores, block_bias(quarter, random_ref, quarter * GROUP + h, chunk))
            row_max = jnp.max(scores, axis=0, keepdims=True)
            probs = jnp.exp(scores - row_max)
            row_sum = jnp.sum(probs, axis=0, keepdims=True)
            out_t = mm(values_t, probs.astype(bf16)) / row_sum
            out_scr[h, rows, :] = out_t.T.astype(bf16)
            lse_ref[pl.ds(h * TP + chunk, 1), :] = row_max + jnp.log(row_sum)
            return carry

        lax.fori_loop(0, TP, chunk_step, 0)
    for slot, a_ref in enumerate((a0, a1, a2, a3)):
        rows = slice(slot * QUARTER, (slot + 1) * QUARTER)
        pack_heads(a_ref, [out_scr[h, rows, :] for h in range(GROUP)])


def attention_back_kernel(
    info, random_ref, q_ref, k_ref, v_ref, lse_ref, g0, g1, g2, g3, gq_ref, sums_ref, do_scr, dk_scr, dv_scr, dq_scr
):
    quarter = info[0]
    for slot, g_ref in enumerate((g0, g1, g2, g3)):
        rows = slice(slot * QUARTER, (slot + 1) * QUARTER)
        for h, piece in enumerate(unpack_heads(g_ref)):
            do_scr[h, rows, :] = piece
    for h in range(GROUP):
        keys = k_ref[h]
        keys_t = keys.T
        values = v_ref[h]
        dk_scr[...] = jnp.zeros_like(dk_scr)
        dv_scr[...] = jnp.zeros_like(dv_scr)

        def chunk_step(chunk, carry, h=h, keys=keys, keys_t=keys_t, values=values):
            rows = pl.ds(pl.multiple_of(chunk * QUARTER, QUARTER), QUARTER)
            queries = q_ref[h, rows, :]
            grad_out = do_scr[h, rows, :]
            scores = mm_nt(keys, queries)
            scores = biased(scores, block_bias(quarter, random_ref, quarter * GROUP + h, chunk))
            probs = jnp.exp(scores - lse_ref[pl.ds(h * TP + chunk, 1), :])
            grad_probs = mm_nt(values, grad_out)
            delta = jnp.sum(probs * grad_probs, axis=0, keepdims=True)
            grad_scores = (probs * (grad_probs - delta)).astype(bf16)
            dv_scr[...] += mm(probs.astype(bf16), grad_out)
            dk_scr[...] += mm(grad_scores, queries)
            dq_t = mm(keys_t, grad_scores) * score_scale
            dq_scr[rows, :] = dq_t.T
            return carry

        lax.fori_loop(0, TP, chunk_step, 0)
        lo = h * HEAD_DIM
        gq_ref[:, lo : lo + HEAD_DIM] = dq_scr[...].astype(bf16)
        gq_ref[:, GROUP_WIDTH + lo : GROUP_WIDTH + lo + HEAD_DIM] = dk_scr[...].astype(bf16)
        gq_ref[:, 2 * GROUP_WIDTH + lo : 2 * GROUP_WIDTH + lo + HEAD_DIM] = dv_scr[...].astype(bf16)
    sums_ref[...] = jnp.zeros_like(sums_ref)
    sums_ref[0:1, :] = jnp.sum(gq_ref[...].astype(f32), axis=0, keepdims=True)


def ffn_kernel(
    info,
    t_ref,
    a0,
    a1,
    a2,
    a3,
    vec_in,
    bias_in_ref,
    cot_ref,
    w_out_hbm,
    w_in_hbm,
    w_back_hbm,
    *rest,
):
    sources = rest[: 2 * (TP - 1)]
    (
        lo_ref,
        g0,
        g1,
        g2,
        g3,
        gin_ref,
        x_ref,
        gb_ref,
        act_ref,
        gpre_ref,
        att_ref,
        gmix_ref,
        vec_ref,
        w_out_s,
        w_in_s,
        w_back_s,
        gp_scr,
        sems,
    ) = rest[2 * (TP - 1) :]
    quarter, mine, z_here = info[0], info[1], info[2]
    first = []
    for slot in range(TP):
        start = pl.multiple_of((quarter ^ slot) * GROUP_WIDTH, GROUP_WIDTH)
        first.append(
            pltpu.make_async_copy(
                w_out_hbm.at[pl.ds(start, GROUP_WIDTH), :],
                w_out_s.at[pl.ds(slot * GROUP_WIDTH, GROUP_WIDTH), :],
                sems.at[slot],
            )
        )
    first.append(pltpu.make_async_copy(w_in_hbm, w_in_s.at[0], sems.at[4]))
    first.append(pltpu.make_async_copy(w_back_hbm, w_back_s.at[0], sems.at[5]))
    held = (w_in_s, w_back_s)
    copies = [[] for _ in range(TP)]
    n = 6
    for q in range(1, TP):
        for side in range(2):
            source = sources[(q - 1) * 2 + side]
            for p in range(4):
                start = pl.multiple_of((mine ^ PLANE_MASKS[p] ^ side) * SLICE, SLICE)
                for part in range(2):
                    copies[q].append(
                        pltpu.make_async_copy(
                            source.at[p, part], held[part].at[q, pl.ds(start, SLICE), :], sems.at[n]
                        )
                    )
                    n += 1
    for copy in first + sum(copies, []):
        copy.start()

    bias_out, gain_one, shift_one = vec_in[0:1, :], vec_in[1:2, :], vec_in[2:3, :]
    bias_back, gain_two, shift_two = vec_in[3:4, :], vec_in[4:5, :], vec_in[5:6, :]
    for slot, a_ref in enumerate((a0, a1, a2, a3)):
        for h, piece in enumerate(unpack_heads(a_ref)):
            lo = slot * GROUP_WIDTH + h * HEAD_DIM
            att_ref[:, lo : lo + HEAD_DIM] = piece
    for copy in first[:4]:
        copy.wait()
    mixed = mm(att_ref[...], w_out_s[...]) + bias_out
    first_in = t_ref[...].astype(f32) + mixed

    def spread(h):
        centred = h - jnp.mean(h, axis=-1, keepdims=True)
        scale = lax.rsqrt(jnp.mean(centred * centred, axis=-1, keepdims=True) + epsilon)
        return centred * scale, scale

    def spread_back(grad, gain, normal, scale):
        weighted = grad * gain
        mean_one = jnp.mean(weighted, axis=-1, keepdims=True)
        mean_two = jnp.mean(weighted * normal, axis=-1, keepdims=True)
        return scale * (weighted - mean_one - normal * mean_two)

    normal_one, scale_one = spread(first_in)
    first_norm = normal_one * gain_one + shift_one
    x = first_norm.astype(bf16)
    x_ref[...] = x
    for copy in first[4:]:
        copy.wait()
    branch = jnp.zeros((QUARTER, WIDTH), f32)
    for q in range(TP):
        for copy in copies[q]:
            copy.wait()
        cols = slice(q * WIDTH, (q + 1) * WIDTH)
        bias_q = bias_in_ref[q : q + 1, :]
        pre = mm(x, w_in_s[q]) + bias_q
        inner = 0.7978845608028654 * (pre + 0.044715 * pre * pre * pre)
        tanh = jnp.tanh(inner)
        half = 0.5 * (1.0 + tanh)
        act = (pre * half).astype(bf16)
        act_ref[:, cols] = act
        slope = 0.7978845608028654 * (1.0 + 3.0 * 0.044715 * pre * pre)
        gp_scr[:, cols] = half + 0.5 * pre * (1.0 - tanh * tanh) * slope
        branch = branch + mm_nt(act, w_back_s[q])
    second_in = first_norm + branch + bias_back
    normal_two, scale_two = spread(second_in)
    lo_ref[...] = (normal_two * gain_two + shift_two).astype(bf16)
    grad_out = cot_ref[...].astype(f32)
    vec_ref[...] = jnp.zeros_like(vec_ref)
    vec_ref[0:1, :] = jnp.sum(grad_out, axis=0, keepdims=True)
    vec_ref[1:2, :] = jnp.sum(grad_out * normal_two, axis=0, keepdims=True)
    grad_second = spread_back(grad_out, gain_two, normal_two, scale_two)
    grad_branch = grad_second.astype(bf16)
    gb_ref[...] = grad_branch
    vec_ref[2:3, :] = jnp.sum(grad_branch.astype(f32), axis=0, keepdims=True)
    grad_first = grad_second
    for q in range(TP):
        cols = slice(q * WIDTH, (q + 1) * WIDTH)
        grad_pre = (mm(grad_branch, w_back_s[q]) * gp_scr[:, cols]).astype(bf16)
        gpre_ref[:, cols] = grad_pre
        vec_ref[pl.ds(6 + (z_here ^ q), 1), :] = jnp.sum(grad_pre.astype(f32), axis=0, keepdims=True)
        grad_first = grad_first + mm_nt(grad_pre, w_in_s[q])
    vec_ref[3:4, :] = jnp.sum(grad_first, axis=0, keepdims=True)
    vec_ref[4:5, :] = jnp.sum(grad_first * normal_one, axis=0, keepdims=True)
    grad_in = spread_back(grad_first, gain_one, normal_one, scale_one)
    gin_ref[...] = grad_in
    grad_mixed = grad_in.astype(bf16)
    gmix_ref[...] = grad_mixed
    vec_ref[5:6, :] = jnp.sum(grad_mixed.astype(f32), axis=0, keepdims=True)
    grad_att = mm_nt(grad_mixed, w_out_s[...]).astype(bf16)
    for slot, g_ref in enumerate((g0, g1, g2, g3)):
        lo = slot * GROUP_WIDTH
        pack_heads(
            g_ref, [grad_att[:, lo + h * HEAD_DIM : lo + (h + 1) * HEAD_DIM] for h in range(GROUP)]
        )


def position_mask(position, order):
    mask = 0
    for n, bit in enumerate(order):
        if (position >> (2 - n)) & 1:
            mask |= bit
    return mask


ORDER_A = (CORE, X_BIT, Y_BIT)
ORDER_B = (CORE, Y_BIT, X_BIT)


def weight_grad_kernel(
    info,
    x_ref,
    gb_ref,
    act_ref,
    gpre_ref,
    att_ref,
    gmix_ref,
    ga_keep,
    ga_send,
    gb_keep,
    gb_send,
    go_keep,
    go_send,
    flip_scr,
    lhs_scr,
):
    mine = info[1]
    for left, right, keep, send, order in (
        (gb_ref, act_ref, gb_keep, gb_send, ORDER_B),
        (x_ref, gpre_ref, ga_keep, ga_send, ORDER_A),
    ):
        flip_scr[...] = left[...].T
        for p in range(SLOTS):
            start = pl.multiple_of((mine ^ position_mask(p, order)) * SLICE, SLICE)
            lhs_scr[p * SLICE : (p + 1) * SLICE, :] = flip_scr[pl.ds(start, SLICE), :]
        for q in range(TP):
            product = mm(lhs_scr[...], right[:, q * WIDTH : (q + 1) * WIDTH]).astype(bf16)
            for p in range(SLOTS):
                out = send if p >= SLOTS // 2 else keep
                out[p % (SLOTS // 2), q] = product[p * SLICE : (p + 1) * SLICE, :]
    product = mm(gmix_ref[...].T, att_ref[...]).astype(bf16)
    go_keep[...] = product[:, : 2 * GROUP_WIDTH]
    go_send[...] = product[:, 2 * GROUP_WIDTH :]


ORDER_LA = (4, 2, 1)
ORDER_LB = (2, 4, 1)


VEC_ROWS = 16
HALF = WIDTH // 2
HELD = SLOTS // 2 * SLICE


def flip_kernel(t0, t1, t2, t3, out_ref):
    for slot, t_ref in enumerate((t0, t1, t2, t3)):
        out_ref[:, slot * QUARTER : (slot + 1) * QUARTER] = t_ref[...].T


def qkv_grad_kernel(
    info, tokens_t, gq_ref, go_ref, vec_ref, sums_ref, la_keep, la_send, lb_keep, lb_send, out_scr
):
    quarter, here = info[0], info[3]
    out_scr[:, : 3 * GROUP_WIDTH] = mm(tokens_t[...], gq_ref[...]).astype(bf16)
    out_scr[:, 3 * GROUP_WIDTH :] = go_ref[...]
    for keep, send, order, lo in (
        (la_keep, la_send, ORDER_LA, 0),
        (lb_keep, lb_send, ORDER_LB, HALF),
    ):
        for p in range(SLOTS):
            start = pl.multiple_of((here ^ position_mask(p, order)) * SLICE, SLICE)
            out = send if p >= SLOTS // 2 else keep
            row = p % (SLOTS // 2) * SLICE
            out[row : row + SLICE, :] = out_scr[pl.ds(start, SLICE), lo : lo + HALF]
    sums = sums_ref[0:1, :]
    placed = []
    for kind in (0, 2):
        piece = sums[:, kind * GROUP_WIDTH : (kind + 1) * GROUP_WIDTH]
        placed.append(
            jnp.concatenate([jnp.where(quarter == g, piece, 0.0) for g in range(TP)], axis=1)
        )
    vectors = jnp.concatenate([vec_ref[0:10, :]] + placed + [vec_ref[12:VEC_ROWS, :]], axis=0)
    vectors = vectors.astype(bf16)
    for out in (la_keep, la_send):
        out[HELD : HELD + VEC_ROWS, :] = vectors[:, :HALF]
        out[HELD + VEC_ROWS :, :] = vectors[:, HALF:]


def token_grad_kernel(gq_ref, w_ref, keep_ref, send_ref):
    half = LENGTH // 2
    keep_ref[...] = mm_nt(gq_ref[:half, :], w_ref[...]).astype(bf16)
    send_ref[...] = mm_nt(gq_ref[half:, :], w_ref[...]).astype(bf16)


def ffn_out_kernel(info, f_ref, f_other, w_in_out, w_back_out, flip_scr):
    mine = info[1]
    for side, ref in enumerate((f_ref, f_other)):
        for place_xy in range(4):
            mask = side | (X_BIT if place_xy & 1 else 0) | (Y_BIT if place_xy & 2 else 0)
            start = pl.multiple_of((mine ^ mask) * SLICE, SLICE)
            w_in_out[pl.ds(start, SLICE), :] = ref[place_xy, 0].astype(f32)
            flip_scr[pl.ds(start, SLICE), :] = ref[place_xy, 1].astype(f32)
    w_back_out[...] = flip_scr[...].T


def qkv_out_kernel(info, c_ref, c_other, qkv_out, out_out, *rest):
    vec_outs, (all_scr, flip_scr) = rest[:9], rest[9:]
    quarter, z_here, here = info[0], info[2], info[3]
    count = 16 * SLICE
    for side, ref in enumerate((c_ref, c_other)):
        for n in range(16):
            all_scr[side * 16 + n] = ref[n * SLICE : (n + 1) * SLICE, :]
    vectors = total(c_ref[count:, :], c_other[count:, :])
    bias_in = jnp.zeros((1, WIDTH), f32)
    for q in range(TP):
        bias_in = jnp.where(z_here == q, vectors[6 + q : 7 + q, :], bias_in)
    for out, n in zip(vec_outs[:8], (0, 1, 2, 3, 4, 5, 10, 11)):
        out[...] = vectors[n]
    vec_outs[8][...] = bias_in[0]
    for block in range(SLOTS):
        pieces = []
        for group in range(TP):
            group_off = quarter ^ group
            block_off = here ^ block
            xy = ((block_off >> 2) & 1) + (block_off & 2)
            z_off = (group_off & 1) + 2 * (block_off & 1)
            slot = (group_off >> 1) * 16 + xy * 4 + z_off
            pieces.append(all_scr[slot])
        rows = slice(block * SLICE, (block + 1) * SLICE)
        for kind in range(4):
            cols = slice(kind * GROUP_WIDTH, (kind + 1) * GROUP_WIDTH)
            joined = jnp.concatenate([piece[:, cols] for piece in pieces], axis=1).astype(f32)
            if kind < 3:
                qkv_out[rows, kind * WIDTH : (kind + 1) * WIDTH] = joined
            else:
                flip_scr[rows, :] = joined
    out_out[...] = flip_scr[...].T


VMEM = pl.BlockSpec(memory_space=pltpu.VMEM)
SMEM = pl.BlockSpec(memory_space=pltpu.SMEM)
HBM = pl.BlockSpec(memory_space=pl.ANY)


def call(kernel, in_specs, outs, scratch, flops, moved, name):
    return pl.pallas_call(
        kernel,
        out_shape=[jax.ShapeDtypeStruct(shape, dtype) for shape, dtype in outs],
        in_specs=in_specs,
        out_specs=[VMEM] * len(outs),
        scratch_shapes=scratch,
        compiler_params=pltpu.CompilerParams(vmem_limit_bytes=VMEM_LIMIT),
        cost_estimate=pl.CostEstimate(flops=flops, bytes_accessed=moved, transcendentals=0),
        name=name,
    )


def per_device(
    tokens,
    w_qkv,
    bias_query,
    bias_value,
    w_out,
    bias_out,
    gain_attn,
    shift_attn,
    w_in,
    bias_in,
    w_back,
    bias_back,
    gain_ffn,
    shift_ffn,
    random_blocks,
    cotangent,
):
    dp_count = lax.axis_size("dp")
    d = lax.axis_index("dp")
    z = lax.axis_index("tp")
    core = d & 1
    quarter = (z & 1) + 2 * core
    mine = d & (SLOTS - 1)
    here = ((d >> 1) & 1) * 4 + ((d >> 2) & 1) * 2 + (z >> 1)
    info = jnp.stack([quarter, mine, z, here]).astype(jnp.int32)
    extra_bits = [1 << b for b in range(3, dp_count.bit_length() - 1)]

    own_tokens = place(tokens[0])
    random_here = place(random_blocks).reshape(-1)
    near_tokens = hop(own_tokens, 0, 1)
    core_tokens = hop(own_tokens, CORE, 0)
    far_tokens = hop(near_tokens, CORE, 0)
    token_slots = (own_tokens, near_tokens, core_tokens, far_tokens)

    w_back_t = w_back.T
    piece = jnp.stack(
        [
            lax.dynamic_slice_in_dim(w_in, mine * SLICE, SLICE, 0),
            lax.dynamic_slice_in_dim(w_back_t, mine * SLICE, SLICE, 0),
        ]
    )
    bias_piece = jnp.broadcast_to(bias_in[None], (16, WIDTH))

    def spread_plane(own, by_rows):
        by_x = hop(own, X_BIT, 0)
        by_y = hop(own, Y_BIT, 0)
        diag = hop(by_x, Y_BIT, 0) if by_rows else hop(by_y, X_BIT, 0)
        held = jnp.stack([own, by_x, by_y, diag])
        return [held, hop(held, CORE, 0)]

    sources = spread_plane(hop(piece, 0, 1), True)
    piece_two = hop(after(piece, own_tokens), 0, 2)
    piece_three = hop(after(piece, near_tokens), 0, 3)
    bias_all = [bias_piece] + [hop(after(bias_piece, near_tokens), 0, q) for q in range(1, TP)]

    start = quarter * GROUP_WIDTH

    def group_cols(array, kind):
        return lax.dynamic_slice_in_dim(array, kind * WIDTH + start, GROUP_WIDTH, 1)

    w_group = jnp.concatenate([group_cols(w_qkv, kind) for kind in range(3)], axis=1)
    bias_query_group = lax.dynamic_slice_in_dim(bias_query, start, GROUP_WIDTH, 0)
    bias_value_group = lax.dynamic_slice_in_dim(bias_value, start, GROUP_WIDTH, 0)
    bias_group = jnp.concatenate(
        [bias_query_group, jnp.zeros_like(bias_query_group), bias_value_group]
    ).astype(f32)[None]
    packed = ((QUARTER + QUARTER // 2, 2 * HEAD_DIM), bf16)
    per_head = ((GROUP, LENGTH, HEAD_DIM), bf16)
    a0, a1, a2, a3, queries, keys, values, lse = call(
        attention_kernel,
        [SMEM, SMEM] + [VMEM] * 6,
        [packed] * 4 + [per_head] * 3 + [((16, QUARTER), f32)],
        [pltpu.VMEM((GROUP, LENGTH, HEAD_DIM), bf16)],
        2 * 10**9,
        8 * 10**6,
        "attention",
    )(info, random_here, *token_slots, w_group, bias_group)
    a0_done = a0
    a1 = hop(a1, 0, 1)
    a2 = hop(a2, CORE, 0)
    a3 = hop(a3, CORE, 1)
    tokens_t = call(
        flip_kernel, [VMEM] * 4, [((WIDTH, LENGTH), bf16)], [], 0, 3 * 10**6, "flip_tokens"
    )(after(own_tokens, a0_done), near_tokens, core_tokens, far_tokens)[0]
    cot = place(after(cotangent[0], a0_done))
    sources += spread_plane(after(piece_two, a0_done), False)
    sources += spread_plane(after(piece_three, a0_done), True)
    bias_all = jnp.concatenate([bias[:1] for bias in bias_all]).astype(f32)

    vec_in = jnp.stack(
        [bias_out, gain_attn, shift_attn, bias_back, gain_ffn, shift_ffn, bias_out, bias_out]
    ).astype(f32)
    rows = ((QUARTER, WIDTH), bf16)
    wide = ((QUARTER, TP * WIDTH), bf16)
    (
        out_here,
        g0,
        g1,
        g2,
        g3,
        grad_in,
        ffn_input,
        grad_branch,
        activated,
        grad_pre,
        attended,
        grad_mixed,
        vectors,
    ) = call(
        ffn_kernel,
        [SMEM] + [VMEM] * 8 + [HBM] * 9,
        [rows] + [packed] * 4 + [((QUARTER, WIDTH), f32), rows, rows, wide, wide, rows, rows, ((16, WIDTH), f32)],
        [
            pltpu.VMEM((WIDTH, WIDTH), bf16),
            pltpu.VMEM((TP, WIDTH, WIDTH), bf16),
            pltpu.VMEM((TP, WIDTH, WIDTH), bf16),
            pltpu.VMEM((QUARTER, TP * WIDTH), f32),
            pltpu.SemaphoreType.DMA((6 + 16 * (TP - 1),)),
        ],
        6 * 10**9,
        25 * 10**6,
        "ffn",
    )(info, own_tokens, a0, a1, a2, a3, vec_in, bias_all, cot, w_out, w_in, w_back_t, *sources)
    g1 = hop(g1, 0, 1)
    g2 = hop(g2, CORE, 0)
    g3 = hop(g3, CORE, 1)

    quads = ((SLOTS // 2, TP, SLICE, WIDTH), bf16)
    halves = ((WIDTH, 2 * GROUP_WIDTH), bf16)
    ga_keep, ga_send, gb_keep, gb_send, go_keep, go_send = call(
        weight_grad_kernel,
        [SMEM] + [VMEM] * 6,
        [quads] * 4 + [halves] * 2,
        [pltpu.VMEM((WIDTH, QUARTER), bf16), pltpu.VMEM((WIDTH, QUARTER), bf16)],
        3 * 10**9,
        14 * 10**6,
        "weight_grads",
    )(info, ffn_input, grad_branch, activated, grad_pre, attended, grad_mixed)

    grad_qkv, qkv_sums = call(
        attention_back_kernel,
        [SMEM, SMEM] + [VMEM] * 8,
        [((LENGTH, 3 * GROUP_WIDTH), bf16), ((8, 3 * GROUP_WIDTH), f32)],
        [
            pltpu.VMEM((GROUP, LENGTH, HEAD_DIM), bf16),
            pltpu.VMEM((LENGTH, HEAD_DIM), f32),
            pltpu.VMEM((LENGTH, HEAD_DIM), f32),
            pltpu.VMEM((LENGTH, HEAD_DIM), f32),
        ],
        4 * 10**9,
        8 * 10**6,
        "attention_back",
    )(info, random_here, queries, keys, values, lse, g0, g1, g2, g3)

    layer_out = place(after(out_here, grad_qkv))[None]

    go_other = hop(go_send, CORE, 0)
    go_near = hop(add_low(go_keep, go_other)[:, GROUP_WIDTH:], 0, 1)
    go_here = add_low(go_keep[:, :GROUP_WIDTH], go_other[:, :GROUP_WIDTH], go_near)

    la_keep, la_send, lb_keep, lb_send = call(
        qkv_grad_kernel,
        [SMEM] + [VMEM] * 5,
        [((HELD + 2 * VEC_ROWS, HALF), bf16)] * 2 + [((HELD, HALF), bf16)] * 2,
        [pltpu.VMEM((WIDTH, 4 * GROUP_WIDTH), bf16)],
        10**9,
        5 * 10**6,
        "qkv_grads",
    )(info, tokens_t, grad_qkv, go_here, vectors, qkv_sums)
    ra = hop(la_send, X_BIT, 0)
    rb = hop(lb_send, Y_BIT, 0)
    two = 2 * SLICE
    ra2 = hop(add_low(la_keep[two:], ra[two:]), Y_BIT, 0)
    rb2 = hop(add_low(lb_keep[two:], rb[two:]), X_BIT, 0)

    def joined(slot):
        rows = slice(slot * SLICE, (slot + 1) * SLICE)
        both = jnp.concatenate(
            [total(la_keep[rows], ra[rows], ra2[rows]), total(lb_keep[rows], rb[rows], rb2[rows])],
            axis=1,
        )
        vec = total(la_keep[HELD:], ra[HELD:], ra2[two:])
        vec = jnp.concatenate([vec[:VEC_ROWS], vec[VEC_ROWS:]], axis=1)
        return jnp.concatenate([both, vec]).astype(bf16)

    sum_l = add_low(joined(0), hop(joined(1), 0, 2))
    for bit in extra_bits:
        sum_l = add_low(sum_l, hop(sum_l, bit, 0))
    z_one, z_two, z_three = hop(sum_l, 0, 1), hop(sum_l, 0, 2), hop(sum_l, 0, 3)
    by_z = jnp.concatenate([part[:SLICE] for part in (sum_l, z_one, z_two, z_three)])
    vec = add_low(sum_l[SLICE:], z_one[SLICE:])
    z_x = hop(by_z, X_BIT, 0)
    z_y = hop(by_z, Y_BIT, 0)
    z_d0 = hop(z_x[:two], Y_BIT, 0)
    z_d1 = hop(z_y[two:], X_BIT, 0)
    plane = jnp.concatenate([by_z, z_x, z_y, z_d0, z_d1, vec])
    grad_w_qkv, grad_w_out, *vec_outs = call(
        qkv_out_kernel,
        [SMEM, VMEM, VMEM],
        [((WIDTH, 3 * WIDTH), f32), ((WIDTH, WIDTH), f32)] + [((WIDTH,), f32)] * 9,
        [pltpu.VMEM((32, SLICE, WIDTH), bf16), pltpu.VMEM((WIDTH, WIDTH), f32)],
        10**6,
        14 * 10**6,
        "qkv_out",
    )(info, plane, hop(plane, CORE, 0))

    keep, send = call(
        token_grad_kernel,
        [VMEM, VMEM],
        [((LENGTH // 2, WIDTH), bf16)] * 2,
        [],
        10**9,
        4 * 10**6,
        "token_grad",
    )(grad_qkv, w_group)
    other = hop(send, CORE, 0)
    near = hop(add_low(keep[QUARTER:], other[QUARTER:]), 0, 1)
    grad_tokens = place(add_low(keep[:QUARTER], other[:QUARTER], near, grad_in))[None]

    ra = hop(ga_send, CORE, 0)
    rb = hop(gb_send, CORE, 0)
    xa = hop(add_low(ga_keep[2:], ra[2:]), X_BIT, 0)
    yb = hop(add_low(gb_keep[2:], rb[2:]), Y_BIT, 0)
    ya = hop(add_low(ga_keep[1], ra[1], xa[1]), Y_BIT, 0)
    xb = hop(add_low(gb_keep[1], rb[1], yb[1]), X_BIT, 0)

    def both(q):
        return jnp.stack(
            [
                total(ga_keep[0, q], ra[0, q], xa[0, q], ya[q]),
                total(gb_keep[0, q], rb[0, q], yb[0, q], xb[q]),
            ]
        )

    parts = [hop(both(q).astype(bf16), 0, q) for q in range(1, TP)]
    sum_f = add_low(both(0), *parts)
    for bit in extra_bits:
        sum_f = add_low(sum_f, hop(sum_f, bit, 0))
    f_x = hop(sum_f, X_BIT, 0)
    f_y = hop(sum_f, Y_BIT, 0)
    f_d = jnp.stack([hop(f_x[0], Y_BIT, 0), hop(f_y[1], X_BIT, 0)])
    f_all = jnp.stack([sum_f, f_x, f_y, f_d])
    grad_w_in, grad_w_back = call(
        ffn_out_kernel,
        [SMEM, VMEM, VMEM],
        [((WIDTH, WIDTH), f32)] * 2,
        [pltpu.VMEM((WIDTH, WIDTH), f32)],
        10**6,
        7 * 10**6,
        "ffn_out",
    )(info, f_all, hop(f_all, CORE, 0))

    (
        grad_shift_ffn,
        grad_gain_ffn,
        grad_bias_back,
        grad_shift_attn,
        grad_gain_attn,
        grad_bias_out,
        grad_bias_query,
        grad_bias_value,
        grad_bias_in,
    ) = vec_outs
    return (
        layer_out,
        grad_tokens,
        grad_w_qkv,
        grad_bias_query,
        grad_bias_value,
        grad_w_out,
        grad_bias_out,
        grad_gain_attn,
        grad_shift_attn,
        grad_w_in,
        grad_bias_in,
        grad_w_back,
        grad_bias_back,
        grad_gain_ffn,
        grad_shift_ffn,
    )


def solution(mesh):
    in_specs = (
        P("dp", "tp", None),
        P(),
        P(),
        P(),
        P(),
        P(),
        P(),
        P(),
        P(None, "tp"),
        P("tp"),
        P("tp", None),
        P(),
        P(),
        P(),
        P("dp", None, None, None),
        P("dp", "tp", None),
    )
    out_specs = (
        P("dp", "tp", None),
        P("dp", "tp", None),
        P(),
        P(),
        P(),
        P(),
        P(),
        P(),
        P(),
        P(None, "tp"),
        P("tp"),
        P("tp", None),
        P(),
        P(),
        P(),
    )
    return jax.shard_map(
        per_device, mesh=mesh, in_specs=in_specs, out_specs=out_specs, check_vma=False
    )
```

time: 1050 us -> 359 us (0.34)
  waiting for transfers between devices: 419 us -> 127 us
  other arithmetic: 249 us -> 13.5 us
  local copies, waits for them, and re-layouts: 209 us -> 22 us
  starting transfers between devices: 0.82 us -> 116 us
  matrix products: 94.2 us -> 0 us
  Pallas kernels: 0 us -> 77.9 us
  blocking collectives: 55.5 us -> 0 us
  between operations: 15.2 us -> 1.39 us
    psum x2 -> x0, waiting for transfers between devices: 205 us -> none  [the longest x1 121 us: per_device(): lax.psum((grad_w_qkv, grad_bias_query, grad_bias_value, grad_w_out, grad_...]
    scatter-add x2 -> x0, other arithmetic: 198 us -> none  [add_to_blocks(): return start_rows.at[block_index].add(picked_rows)]
    ppermute x0 -> x63, waiting for transfers between devices: none -> 127 us  [the longest x58 107 us: hop(): return lax.ppermute(array, ('dp', 'tp'), pairs)]
    ppermute x0 -> x63, starting transfers between devices: none -> 116 us  [the longest x58 93.4 us: hop(): return lax.ppermute(array, ('dp', 'tp'), pairs)]
    reduce_scatter x4 -> x0, waiting for transfers between devices: 108 us -> none  [the longest x1 54.2 us: per_device(): lax.psum_scatter(times_transposed(grad_pre, w_in), 'tp', scatter_dimensio...]
    all_gather x4 -> x0, waiting for transfers between devices: 107 us -> none  [the longest x1 36.2 us: per_device(): branch_rows = lax.all_gather(grad_branch, 'tp', axis=0, tiled=True)]
    dot_general x24 -> x0, matrix products: 94.2 us -> none  [the longest x4 16.6 us: contract_rows(): lax.dot_general(left, right, (((0,), (0,)), ((), ())), preferred_element_...]
    reshape x15 -> x1, local copies, waits for them, and re-layouts: 85.3 us -> 0.79 us  [per_device(): random_here = place(random_blocks).reshape(-1)]
  transfers between devices with their start and end apart: 10 -> 63, of which waited for: 9 -> 28; matrix products, arithmetic and copies ran while one was open for 12% -> 8% of each run, Pallas kernels for 0% -> 14%
where the time goes in v1:
time: 359 us; the launch traced here: 357 us
  waiting for transfers between devices  127 us (35%)
  starting transfers between devices  116 us (32%)
  Pallas kernels  77.9 us (22%)
  local copies, waits for them, and re-layouts  22 us (6%)
  other arithmetic  13.5 us (4%)
    ppermute x58, waiting for transfers between devices, hop(): return lax.ppermute(array, ('dp', 'tp'), pairs)  107 us
    ppermute x58, starting transfers between devices, hop(): return lax.ppermute(array, ('dp', 'tp'), pairs)  93.4 us
    ppermute x5, starting transfers between devices, place(): return lax.ppermute(array, ('dp', 'tp'), pairs)  22.7 us
    ppermute x5, waiting for transfers between devices, place(): return lax.ppermute(array, ('dp', 'tp'), pairs)  19.8 us
    pallas_call x1, Pallas kernels, per_device(): call(attention_back_kernel, [SMEM, SMEM] + [VMEM] * 8, [((LENGTH, 3 * GRO...  16.4 us
    pallas_call x1, Pallas kernels, per_device(): call(attention_kernel, [SMEM, SMEM] + [VMEM] * 6, [packed] * 4 + [per_hea...  14.3 us
    pallas_call x1, Pallas kernels, per_device(): call(ffn_kernel, [SMEM] + [VMEM] * 8 + [HBM] * 9, [rows] + [packed] * 4 +...  14.1 us
    pallas_call x1, Pallas kernels, per_device(): call(weight_grad_kernel, [SMEM] + [VMEM] * 6, [quads] * 4 + [halves] * 2,...  9.27 us
  transfers between devices with their start and end apart: 63, of which 28 were waited for; matrix products, arithmetic and copies ran while one was open for 8% of the time, Pallas kernels for 14%

profile of v1, /device:TPU:1, one launch (start us, length us, event | category | flops | bytes accessed | tf_op | source)
XLA Modules:
  0.0 357.4 jit_solution(1492155510725802321)
XLA Ops:
  0.6 5.6 %collective-permute-start = (bf16[256,768]{1,0:T(8,128)(2,1)}, bf16[256,768]{1,0:T(8,128)(2,1)S(1)}, u32[]{:S(2)}, u32[]{:S(2)}) collective-permute-start(bf16[256,768]{1,0:T(8,128)(2,1)} %bitcast.91), channel_id=1, source_target_pairs={{0,0},{1,1},{2,4},{3,5},{4,2},{5,3},{6,6},{7,7},{8,8},{9,9},{10,12... | collective-permute-start | bytes 1179656 | tf_op jit(solution)/shard_map/ppermute | solution.py:72
  6.3 9.2 %collective-permute-done.t0.t_ref = bf16[256,768]{1,0:T(8,128)(2,1)S(1)} collective-permute-done((bf16[256,768]{1,0:T(8,128)(2,1)}, bf16[256,768]{1,0:T(8,128)(2,1)S(1)}, u32[]{:S(2)}, u32[]{:S(2)}) %collective-permute-start) | collective-permute-done | bytes 393248 | tf_op jit(solution)/shard_map/ppermute | solution.py:72
  17.4 4.8 %collective-permute-start.1 = (s32[1,12,16,3]{2,0,3,1:T(1,128)}, s32[1,12,16,3]{2,0,3,1:T(1,128)}, u32[]{:S(2)}, u32[]{:S(2)}) collective-permute-start(s32[1,12,16,3]{2,0,3,1:T(1,128)} %param.30), channel_id=1, source_target_pairs={{0,0},{1,1},{2,4},{3,5},{4,2},{5,3},{6,6},{7,7},{8,8},{9,9},{10,12... | collective-permute-start | bytes 6920 | tf_op jit(solution)/shard_map/ppermute | solution.py:72
  38.7 14.3 %attention.1 = (bf16[384,128]{1,0:T(8,128)(2,1)}, bf16[384,128]{1,0:T(8,128)(2,1)}, bf16[384,128]{1,0:T(8,128)(2,1)}, bf16[384,128]{1,0:T(8,128)(2,1)}, bf16[3,1...) custom-call(s32[4]{0:T(128)} %pad_add_fusion.info, ...), custom_call_target="tpu_custom_call" | custom-call | flops 2000000000 | bytes 8000000 | tf_op jit(solution)/shard_map/attention/pallas_call | solution.py:559
  54.6 6.0 %collective-permute-done.17 = bf16[2,96,768]{2,1,0:T(8,128)(2,1)S(1)} collective-permute-done((bf16[2,96,768]{2,1,0:T(8,128)(2,1)}, bf16[2,96,768]{2,1,0:T(8,128)(2,1)S(1)}, u32[]{:S(2)}, u32[]{:S(2)}) %collective-permute-start.17) | collective-permute-done | bytes 294944 | tf_op jit(solution)/shard_map/ppermute | solution.py:57
  64.7 3.3 collective-permute-done.19
  69.2 5.1 %collective-permute-done.15 = bf16[2,96,768]{2,1,0:T(8,128)(2,1)S(1)} collective-permute-done((bf16[2,96,768]{2,1,0:T(8,128)(2,1)S(1)}, bf16[2,96,768]{2,1,0:T(8,128)(2,1)S(1)}, u32[]{:S(2)}, u32[]{:S(2)}) %collective-permute-start.15) | collective-permute-done | bytes 294944 | tf_op jit(solution)/shard_map/ppermute | solution.py:57
  75.5 3.5 collective-permute-start.16
  80.7 6.3 %collective-permute-done.25 = bf16[2,96,768]{2,1,0:T(8,128)(2,1)S(1)} collective-permute-done((bf16[2,96,768]{2,1,0:T(8,128)(2,1)S(1)}, bf16[2,96,768]{2,1,0:T(8,128)(2,1)S(1)}, u32[]{:S(2)}, u32[]{:S(2)}) %collective-permute-start.25) | collective-permute-done | bytes 294944 | tf_op jit(solution)/shard_map/ppermute | solution.py:57
  90.1 3.7 %collective-permute-start.11 = (bf16[256,768]{1,0:T(8,128)(2,1)}, bf16[256,768]{1,0:T(8,128)(2,1)}, u32[]{:S(2)}, u32[]{:S(2)}) collective-permute-start(bf16[256,768]{1,0:T(8,128)(2,1)} %bitcast.5), channel_id=1, source_target_pairs={{0,0},{1,1},{2,4},{3,5},{4,2},{5,3},{6,6},{7,7},{8,8},{9,9},{10,12... | collective-permute-start | bytes 1179656 | tf_op jit(solution)/shard_map/ppermute | solution.py:72
  95.9 3.3 collective-permute-done.10
  99.1 6.4 %collective-permute-start.9 = (bf16[16,768]{1,0:T(8,128)(2,1)S(1)}, bf16[16,768]{1,0:T(8,128)(2,1)S(1)}, u32[]{:S(2)}, u32[]{:S(2)}) collective-permute-start(bf16[16,768]{1,0:T(8,128)(2,1)S(1)} %broadcast_in_dim.17), channel_id=1, source_target_pairs={{0,2},{1,3},{2,0},{3,1},{4,6},{5,7},{6,4},{7,5},{8,10},{9,11},{10,... | collective-permute-start | bytes 73736 | tf_op jit(solution)/shard_map/ppermute | solution.py:57
  110.6 2.6 collective-permute-done.5.a1
  113.2 5.0 %collective-permute-start.6 = (bf16[384,128]{1,0:T(8,128)(2,1)}, bf16[384,128]{1,0:T(8,128)(2,1)}, u32[]{:S(2)}, u32[]{:S(2)}) collective-permute-start(bf16[384,128]{1,0:T(8,128)(2,1)} %get-tuple-element.73), channel_id=1, source_target_pairs={{0,4},{1,5},{2,6},{3,7},{4,0},{5,1},{6,2},{7,3},{8,12},{9,13},{10,... | collective-permute-start | bytes 294920 | tf_op jit(solution)/shard_map/ppermute | solution.py:57
  128.0 2.1 collective-permute-done.7.a3
  130.7 14.1 %ffn.1 = (bf16[256,768]{1,0:T(8,128)(2,1)}, bf16[384,128]{1,0:T(8,128)(2,1)}, bf16[384,128]{1,0:T(8,128)(2,1)}, bf16[384,128]{1,0:T(8,128)(2,1)}, bf16[384,128]{...) custom-call(s32[4]{0:T(128)} %pad_add_fusion.info, ...), custom_call_target="tpu_custom_call" | custom-call | flops 6000000000 | bytes 25000000 | tf_op jit(solution)/shard_map/ffn/pallas_call | solution.py:599
  144.9 9.3 %weight_grads.1 = (bf16[4,4,96,768]{3,2,1,0:T(8,128)(2,1)}, bf16[4,4,96,768]{3,2,1,0:T(8,128)(2,1)}, bf16[4,4,96,768]{3,2,1,0:T(8,128)(2,1)}, bf16[4,4,96,768]{3...) custom-call(s32[4]{0:T(128)} %pad_add_fusion.info, bf16[256,768]{1,0:T(8,128)(2,1)} %get-tuple-element.96.x_ref, ...), custom_call_target="tpu_custom_call" | custom-call | flops 3000000000 | bytes 14000000 | tf_op jit(solution)/shard_map/weight_grads/pallas_call | solution.py:620
  154.5 3.2 flip_tokens.1.tokens_t
  162.0 2.7 collective-permute-done.29.g3
  165.3 16.4 %attention_back.1 = (bf16[1024,576]{1,0:T(8,128)(2,1)}, f32[8,576]{1,0:T(8,128)}) custom-call(s32[4]{0:T(128)} %pad_add_fusion.info, s32[576]{0:T(1024)} %reshape.411.random_ref, bf16[3,1024,64]{2,1,0:T(8,128)(2,1)} %get-tuple-element.82.q_ref, bf16[3,1024,64]{2,1,0:T(8,128)(2,1)} %get-tuple-element.83.k_ref, bf16[3,1024,64]{2,1,0:T(8,128)(2,1)} %get-tuple-element.84.v_ref, ...), custom_call_target="tpu_custom_call" | custom-call | flops 4000000000 | bytes 8000000 | tf_op jit(solution)/shard_map/attention_back/pallas_call | solution.py:630
  182.6 4.5 %qkv_grads.1 = (bf16[416,384]{1,0:T(8,128)(2,1)}, bf16[416,384]{1,0:T(8,128)(2,1)}, bf16[384,384]{1,0:T(8,128)(2,1)}, bf16[384,384]{1,0:T(8,128)(2,1)}) custom-call(s32[4]{0:T(128)} %pad_add_fusion.info, bf16[768,1024]{1,0:T(8,128)(2,1)} %flip_tokens.1.tokens_t, bf16[1024,576]{1,0:T(8,128)(2,1)} %get-tuple-element.90.gq_ref, ...), custom_call_target="tpu_custom_call" | custom-call | flops 1000000000 | bytes 5000000 | tf_op jit(solution)/shard_map/qkv_grads/pallas_call | solution.py:651
  190.3 5.4 %collective-permute-done.38 = bf16[384,384]{1,0:T(8,128)(2,1)S(1)} collective-permute-done((bf16[384,384]{1,0:T(8,128)(2,1)}, bf16[384,384]{1,0:T(8,128)(2,1)S(1)}, u32[]{:S(2)}, u32[]{:S(2)}) %collective-permute-start.38) | collective-permute-done | bytes 294944 | tf_op jit(solution)/shard_map/ppermute | solution.py:57
  204.5 4.2 %collective-permute-done.40 = bf16[112,768]{1,0:T(8,128)(2,1)S(1)} collective-permute-done((bf16[112,768]{1,0:T(8,128)(2,1)S(1)}, bf16[112,768]{1,0:T(8,128)(2,1)S(1)}, u32[]{:S(2)}, u32[]{:S(2)}) %collective-permute-start.40) | collective-permute-done | bytes 172064 | tf_op jit(solution)/shard_map/ppermute | solution.py:57
  208.7 7.1 %collective-permute-start.43 = (bf16[112,768]{1,0:T(8,128)(2,1)S(1)}, bf16[112,768]{1,0:T(8,128)(2,1)S(1)}, u32[]{:S(2)}, u32[]{:S(2)}) collective-permute-start(bf16[112,768]{1,0:T(8,128)(2,1)S(1)} %add_convert_fusion.8), channel_id=1, source_target_pairs={{0,3},{1,2},{2,1},{3,0},{4,7},{5,6},{6,5},{7,4},{8,11},{9,10},{10,... | collective-permute-start | bytes 516104 | tf_op jit(solution)/shard_map/ppermute | solution.py:57
  219.3 6.6 %collective-permute-done.41 = bf16[112,768]{1,0:T(8,128)(2,1)S(1)} collective-permute-done((bf16[112,768]{1,0:T(8,128)(2,1)S(1)}, bf16[112,768]{1,0:T(8,128)(2,1)S(1)}, u32[]{:S(2)}, u32[]{:S(2)}) %collective-permute-start.41) | collective-permute-done | bytes 172064 | tf_op jit(solution)/shard_map/ppermute | solution.py:57
  225.9 3.1 collective-permute-done.42
  231.0 5.8 %collective-permute-done.50 = bf16[2,4,96,768]{3,2,1,0:T(8,128)(2,1)S(1)} collective-permute-done((bf16[2,4,96,768]{3,2,1,0:T(8,128)(2,1)S(1)}, bf16[2,4,96,768]{3,2,1,0:T(8,128)(2,1)S(1)}, u32[]{:S(2)}, u32[]{:S(2)}) %collective-permute-start.50) | collective-permute-done | bytes 1179680 | tf_op jit(solution)/shard_map/ppermute | solution.py:57
  237.0 3.7 %collective-permute-start.51 = (bf16[4,96,768]{2,1,0:T(8,128)(2,1)S(1)}, bf16[4,96,768]{2,1,0:T(8,128)(2,1)S(1)}, u32[]{:S(2)}, u32[]{:S(2)}) collective-permute-start(bf16[4,96,768]{2,1,0:T(8,128)(2,1)S(1)} %fusion), channel_id=1, source_target_pairs={{0,16},{1,17},{2,18},{3,19},{4,20},{5,21},{6,22},{7,23},{8,24},{9,... | collective-permute-start | bytes 1769480 | tf_op jit(solution)/shard_map/ppermute | solution.py:57
  241.2 9.3 %collective-permute-done.45 = bf16[384,768]{1,0:T(8,128)(2,1)S(1)} collective-permute-done((bf16[384,768]{1,0:T(8,128)(2,1)S(1)}, bf16[384,768]{1,0:T(8,128)(2,1)S(1)}, u32[]{:S(2)}, u32[]{:S(2)}) %collective-permute-start.45) | collective-permute-done | bytes 589856 | tf_op jit(solution)/shard_map/ppermute | solution.py:57
  250.7 2.5 collective-permute-start.46
  253.2 10.0 %collective-permute-done.51 = bf16[4,96,768]{2,1,0:T(8,128)(2,1)S(1)} collective-permute-done((bf16[4,96,768]{2,1,0:T(8,128)(2,1)S(1)}, bf16[4,96,768]{2,1,0:T(8,128)(2,1)S(1)}, u32[]{:S(2)}, u32[]{:S(2)}) %collective-permute-start.51) | collective-permute-done | bytes 589856 | tf_op jit(solution)/shard_map/ppermute | solution.py:57
  263.8 4.4 %collective-permute-start.56 = (bf16[2,96,768]{2,1,0:T(8,128)(2,1)S(1)}, bf16[2,96,768]{2,1,0:T(8,128)(2,1)S(1)}, u32[]{:S(2)}, u32[]{:S(2)}) collective-permute-start(bf16[2,96,768]{2,1,0:T(8,128)(2,1)S(1)} %pad_maximum_fusion.8), channel_id=1, source_target_pairs={{0,2},{1,3},{2,0},{3,1},{4,6},{5,7},{6,4},{7,5},{8,10},{9,11},{10,... | collective-permute-start | bytes 884744 | tf_op jit(solution)/shard_map/ppermute | solution.py:57
  268.2 2.4 collective-permute-start.57
  271.1 7.6 %collective-permute-done.56 = bf16[2,96,768]{2,1,0:T(8,128)(2,1)S(1)} collective-permute-done((bf16[2,96,768]{2,1,0:T(8,128)(2,1)S(1)}, bf16[2,96,768]{2,1,0:T(8,128)(2,1)S(1)}, u32[]{:S(2)}, u32[]{:S(2)}) %collective-permute-start.56) | collective-permute-done | bytes 294944 | tf_op jit(solution)/shard_map/ppermute | solution.py:57
  278.7 2.2 collective-permute-done.55
  281.1 2.7 collective-permute-start.59
  283.8 10.9 %collective-permute-start.48 = (bf16[1552,768]{1,0:T(8,128)(2,1)S(1)}, bf16[1552,768]{1,0:T(8,128)(2,1)S(1)}, u32[]{:S(2)}, u32[]{:S(2)}) collective-permute-start(bf16[1552,768]{1,0:T(8,128)(2,1)S(1)} %fusion.11.c_ref), channel_id=1, source_target_pairs={{0,4},{1,5},{2,6},{3,7},{4,0},{5,1},{6,2},{7,3},{8,12},{9,13},{10,... | collective-permute-start | bytes 7151624 | tf_op jit(solution)/shard_map/ppermute | solution.py:57
  294.9 3.9 %token_grad.1 = (bf16[512,768]{1,0:T(8,128)(2,1)}, bf16[512,768]{1,0:T(8,128)(2,1)}) custom-call(bf16[1024,576]{1,0:T(8,128)(2,1)} %get-tuple-element.90.gq_ref, bf16[768,576]{1,0:T(8,128)(2,1)} %pad_maximum_fusion.4.w_ref), custom_call_target="tpu_custom_call" | custom-call | flops 1000000000 | bytes 4000000 | tf_op jit(solution)/shard_map/token_grad/pallas_call | solution.py:697
  300.5 2.8 collective-permute-done.58
  303.4 3.1 collective-permute-done.61
  307.6 2.5 collective-permute-start.62
  310.2 3.8 %collective-permute-start.32 = (bf16[256,768]{1,0:T(8,128)(2,1)S(1)}, bf16[256,768]{1,0:T(8,128)(2,1)S(1)}, u32[]{:S(2)}, u32[]{:S(2)}) collective-permute-start(bf16[256,768]{1,0:T(8,128)(2,1)S(1)} %add_convert_fusion.7), channel_id=1, source_target_pairs={{0,1},{1,0},{2,3},{3,2},{4,5},{5,4},{6,7},{7,6},{8,9},{9,8},{10,11... | collective-permute-start | bytes 1179656 | tf_op jit(solution)/shard_map/ppermute | solution.py:57
  314.0 4.9 %collective-permute-start.30 = (bf16[256,768]{1,0:T(8,128)(2,1)S(1)}, bf16[256,768]{1,0:T(8,128)(2,1)S(1)}, u32[]{:S(2)}, u32[]{:S(2)}) collective-permute-start(bf16[256,768]{1,0:T(8,128)(2,1)S(1)} %copy-done.29), channel_id=1, source_target_pairs={{0,0},{1,1},{2,4},{3,5},{4,2},{5,3},{6,6},{7,7},{8,8},{9,9},{10,12... | collective-permute-start | bytes 1179656 | tf_op jit(solution)/shard_map/ppermute | solution.py:72
  319.0 7.8 %collective-permute-done.32 = bf16[256,768]{1,0:T(8,128)(2,1)S(1)} collective-permute-done((bf16[256,768]{1,0:T(8,128)(2,1)S(1)}, bf16[256,768]{1,0:T(8,128)(2,1)S(1)}, u32[]{:S(2)}, u32[]{:S(2)}) %collective-permute-start.32) | collective-permute-done | bytes 393248 | tf_op jit(solution)/shard_map/ppermute | solution.py:57
  327.0 3.6 %collective-permute-start.33 = (bf16[256,768]{1,0:T(8,128)(2,1)S(1)}, bf16[256,768]{1,0:T(8,128)(2,1)S(1)}, u32[]{:S(2)}, u32[]{:S(2)}) collective-permute-start(bf16[256,768]{1,0:T(8,128)(2,1)S(1)} %add_convert_fusion.6), channel_id=1, source_target_pairs={{0,0},{1,1},{2,4},{3,5},{4,2},{5,3},{6,6},{7,7},{8,8},{9,9},{10,12... | collective-permute-start | bytes 1179656 | tf_op jit(solution)/shard_map/ppermute | solution.py:72
  330.6 10.6 %collective-permute-done.33 = bf16[256,768]{1,0:T(8,128)(2,1)S(1)} collective-permute-done((bf16[256,768]{1,0:T(8,128)(2,1)S(1)}, bf16[256,768]{1,0:T(8,128)(2,1)S(1)}, u32[]{:S(2)}, u32[]{:S(2)}) %collective-permute-start.33) | collective-permute-done | bytes 393248 | tf_op jit(solution)/shard_map/ppermute | solution.py:72
  342.6 7.6 %qkv_out.1 = (f32[768,2304]{1,0:T(8,128)}, f32[768,768]{1,0:T(8,128)}, f32[768]{0:T(1024)}, f32[768]{0:T(1024)}, f32[768]{0:T(1024)}, /*index=5*/f32[768]{0:T(10...) custom-call(s32[4]{0:T(128)} %pad_add_fusion.info, ...), custom_call_target="tpu_custom_call" | custom-call | flops 1000000 | bytes 14000000 | tf_op jit(solution)/shard_map/qkv_out/pallas_call | solution.py:687
  351.2 4.7 %ffn_out.1 = (f32[768,768]{1,0:T(8,128)}, f32[768,768]{1,0:T(8,128)}) custom-call(s32[4]{0:T(128)} %pad_add_fusion.info, bf16[4,2,96,768]{3,2,1,0:T(8,128)(2,1)} %copy-done, bf16[4,2,96,768]{3,2,1,0:T(8,128)(2,1)} %copy-done.6), custom_call_target="tpu_custom_call" | custom-call | flops 1000000 | bytes 7000000 | tf_op jit(solution)/shard_map/ffn_out/pallas_call | solution.py:733
  (239 shorter events, 81.7 us)
Async XLA Ops:
  0.6 14.8 %collective-permute-start = (bf16[256,768]{1,0:T(8,128)(2,1)}, bf16[256,768]{1,0:T(8,128)(2,1)S(1)}, u32[]{:S(2)}, u32[]{:S(2)}) collective-permute-start(bf16[256,768]{1,0:T(8,128)(2,1)} %bitcast.91), channel_id=1, source_target_pairs={{0,0},{1,1},{2,4},{3,5},{4,2},{5,3},{6,6},{7,7},{8,8},{9,9},{10,12... | collective-permute-start | bytes 1179656 | tf_op jit(solution)/shard_map/ppermute | solution.py:72
  15.5 10.4 %collective-permute-start.2 = (bf16[256,768]{1,0:T(8,128)(2,1)S(1)}, bf16[256,768]{1,0:T(8,128)(2,1)S(1)}, u32[]{:S(2)}, u32[]{:S(2)}) collective-permute-start(bf16[256,768]{1,0:T(8,128)(2,1)S(1)} %collective-permute-done.t0.t_ref), channel_id=1, source_target_pairs={{0,1},{1,0},{2,3},{3,2},{4,5},{5,4},{6,7},{7,6},{8,9},{9,8},{10,11... | collective-permute-start | bytes 1179656 | tf_op jit(solution)/shard_map/ppermute | solution.py:57
  17.4 16.6 %collective-permute-start.1 = (s32[1,12,16,3]{2,0,3,1:T(1,128)}, s32[1,12,16,3]{2,0,3,1:T(1,128)}, u32[]{:S(2)}, u32[]{:S(2)}) collective-permute-start(s32[1,12,16,3]{2,0,3,1:T(1,128)} %param.30), channel_id=1, source_target_pairs={{0,0},{1,1},{2,4},{3,5},{4,2},{5,3},{6,6},{7,7},{8,8},{9,9},{10,12... | collective-permute-start | bytes 6920 | tf_op jit(solution)/shard_map/ppermute | solution.py:72
  25.8 10.0 %collective-permute-start.12 = (bf16[2,96,768]{2,1,0:T(8,128)(2,1)}, bf16[2,96,768]{2,1,0:T(8,128)(2,1)}, u32[]{:S(2)}, u32[]{:S(2)}) collective-permute-start(bf16[2,96,768]{2,1,0:T(8,128)(2,1)} %pad_maximum_fusion.6), channel_id=1, source_target_pairs={{0,1},{1,0},{2,3},{3,2},{4,5},{5,4},{6,7},{7,6},{8,9},{9,8},{10,11... | collective-permute-start | bytes 884744 | tf_op jit(solution)/shard_map/ppermute | solution.py:57
  25.9 12.1 %collective-permute-start.3 = (bf16[256,768]{1,0:T(8,128)(2,1)S(1)}, bf16[256,768]{1,0:T(8,128)(2,1)S(1)}, u32[]{:S(2)}, u32[]{:S(2)}) collective-permute-start(bf16[256,768]{1,0:T(8,128)(2,1)S(1)} %collective-permute-done.t0.t_ref), channel_id=1, source_target_pairs={{0,4},{1,5},{2,6},{3,7},{4,0},{5,1},{6,2},{7,3},{8,12},{9,13},{10,... | collective-permute-start | bytes 1179656 | tf_op jit(solution)/shard_map/ppermute | solution.py:57
  25.9 12.1 %collective-permute-start.4 = (bf16[256,768]{1,0:T(8,128)(2,1)S(1)}, bf16[256,768]{1,0:T(8,128)(2,1)}, u32[]{:S(2)}, u32[]{:S(2)}) collective-permute-start(bf16[256,768]{1,0:T(8,128)(2,1)S(1)} %collective-permute-done.2.t1), channel_id=1, source_target_pairs={{0,4},{1,5},{2,6},{3,7},{4,0},{5,1},{6,2},{7,3},{8,12},{9,13},{10,... | collective-permute-start | bytes 1179656 | tf_op jit(solution)/shard_map/ppermute | solution.py:57
  32.0 21.1 %collective-permute-start.22 = (bf16[2,96,768]{2,1,0:T(8,128)(2,1)}, bf16[2,96,768]{2,1,0:T(8,128)(2,1)S(1)}, u32[]{:S(2)}, u32[]{:S(2)}) collective-permute-start(bf16[2,96,768]{2,1,0:T(8,128)(2,1)} %pad_maximum_fusion.6), channel_id=1, source_target_pairs={{0,3},{1,2},{2,1},{3,0},{4,7},{5,6},{6,5},{7,4},{8,11},{9,10},{10,... | collective-permute-start | bytes 884744 | tf_op jit(solution)/shard_map/ppermute | solution.py:57
  35.7 26.1 %collective-permute-start.13 = (bf16[2,96,768]{2,1,0:T(8,128)(2,1)}, bf16[2,96,768]{2,1,0:T(8,128)(2,1)S(1)}, u32[]{:S(2)}, u32[]{:S(2)}) collective-permute-start(bf16[2,96,768]{2,1,0:T(8,128)(2,1)} %collective-permute-done.12), channel_id=1, source_target_pairs={{0,8},{1,9},{2,10},{3,11},{4,12},{5,13},{6,14},{7,15},{8,0},{9,1},... | collective-permute-start | bytes 884744 | tf_op jit(solution)/shard_map/ppermute | solution.py:57
  36.9 23.6 %collective-permute-start.17 = (bf16[2,96,768]{2,1,0:T(8,128)(2,1)}, bf16[2,96,768]{2,1,0:T(8,128)(2,1)S(1)}, u32[]{:S(2)}, u32[]{:S(2)}) collective-permute-start(bf16[2,96,768]{2,1,0:T(8,128)(2,1)} %pad_maximum_fusion.6), channel_id=1, source_target_pairs={{0,2},{1,3},{2,0},{3,1},{4,6},{5,7},{6,4},{7,5},{8,10},{9,11},{10,... | collective-permute-start | bytes 884744 | tf_op jit(solution)/shard_map/ppermute | solution.py:57
  53.0 10.2 %collective-permute-start.23 = (bf16[2,96,768]{2,1,0:T(8,128)(2,1)S(1)}, bf16[2,96,768]{2,1,0:T(8,128)(2,1)S(1)}, u32[]{:S(2)}, u32[]{:S(2)}) collective-permute-start(bf16[2,96,768]{2,1,0:T(8,128)(2,1)S(1)} %collective-permute-done.22), channel_id=1, source_target_pairs={{0,8},{1,9},{2,10},{3,11},{4,12},{5,13},{6,14},{7,15},{8,0},{9,1},... | collective-permute-start | bytes 884744 | tf_op jit(solution)/shard_map/ppermute | solution.py:57
  53.3 10.1 %collective-permute-start.14 = (bf16[2,96,768]{2,1,0:T(8,128)(2,1)}, bf16[2,96,768]{2,1,0:T(8,128)(2,1)S(1)}, u32[]{:S(2)}, u32[]{:S(2)}) collective-permute-start(bf16[2,96,768]{2,1,0:T(8,128)(2,1)} %collective-permute-done.12), channel_id=1, source_target_pairs={{0,16},{1,17},{2,18},{3,19},{4,20},{5,21},{6,22},{7,23},{8,24},{9,... | collective-permute-start | bytes 884744 | tf_op jit(solution)/shard_map/ppermute | solution.py:57
  61.8 12.6 %collective-permute-start.15 = (bf16[2,96,768]{2,1,0:T(8,128)(2,1)S(1)}, bf16[2,96,768]{2,1,0:T(8,128)(2,1)S(1)}, u32[]{:S(2)}, u32[]{:S(2)}) collective-permute-start(bf16[2,96,768]{2,1,0:T(8,128)(2,1)S(1)} %collective-permute-done.13), channel_id=1, source_target_pairs={{0,16},{1,17},{2,18},{3,19},{4,20},{5,21},{6,22},{7,23},{8,24},{9,... | collective-permute-start | bytes 884744 | tf_op jit(solution)/shard_map/ppermute | solution.py:57
  62.0 18.7 %collective-permute-start.24 = (bf16[2,96,768]{2,1,0:T(8,128)(2,1)S(1)}, bf16[2,96,768]{2,1,0:T(8,128)(2,1)S(1)}, u32[]{:S(2)}, u32[]{:S(2)}) collective-permute-start(bf16[2,96,768]{2,1,0:T(8,128)(2,1)S(1)} %collective-permute-done.22), channel_id=1, source_target_pairs={{0,16},{1,17},{2,18},{3,19},{4,20},{5,21},{6,22},{7,23},{8,24},{9,... | collective-permute-start | bytes 884744 | tf_op jit(solution)/shard_map/ppermute | solution.py:57
  63.3 23.7 %collective-permute-start.25 = (bf16[2,96,768]{2,1,0:T(8,128)(2,1)S(1)}, bf16[2,96,768]{2,1,0:T(8,128)(2,1)S(1)}, u32[]{:S(2)}, u32[]{:S(2)}) collective-permute-start(bf16[2,96,768]{2,1,0:T(8,128)(2,1)S(1)} %collective-permute-done.23), channel_id=1, source_target_pairs={{0,16},{1,17},{2,18},{3,19},{4,20},{5,21},{6,22},{7,23},{8,24},{9,... | collective-permute-start | bytes 884744 | tf_op jit(solution)/shard_map/ppermute | solution.py:57
  63.5 25.7 %collective-permute-start.18 = (bf16[2,96,768]{2,1,0:T(8,128)(2,1)S(1)}, bf16[2,96,768]{2,1,0:T(8,128)(2,1)S(1)}, u32[]{:S(2)}, u32[]{:S(2)}) collective-permute-start(bf16[2,96,768]{2,1,0:T(8,128)(2,1)S(1)} %collective-permute-done.17), channel_id=1, source_target_pairs={{0,8},{1,9},{2,10},{3,11},{4,12},{5,13},{6,14},{7,15},{8,0},{9,1},... | collective-permute-start | bytes 884744 | tf_op jit(solution)/shard_map/ppermute | solution.py:57
  68.0 21.1 %collective-permute-start.20 = (bf16[2,96,768]{2,1,0:T(8,128)(2,1)S(1)}, bf16[2,96,768]{2,1,0:T(8,128)(2,1)S(1)}, u32[]{:S(2)}, u32[]{:S(2)}) collective-permute-start(bf16[2,96,768]{2,1,0:T(8,128)(2,1)S(1)} %collective-permute-done.19), channel_id=1, source_target_pairs={{0,8},{1,9},{2,10},{3,11},{4,12},{5,13},{6,14},{7,15},{8,0},{9,1},... | collective-permute-start | bytes 884744 | tf_op jit(solution)/shard_map/ppermute | solution.py:57
  75.5 54.6 %collective-permute-start.16 = (bf16[4,2,96,768]{3,2,1,0:T(8,128)(2,1)S(1)}, bf16[4,2,96,768]{3,2,1,0:T(8,128)(2,1)}, u32[]{:S(2)}, u32[]{:S(2)}) collective-permute-start(bf16[4,2,96,768]{3,2,1,0:T(8,128)(2,1)S(1)} %pad_maximum_fusion.rest_0_), channel_id=1, source_target_pairs={{0,4},{1,5},{2,6},{3,7},{4,0},{5,1},{6,2},{7,3},{8,12},{9,13},{10,... | collective-permute-start | bytes 3538952 | tf_op jit(solution)/shard_map/ppermute | solution.py:57
  87.2 42.9 %collective-permute-start.26 = (bf16[4,2,96,768]{3,2,1,0:T(8,128)(2,1)S(1)}, bf16[4,2,96,768]{3,2,1,0:T(8,128)(2,1)}, u32[]{:S(2)}, u32[]{:S(2)}) collective-permute-start(bf16[4,2,96,768]{3,2,1,0:T(8,128)(2,1)S(1)} %pad_maximum_fusion.2.rest_4_), channel_id=1, source_target_pairs={{0,4},{1,5},{2,6},{3,7},{4,0},{5,1},{6,2},{7,3},{8,12},{9,13},{10,... | collective-permute-start | bytes 3538952 | tf_op jit(solution)/shard_map/ppermute | solution.py:57
  89.4 40.7 %collective-permute-start.21 = (bf16[4,2,96,768]{3,2,1,0:T(8,128)(2,1)S(1)}, bf16[4,2,96,768]{3,2,1,0:T(8,128)(2,1)}, u32[]{:S(2)}, u32[]{:S(2)}) collective-permute-start(bf16[4,2,96,768]{3,2,1,0:T(8,128)(2,1)S(1)} %pad_maximum_fusion.1.rest_2_), channel_id=1, source_target_pairs={{0,4},{1,5},{2,6},{3,7},{4,0},{5,1},{6,2},{7,3},{8,12},{9,13},{10,... | collective-permute-start | bytes 3538952 | tf_op jit(solution)/shard_map/ppermute | solution.py:57
  90.1 40.0 %collective-permute-start.11 = (bf16[256,768]{1,0:T(8,128)(2,1)}, bf16[256,768]{1,0:T(8,128)(2,1)}, u32[]{:S(2)}, u32[]{:S(2)}) collective-permute-start(bf16[256,768]{1,0:T(8,128)(2,1)} %bitcast.5), channel_id=1, source_target_pairs={{0,0},{1,1},{2,4},{3,5},{4,2},{5,3},{6,6},{7,7},{8,8},{9,9},{10,12... | collective-permute-start | bytes 1179656 | tf_op jit(solution)/shard_map/ppermute | solution.py:72
  113.2 12.1 %collective-permute-start.6 = (bf16[384,128]{1,0:T(8,128)(2,1)}, bf16[384,128]{1,0:T(8,128)(2,1)}, u32[]{:S(2)}, u32[]{:S(2)}) collective-permute-start(bf16[384,128]{1,0:T(8,128)(2,1)} %get-tuple-element.73), channel_id=1, source_target_pairs={{0,4},{1,5},{2,6},{3,7},{4,0},{5,1},{6,2},{7,3},{8,12},{9,13},{10,... | collective-permute-start | bytes 294920 | tf_op jit(solution)/shard_map/ppermute | solution.py:57
  159.7 56.5 %collective-permute-start.49 = (bf16[4,4,96,768]{3,2,1,0:T(8,128)(2,1)S(1)}, bf16[4,4,96,768]{3,2,1,0:T(8,128)(2,1)S(1)}, u32[]{:S(2)}, u32[]{:S(2)}) collective-permute-start(bf16[4,4,96,768]{3,2,1,0:T(8,128)(2,1)S(1)} %copy-done.28), channel_id=1, source_target_pairs={{0,4},{1,5},{2,6},{3,7},{4,0},{5,1},{6,2},{7,3},{8,12},{9,13},{10,... | collective-permute-start | bytes 7077896 | tf_op jit(solution)/shard_map/ppermute | solution.py:57
  160.4 21.3 %collective-permute-start.35 = (bf16[768,192]{1,0:T(8,128)(2,1)S(1)}, bf16[768,192]{1,0:T(8,128)(2,1)S(1)}, u32[]{:S(2)}, u32[]{:S(2)}) collective-permute-start(bf16[768,192]{1,0:T(8,128)(2,1)S(1)} %add_convert_fusion.5), channel_id=1, source_target_pairs={{0,1},{1,0},{2,3},{3,2},{4,5},{5,4},{6,7},{7,6},{8,9},{9,8},{10,11... | collective-permute-start | bytes 884744 | tf_op jit(solution)/shard_map/ppermute | solution.py:57
  187.1 8.6 %collective-permute-start.38 = (bf16[384,384]{1,0:T(8,128)(2,1)}, bf16[384,384]{1,0:T(8,128)(2,1)S(1)}, u32[]{:S(2)}, u32[]{:S(2)}) collective-permute-start(bf16[384,384]{1,0:T(8,128)(2,1)} %get-tuple-element.109), channel_id=1, source_target_pairs={{0,16},{1,17},{2,18},{3,19},{4,20},{5,21},{6,22},{7,23},{8,24},{9,... | collective-permute-start | bytes 884744 | tf_op jit(solution)/shard_map/ppermute | solution.py:57
  188.3 9.6 %collective-permute-start.36 = (bf16[416,384]{1,0:T(8,128)(2,1)}, bf16[416,384]{1,0:T(8,128)(2,1)S(1)}, u32[]{:S(2)}, u32[]{:S(2)}) collective-permute-start(bf16[416,384]{1,0:T(8,128)(2,1)} %get-tuple-element.107), channel_id=1, source_target_pairs={{0,8},{1,9},{2,10},{3,11},{4,12},{5,13},{6,14},{7,15},{8,0},{9,1},... | collective-permute-start | bytes 958472 | tf_op jit(solution)/shard_map/ppermute | solution.py:57
  189.6 27.1 %collective-permute-start.52 = (bf16[4,4,96,768]{3,2,1,0:T(8,128)(2,1)S(1)}, bf16[4,4,96,768]{3,2,1,0:T(8,128)(2,1)S(1)}, u32[]{:S(2)}, u32[]{:S(2)}) collective-permute-start(bf16[4,4,96,768]{3,2,1,0:T(8,128)(2,1)S(1)} %copy-done.27), channel_id=1, source_target_pairs={{0,4},{1,5},{2,6},{3,7},{4,0},{5,1},{6,2},{7,3},{8,12},{9,13},{10,... | collective-permute-start | bytes 7077896 | tf_op jit(solution)/shard_map/ppermute | solution.py:57
  208.7 20.3 %collective-permute-start.43 = (bf16[112,768]{1,0:T(8,128)(2,1)S(1)}, bf16[112,768]{1,0:T(8,128)(2,1)S(1)}, u32[]{:S(2)}, u32[]{:S(2)}) collective-permute-start(bf16[112,768]{1,0:T(8,128)(2,1)S(1)} %add_convert_fusion.8), channel_id=1, source_target_pairs={{0,3},{1,2},{2,1},{3,0},{4,7},{5,6},{6,5},{7,4},{8,11},{9,10},{10,... | collective-permute-start | bytes 516104 | tf_op jit(solution)/shard_map/ppermute | solution.py:57
  215.8 13.2 %collective-permute-start.42 = (bf16[112,768]{1,0:T(8,128)(2,1)S(1)}, bf16[112,768]{1,0:T(8,128)(2,1)S(1)}, u32[]{:S(2)}, u32[]{:S(2)}) collective-permute-start(bf16[112,768]{1,0:T(8,128)(2,1)S(1)} %add_convert_fusion.8), channel_id=1, source_target_pairs={{0,2},{1,3},{2,0},{3,1},{4,6},{5,7},{6,4},{7,5},{8,10},{9,11},{10,... | collective-permute-start | bytes 516104 | tf_op jit(solution)/shard_map/ppermute | solution.py:57
  215.8 10.1 %collective-permute-start.41 = (bf16[112,768]{1,0:T(8,128)(2,1)S(1)}, bf16[112,768]{1,0:T(8,128)(2,1)S(1)}, u32[]{:S(2)}, u32[]{:S(2)}) collective-permute-start(bf16[112,768]{1,0:T(8,128)(2,1)S(1)} %add_convert_fusion.8), channel_id=1, source_target_pairs={{0,1},{1,0},{2,3},{3,2},{4,5},{5,4},{6,7},{7,6},{8,9},{9,8},{10,11... | collective-permute-start | bytes 516104 | tf_op jit(solution)/shard_map/ppermute | solution.py:57
  216.5 20.3 %collective-permute-start.50 = (bf16[2,4,96,768]{3,2,1,0:T(8,128)(2,1)S(1)}, bf16[2,4,96,768]{3,2,1,0:T(8,128)(2,1)S(1)}, u32[]{:S(2)}, u32[]{:S(2)}) collective-permute-start(bf16[2,4,96,768]{3,2,1,0:T(8,128)(2,1)S(1)} %add_convert_fusion.1), channel_id=1, source_target_pairs={{0,8},{1,9},{2,10},{3,11},{4,12},{5,13},{6,14},{7,15},{8,0},{9,1},... | collective-permute-start | bytes 3538952 | tf_op jit(solution)/shard_map/ppermute | solution.py:57
  218.2 22.5 %collective-permute-start.53 = (bf16[2,4,96,768]{3,2,1,0:T(8,128)(2,1)S(1)}, bf16[2,4,96,768]{3,2,1,0:T(8,128)(2,1)S(1)}, u32[]{:S(2)}, u32[]{:S(2)}) collective-permute-start(bf16[2,4,96,768]{3,2,1,0:T(8,128)(2,1)S(1)} %add_convert_fusion), channel_id=1, source_target_pairs={{0,16},{1,17},{2,18},{3,19},{4,20},{5,21},{6,22},{7,23},{8,24},{9,... | collective-permute-start | bytes 3538952 | tf_op jit(solution)/shard_map/ppermute | solution.py:57
  229.1 21.4 %collective-permute-start.45 = (bf16[384,768]{1,0:T(8,128)(2,1)S(1)}, bf16[384,768]{1,0:T(8,128)(2,1)S(1)}, u32[]{:S(2)}, u32[]{:S(2)}) collective-permute-start(bf16[384,768]{1,0:T(8,128)(2,1)S(1)} %pad_maximum_fusion.5), channel_id=1, source_target_pairs={{0,16},{1,17},{2,18},{3,19},{4,20},{5,21},{6,22},{7,23},{8,24},{9,... | collective-permute-start | bytes 1769480 | tf_op jit(solution)/shard_map/ppermute | solution.py:57
  230.5 20.1 %collective-permute-start.44 = (bf16[384,768]{1,0:T(8,128)(2,1)S(1)}, bf16[384,768]{1,0:T(8,128)(2,1)S(1)}, u32[]{:S(2)}, u32[]{:S(2)}) collective-permute-start(bf16[384,768]{1,0:T(8,128)(2,1)S(1)} %pad_maximum_fusion.5), channel_id=1, source_target_pairs={{0,8},{1,9},{2,10},{3,11},{4,12},{5,13},{6,14},{7,15},{8,0},{9,1},... | collective-permute-start | bytes 1769480 | tf_op jit(solution)/shard_map/ppermute | solution.py:57
  237.0 26.2 %collective-permute-start.51 = (bf16[4,96,768]{2,1,0:T(8,128)(2,1)S(1)}, bf16[4,96,768]{2,1,0:T(8,128)(2,1)S(1)}, u32[]{:S(2)}, u32[]{:S(2)}) collective-permute-start(bf16[4,96,768]{2,1,0:T(8,128)(2,1)S(1)} %fusion), channel_id=1, source_target_pairs={{0,16},{1,17},{2,18},{3,19},{4,20},{5,21},{6,22},{7,23},{8,24},{9,... | collective-permute-start | bytes 1769480 | tf_op jit(solution)/shard_map/ppermute | solution.py:57
  240.9 22.5 %collective-permute-start.54 = (bf16[4,96,768]{2,1,0:T(8,128)(2,1)S(1)}, bf16[4,96,768]{2,1,0:T(8,128)(2,1)S(1)}, u32[]{:S(2)}, u32[]{:S(2)}) collective-permute-start(bf16[4,96,768]{2,1,0:T(8,128)(2,1)S(1)} %fusion.1), channel_id=1, source_target_pairs={{0,8},{1,9},{2,10},{3,11},{4,12},{5,13},{6,14},{7,15},{8,0},{9,1},... | collective-permute-start | bytes 1769480 | tf_op jit(solution)/shard_map/ppermute | solution.py:57
  250.6 20.5 %collective-permute-start.47 = (bf16[192,768]{1,0:T(8,128)(2,1)S(1)}, bf16[192,768]{1,0:T(8,128)(2,1)S(1)}, u32[]{:S(2)}, u32[]{:S(2)}) collective-permute-start(bf16[192,768]{1,0:T(8,128)(2,1)S(1)} %slice.368), channel_id=1, source_target_pairs={{0,8},{1,9},{2,10},{3,11},{4,12},{5,13},{6,14},{7,15},{8,0},{9,1},... | collective-permute-start | bytes 884744 | tf_op jit(solution)/shard_map/ppermute | solution.py:57
  250.7 20.3 %collective-permute-start.46 = (bf16[192,768]{1,0:T(8,128)(2,1)S(1)}, bf16[192,768]{1,0:T(8,128)(2,1)S(1)}, u32[]{:S(2)}, u32[]{:S(2)}) collective-permute-start(bf16[192,768]{1,0:T(8,128)(2,1)S(1)} %slice.367), channel_id=1, source_target_pairs={{0,16},{1,17},{2,18},{3,19},{4,20},{5,21},{6,22},{7,23},{8,24},{9,... | collective-permute-start | bytes 884744 | tf_op jit(solution)/shard_map/ppermute | solution.py:57
  263.8 14.9 %collective-permute-start.56 = (bf16[2,96,768]{2,1,0:T(8,128)(2,1)S(1)}, bf16[2,96,768]{2,1,0:T(8,128)(2,1)S(1)}, u32[]{:S(2)}, u32[]{:S(2)}) collective-permute-start(bf16[2,96,768]{2,1,0:T(8,128)(2,1)S(1)} %pad_maximum_fusion.8), channel_id=1, source_target_pairs={{0,2},{1,3},{2,0},{3,1},{4,6},{5,7},{6,4},{7,5},{8,10},{9,11},{10,... | collective-permute-start | bytes 884744 | tf_op jit(solution)/shard_map/ppermute | solution.py:57
  268.2 10.5 %collective-permute-start.57 = (bf16[2,96,768]{2,1,0:T(8,128)(2,1)S(1)}, bf16[2,96,768]{2,1,0:T(8,128)(2,1)S(1)}, u32[]{:S(2)}, u32[]{:S(2)}) collective-permute-start(bf16[2,96,768]{2,1,0:T(8,128)(2,1)S(1)} %pad_maximum_fusion.9), channel_id=1, source_target_pairs={{0,3},{1,2},{2,1},{3,0},{4,7},{5,6},{6,5},{7,4},{8,11},{9,10},{10,... | collective-permute-start | bytes 884744 | tf_op jit(solution)/shard_map/ppermute | solution.py:57
  270.6 10.3 %collective-permute-start.55 = (bf16[2,96,768]{2,1,0:T(8,128)(2,1)S(1)}, bf16[2,96,768]{2,1,0:T(8,128)(2,1)S(1)}, u32[]{:S(2)}, u32[]{:S(2)}) collective-permute-start(bf16[2,96,768]{2,1,0:T(8,128)(2,1)S(1)} %pad_maximum_fusion.7), channel_id=1, source_target_pairs={{0,1},{1,0},{2,3},{3,2},{4,5},{5,4},{6,7},{7,6},{8,9},{9,8},{10,11... | collective-permute-start | bytes 884744 | tf_op jit(solution)/shard_map/ppermute | solution.py:57
  281.1 18.2 %collective-permute-start.59 = (bf16[2,96,768]{2,1,0:T(8,128)(2,1)S(1)}, bf16[2,96,768]{2,1,0:T(8,128)(2,1)S(1)}, u32[]{:S(2)}, u32[]{:S(2)}) collective-permute-start(bf16[2,96,768]{2,1,0:T(8,128)(2,1)S(1)} %fusion.4), channel_id=1, source_target_pairs={{0,16},{1,17},{2,18},{3,19},{4,20},{5,21},{6,22},{7,23},{8,24},{9,... | collective-permute-start | bytes 884744 | tf_op jit(solution)/shard_map/ppermute | solution.py:57
  283.8 57.4 %collective-permute-start.48 = (bf16[1552,768]{1,0:T(8,128)(2,1)S(1)}, bf16[1552,768]{1,0:T(8,128)(2,1)S(1)}, u32[]{:S(2)}, u32[]{:S(2)}) collective-permute-start(bf16[1552,768]{1,0:T(8,128)(2,1)S(1)} %fusion.11.c_ref), channel_id=1, source_target_pairs={{0,4},{1,5},{2,6},{3,7},{4,0},{5,1},{6,2},{7,3},{8,12},{9,13},{10,... | collective-permute-start | bytes 7151624 | tf_op jit(solution)/shard_map/ppermute | solution.py:57
  294.7 8.6 %collective-permute-start.58 = (bf16[2,96,768]{2,1,0:T(8,128)(2,1)S(1)}, bf16[2,96,768]{2,1,0:T(8,128)(2,1)S(1)}, u32[]{:S(2)}, u32[]{:S(2)}) collective-permute-start(bf16[2,96,768]{2,1,0:T(8,128)(2,1)S(1)} %fusion.4), channel_id=1, source_target_pairs={{0,8},{1,9},{2,10},{3,11},{4,12},{5,13},{6,14},{7,15},{8,0},{9,1},... | collective-permute-start | bytes 884744 | tf_op jit(solution)/shard_map/ppermute | solution.py:57
  298.8 11.3 %collective-permute-start.31 = (bf16[512,768]{1,0:T(8,128)(2,1)}, bf16[512,768]{1,0:T(8,128)(2,1)S(1)}, u32[]{:S(2)}, u32[]{:S(2)}) collective-permute-start(bf16[512,768]{1,0:T(8,128)(2,1)} %get-tuple-element.93), channel_id=1, source_target_pairs={{0,4},{1,5},{2,6},{3,7},{4,0},{5,1},{6,2},{7,3},{8,12},{9,13},{10,... | collective-permute-start | bytes 2359304 | tf_op jit(solution)/shard_map/ppermute | solution.py:57
  307.6 42.6 %collective-permute-start.62 = (bf16[4,2,96,768]{3,2,1,0:T(8,128)(2,1)S(1)}, bf16[4,2,96,768]{3,2,1,0:T(8,128)(2,1)S(1)}, u32[]{:S(2)}, u32[]{:S(2)}) collective-permute-start(bf16[4,2,96,768]{3,2,1,0:T(8,128)(2,1)S(1)} %pad_maximum_fusion.3.f_ref), channel_id=1, source_target_pairs={{0,4},{1,5},{2,6},{3,7},{4,0},{5,1},{6,2},{7,3},{8,12},{9,13},{10,... | collective-permute-start | bytes 3538952 | tf_op jit(solution)/shard_map/ppermute | solution.py:57
  310.2 16.5 %collective-permute-start.32 = (bf16[256,768]{1,0:T(8,128)(2,1)S(1)}, bf16[256,768]{1,0:T(8,128)(2,1)S(1)}, u32[]{:S(2)}, u32[]{:S(2)}) collective-permute-start(bf16[256,768]{1,0:T(8,128)(2,1)S(1)} %add_convert_fusion.7), channel_id=1, source_target_pairs={{0,1},{1,0},{2,3},{3,2},{4,5},{5,4},{6,7},{7,6},{8,9},{9,8},{10,11... | collective-permute-start | bytes 1179656 | tf_op jit(solution)/shard_map/ppermute | solution.py:57
  314.0 16.5 %collective-permute-start.30 = (bf16[256,768]{1,0:T(8,128)(2,1)S(1)}, bf16[256,768]{1,0:T(8,128)(2,1)S(1)}, u32[]{:S(2)}, u32[]{:S(2)}) collective-permute-start(bf16[256,768]{1,0:T(8,128)(2,1)S(1)} %copy-done.29), channel_id=1, source_target_pairs={{0,0},{1,1},{2,4},{3,5},{4,2},{5,3},{6,6},{7,7},{8,8},{9,9},{10,12... | collective-permute-start | bytes 1179656 | tf_op jit(solution)/shard_map/ppermute | solution.py:72
  327.0 14.2 %collective-permute-start.33 = (bf16[256,768]{1,0:T(8,128)(2,1)S(1)}, bf16[256,768]{1,0:T(8,128)(2,1)S(1)}, u32[]{:S(2)}, u32[]{:S(2)}) collective-permute-start(bf16[256,768]{1,0:T(8,128)(2,1)S(1)} %add_convert_fusion.6), channel_id=1, source_target_pairs={{0,0},{1,1},{2,4},{3,5},{4,2},{5,3},{6,6},{7,7},{8,8},{9,9},{10,12... | collective-permute-start | bytes 1179656 | tf_op jit(solution)/shard_map/ppermute | solution.py:72
  (54 other events, 561.4 us)

commit v2 on v1

v2 whole, which is shorter than its diff:
```python
import functools

import jax
import jax.numpy as jnp
from jax import lax
from jax.experimental import pallas as pl
from jax.experimental.pallas import tpu as pltpu
from jax.sharding import PartitionSpec as P

HEADS = 12
BLOCK = 64
HEAD_DIM = 64
TP = 4
GROUP = HEADS // TP
QUARTER = 256
LENGTH = TP * QUARTER
WIDTH = HEADS * HEAD_DIM
GROUP_WIDTH = GROUP * HEAD_DIM
SLOTS = 8
SLICE = WIDTH // SLOTS
VEC_ROWS = 16
CORE, X_BIT, Y_BIT = 1, 2, 4
PLANE_MASKS = (0, X_BIT, Y_BIT, X_BIT | Y_BIT)

epsilon = 1e-05
masked_score = -1e30
score_scale = HEAD_DIM ** (-0.5)
f32 = jnp.float32
bf16 = jnp.bfloat16


def mm(left, right):
    return jnp.dot(left, right, preferred_element_type=f32)


def mm_nt(left, right):
    return lax.dot_general(left, right, (((1,), (1,)), ((), ())), preferred_element_type=f32)


def total(*terms):
    acc = terms[0].astype(f32)
    for term in terms[1:]:
        acc = acc + term.astype(f32)
    return acc


def add_low(*terms):
    return total(*terms).astype(bf16)


def hop(array, dp_mask, z_mask):
    dp_count = lax.axis_size("dp")
    pairs = [
        (d * TP + z, (d ^ dp_mask) * TP + (z ^ z_mask)) for d in range(dp_count) for z in range(TP)
    ]
    return lax.ppermute(array, ("dp", "tp"), pairs)


def place(array):
    dp_count = lax.axis_size("dp")
    pairs = []
    for d in range(dp_count):
        for z in range(TP):
            here = d * TP + z
            away = (d ^ CORE) * TP + (z ^ 2)
            pairs.append((here, here if (d & 1) == z // 2 else away))
    return lax.ppermute(array, ("dp", "tp"), pairs)


def piece_kernel(info, w_in_hbm, w_back_ref, bias_ref, piece_ref, flip_scr, sem):
    start = pl.multiple_of(info[1] * SLICE, SLICE)
    copy = pltpu.make_async_copy(
        w_in_hbm.at[pl.ds(start, SLICE), :], piece_ref.at[pl.ds(0, SLICE), :], sem
    )
    copy.start()
    flip_scr[...] = w_back_ref[...].T
    piece_ref[SLICE : 2 * SLICE, :] = flip_scr[pl.ds(start, SLICE), :]
    bias = bias_ref[...].astype(f32).reshape(1, WIDTH)
    piece_ref[2 * SLICE :, :] = jnp.broadcast_to(bias, (VEC_ROWS, WIDTH)).astype(bf16)
    copy.wait()


def group_kernel(info, w_ref, bias_query_ref, bias_value_ref, w_out, b_out):
    bias_query = bias_query_ref[...].astype(f32).reshape(1, WIDTH)
    bias_value = bias_value_ref[...].astype(f32).reshape(1, WIDTH)
    b_out[...] = jnp.zeros_like(b_out)
    for g in range(TP):

        @pl.when(info[0] == g)
        def _(g=g):
            cols = slice(g * GROUP_WIDTH, (g + 1) * GROUP_WIDTH)
            for kind in range(3):
                lo = kind * GROUP_WIDTH
                w_out[:, lo : lo + GROUP_WIDTH] = w_ref[:, kind * WIDTH :][:, cols]
            b_out[:, :GROUP_WIDTH] = bias_query[:, cols]
            b_out[:, 2 * GROUP_WIDTH :] = bias_value[:, cols]


def block_bias(quarter, native, random_refs, head, chunk):
    shape = (LENGTH // BLOCK, QUARTER)
    row = lax.broadcasted_iota(jnp.int32, shape, 0)
    lane_block = lax.broadcasted_iota(jnp.int32, shape, 1) // BLOCK
    key_block = ((row // TP) ^ quarter) * TP + (row % TP)
    base = TP * (quarter ^ chunk)
    query_block = base + lane_block
    last = LENGTH // BLOCK - 1
    allowed = (key_block == 0) | (key_block == last)
    allowed |= (query_block == 0) | (query_block == last)
    allowed |= jnp.abs(key_block - query_block) <= 1
    for pick in range(3):
        chosen = jnp.zeros(shape, jnp.int32)
        for b in range(TP):
            at = (head * (LENGTH // BLOCK) + base + b) * 3 + pick
            value = jnp.where(native == 1, random_refs[0][at], random_refs[1][at])
            chosen = jnp.where(lane_block == b, value, chosen)
        allowed |= key_block == chosen
    return jnp.where(allowed, 0.0, masked_score).astype(f32)


def biased(scores, bias):
    blocks = LENGTH // BLOCK
    spread = scores.reshape(blocks, BLOCK, QUARTER) + bias.reshape(blocks, 1, QUARTER)
    return spread.reshape(LENGTH, QUARTER)


PACKED = QUARTER + QUARTER // 2


def pack_heads(ref, row, pieces):
    end = row + QUARTER
    ref[row:end, 0:64] = pieces[0]
    ref[row:end, 64:128] = pieces[1]
    ref[end : row + PACKED, 0:64] = pieces[2][: QUARTER // 2]
    ref[end : row + PACKED, 64:128] = pieces[2][QUARTER // 2 :]


def unpack_heads(ref, row):
    end = row + QUARTER
    third = jnp.concatenate([ref[end : row + PACKED, 0:64], ref[end : row + PACKED, 64:128]], axis=0)
    return [ref[row:end, 0:64], ref[row:end, 64:128], third]


def attention_kernel(info, rnd_own, rnd_other, t0, t1, t2, t3, w_ref, b_ref, a0, a13, a2, *rest):
    heads, lse_ref, out_scr = rest[:9], rest[9], rest[10]
    quarter, native = info[0], info[4]
    for slot, t_ref in enumerate((t0, t1, t2, t3)):
        rows = pl.ds(slot * QUARTER, QUARTER)
        proj = mm(t_ref[...], w_ref[...]) + b_ref[...]
        for h in range(GROUP):
            for kind in range(3):
                lo = kind * GROUP_WIDTH + h * HEAD_DIM
                piece = proj[:, lo : lo + HEAD_DIM].astype(bf16)
                if kind == 0:
                    piece = (piece.astype(f32) * score_scale).astype(bf16)
                heads[3 * h + kind][rows, :] = piece
    for h in range(GROUP):
        q_ref, k_ref, v_ref = heads[3 * h : 3 * h + 3]
        keys = k_ref[...]
        values_t = v_ref[...].T

        def chunk_step(chunk, carry, h=h, q_ref=q_ref, keys=keys, values_t=values_t):
            rows = pl.ds(pl.multiple_of(chunk * QUARTER, QUARTER), QUARTER)
            scores = mm_nt(keys, q_ref[rows, :])
            head = quarter * GROUP + h
            scores = biased(scores, block_bias(quarter, native, (rnd_own, rnd_other), head, chunk))
            row_max = jnp.max(scores, axis=0, keepdims=True)
            probs = jnp.exp(scores - row_max)
            row_sum = jnp.sum(probs, axis=0, keepdims=True)
            out_t = mm(values_t, probs.astype(bf16)) / row_sum
            out_scr[h, rows, :] = out_t.T.astype(bf16)
            lse_ref[pl.ds(h * TP + chunk, 1), :] = row_max + jnp.log(row_sum)
            return carry

        lax.fori_loop(0, TP, chunk_step, 0, unroll=True)
    for slot, (a_ref, row) in enumerate(((a0, 0), (a13, 0), (a2, 0), (a13, PACKED))):
        rows = slice(slot * QUARTER, (slot + 1) * QUARTER)
        pack_heads(a_ref, row, [out_scr[h, rows, :] for h in range(GROUP)])


def attention_back_kernel(
    h, info, rnd_own, rnd_other, q_ref, k_ref, v_ref, lse_ref, g0, g1, g2, g3, out_ref, sums_ref, do_scr, dk_scr, dv_scr, dq_scr
):
    quarter, native = info[0], info[4]
    for slot, g_ref in enumerate((g0, g1, g2, g3)):
        do_scr[slot * QUARTER : (slot + 1) * QUARTER, :] = unpack_heads(g_ref, 0)[h]
    keys = k_ref[...]
    keys_t = keys.T
    values = v_ref[...]
    dk_scr[...] = jnp.zeros_like(dk_scr)
    dv_scr[...] = jnp.zeros_like(dv_scr)

    def chunk_step(chunk, carry):
        rows = pl.ds(pl.multiple_of(chunk * QUARTER, QUARTER), QUARTER)
        queries = q_ref[rows, :]
        grad_out = do_scr[rows, :]
        scores = mm_nt(keys, queries)
        head = quarter * GROUP + h
        scores = biased(scores, block_bias(quarter, native, (rnd_own, rnd_other), head, chunk))
        probs = jnp.exp(scores - lse_ref[pl.ds(h * TP + chunk, 1), :])
        grad_probs = mm_nt(values, grad_out)
        delta = jnp.sum(probs * grad_probs, axis=0, keepdims=True)
        grad_scores = (probs * (grad_probs - delta)).astype(bf16)
        dv_scr[...] += mm(probs.astype(bf16), grad_out)
        dk_scr[...] += mm(grad_scores, queries)
        dq_t = mm(keys_t, grad_scores) * score_scale
        dq_scr[rows, :] = dq_t.T
        return carry

    lax.fori_loop(0, TP, chunk_step, 0, unroll=True)
    for n, scr in enumerate((dq_scr, dk_scr, dv_scr)):
        out_ref[:, n * HEAD_DIM : (n + 1) * HEAD_DIM] = scr[...].astype(bf16)
    sums_ref[...] = jnp.zeros_like(sums_ref)
    sums_ref[0:1, :] = jnp.sum(out_ref[...].astype(f32), axis=0, keepdims=True)


PIECE = 2 * SLICE + VEC_ROWS


def held_kernel(own, by_x, by_y, third, third_x, third_y, out):
    for q in range(2):
        for p, ref in enumerate((own, by_x, by_y)):
            at = (4 * q + p) * PIECE
            out[at : at + PIECE] = ref[q * PIECE : (q + 1) * PIECE]
        at = (4 * q + 3) * PIECE
        out[at : at + CUT] = third_y[PIECE + q * CUT : PIECE + (q + 1) * CUT]
        out[at + CUT : at + PIECE] = third_x[PIECE + q * (PIECE - CUT) : PIECE + (q + 1) * (PIECE - CUT)]
    for p, ref in enumerate((third, third_x, third_y)):
        at = (8 + p) * PIECE
        out[at : at + PIECE] = ref[:PIECE]


def assemble_kernel(info, held, other, last_in, last_back, other_last, w_out_ref, w_in_s, w_back_s, w_out_s, bias_s):
    quarter, mine = info[0], info[1]
    for slot in range(TP):
        start = pl.multiple_of((quarter ^ slot) * GROUP_WIDTH, GROUP_WIDTH)
        w_out_s[slot * GROUP_WIDTH : (slot + 1) * GROUP_WIDTH, :] = w_out_ref[pl.ds(start, GROUP_WIDTH), :]
    for side, main in enumerate((held, other)):
        for q in range(TP - 1):
            for p in range(4):
                start = pl.multiple_of((mine ^ PLANE_MASKS[p] ^ side) * SLICE, SLICE)
                at = (4 * q + p) * PIECE
                if q == TP - 2 and p == 3:
                    left = other_last[:SLICE] if side else last_in[...]
                    right = other_last[SLICE : 2 * SLICE] if side else last_back[:SLICE]
                else:
                    left, right = main[at : at + SLICE], main[at + SLICE : at + 2 * SLICE]
                w_in_s[q, pl.ds(start, SLICE), :] = left
                w_back_s[q, pl.ds(start, SLICE), :] = right
                if p == 0 and side == 0:
                    bias_s[q] = main[at + 2 * SLICE : at + PIECE]


def row(ref):
    return ref[...].astype(f32).reshape(1, WIDTH)


def spread(h):
    centred = h - jnp.mean(h, axis=-1, keepdims=True)
    scale = lax.rsqrt(jnp.mean(centred * centred, axis=-1, keepdims=True) + epsilon)
    return centred * scale, scale


def spread_back(grad, gain, normal, scale):
    weighted = grad * gain
    mean_one = jnp.mean(weighted, axis=-1, keepdims=True)
    mean_two = jnp.mean(weighted * normal, axis=-1, keepdims=True)
    return scale * (weighted - mean_one - normal * mean_two)


def ffn_kernel(info, t_ref, a0, a1, a2, a3, *rest):
    bias_out_ref, gain_one_ref, shift_one_ref, bias_back_ref, gain_two_ref, shift_two_ref, bias_in_ref = rest[:7]
    cot_ref, w_out_s, w_in_ref, w_back_ref, w_in_s, w_back_s, bias_s = rest[7:14]
    lo_ref, first_ref, second_ref, x_ref, gb_ref, act_ref, gp_ref, att_ref, vec_ref = rest[14:]
    for slot, a_ref in enumerate((a0, a1, a2, a3)):
        for h, piece in enumerate(unpack_heads(a_ref, 0)):
            lo = slot * GROUP_WIDTH + h * HEAD_DIM
            att_ref[:, lo : lo + HEAD_DIM] = piece
    first_in = t_ref[...].astype(f32) + (mm(att_ref[...], w_out_s[...]) + row(bias_out_ref))
    first_ref[...] = first_in
    first_norm = spread(first_in)[0] * row(gain_one_ref) + row(shift_one_ref)
    x = first_norm.astype(bf16)
    x_ref[...] = x
    branch = jnp.zeros((QUARTER, WIDTH), f32)
    for q in range(TP):
        cols = slice(q * WIDTH, (q + 1) * WIDTH)
        bias_q = bias_s[q - 1, 0:1, :].astype(f32) if q else row(bias_in_ref)
        pre = mm(x, w_in_s[q - 1] if q else w_in_ref[...]) + bias_q
        inner = 0.7978845608028654 * (pre + 0.044715 * pre * pre * pre)
        tanh = jnp.tanh(inner)
        half = 0.5 * (1.0 + tanh)
        act = (pre * half).astype(bf16)
        act_ref[:, cols] = act
        slope = 0.7978845608028654 * (1.0 + 3.0 * 0.044715 * pre * pre)
        gp_ref[:, cols] = half + 0.5 * pre * (1.0 - tanh * tanh) * slope
        branch = branch + (mm_nt(act, w_back_s[q - 1]) if q else mm(act, w_back_ref[...]))
    second_in = first_norm + branch + row(bias_back_ref)
    normal_two, scale_two = spread(second_in)
    lo_ref[...] = (normal_two * row(gain_two_ref) + row(shift_two_ref)).astype(bf16)
    grad_out = cot_ref[...].astype(f32)
    grad_second = spread_back(grad_out, row(gain_two_ref), normal_two, scale_two)
    second_ref[...] = grad_second
    grad_branch = grad_second.astype(bf16)
    gb_ref[...] = grad_branch
    vec_ref[...] = jnp.zeros_like(vec_ref)
    vec_ref[0:1, :] = jnp.sum(grad_out, axis=0, keepdims=True)
    vec_ref[1:2, :] = jnp.sum(grad_out * normal_two, axis=0, keepdims=True)
    vec_ref[2:3, :] = jnp.sum(grad_branch.astype(f32), axis=0, keepdims=True)


def position_mask(position, order):
    mask = 0
    for n, bit in enumerate(order):
        if (position >> (2 - n)) & 1:
            mask |= bit
    return mask


FFN_ORDERS = ((CORE, X_BIT, Y_BIT), (CORE, Y_BIT, X_BIT))


def weight_grads(info, left, right, keep, send, flip_scr, lhs_scr):
    mine = info[1]
    flip_scr[...] = left[...].T
    for n, order in enumerate(FFN_ORDERS):
        for p in range(SLOTS):
            start = pl.multiple_of((mine ^ position_mask(p, order)) * SLICE, SLICE)
            lhs_scr[p * SLICE : (p + 1) * SLICE, :] = flip_scr[pl.ds(start, SLICE), :]
        for pair in range(2):
            q = 2 * n + pair
            product = mm(lhs_scr[...], right[:, q * WIDTH : (q + 1) * WIDTH]).astype(bf16)
            for p in range(SLOTS):
                out = send if p >= SLOTS // 2 else keep
                out[n, p % (SLOTS // 2), pair] = product[p * SLICE : (p + 1) * SLICE, :]


def ffn_back_kernel(info, first_ref, second_ref, gb_ref, gp_ref, gain_one_ref, vec_in, *rest):
    w_out_s, w_in_ref, w_back_ref, w_in_s, w_back_s, x_ref, att_ref = rest[:7]
    g0, g13, g2, gin_ref, vec_ref, keep, send, go_keep, go_send = rest[7:16]
    gpre_ref, flip_scr, lhs_scr = rest[16:]
    grad_branch = gb_ref[...]
    grad_first = second_ref[...]
    vec_ref[...] = vec_in[...]
    for q in range(TP):
        cols = slice(q * WIDTH, (q + 1) * WIDTH)
        grad_act = mm(grad_branch, w_back_s[q - 1]) if q else mm_nt(grad_branch, w_back_ref[...])
        grad_pre = (grad_act * gp_ref[:, cols]).astype(bf16)
        gpre_ref[:, cols] = grad_pre
        vec_ref[pl.ds(6 + (info[2] ^ q), 1), :] = jnp.sum(grad_pre.astype(f32), axis=0, keepdims=True)
        grad_first = grad_first + mm_nt(grad_pre, w_in_s[q - 1] if q else w_in_ref[...])
    normal_one, scale_one = spread(first_ref[...])
    vec_ref[3:4, :] = jnp.sum(grad_first, axis=0, keepdims=True)
    vec_ref[4:5, :] = jnp.sum(grad_first * normal_one, axis=0, keepdims=True)
    grad_in = spread_back(grad_first, row(gain_one_ref), normal_one, scale_one)
    gin_ref[...] = grad_in
    grad_mixed = grad_in.astype(bf16)
    vec_ref[5:6, :] = jnp.sum(grad_mixed.astype(f32), axis=0, keepdims=True)
    grad_att = mm_nt(grad_mixed, w_out_s[...]).astype(bf16)
    for slot, (g_ref, row_at) in enumerate(((g0, 0), (g13, 0), (g2, 0), (g13, PACKED))):
        lo = slot * GROUP_WIDTH
        pack_heads(
            g_ref, row_at, [grad_att[:, lo + h * HEAD_DIM : lo + (h + 1) * HEAD_DIM] for h in range(GROUP)]
        )
    weight_grads(info, x_ref, gpre_ref, keep, send, flip_scr, lhs_scr)
    product = mm(grad_mixed.T, att_ref[...]).astype(bf16)
    go_keep[...] = product[:, : 2 * GROUP_WIDTH]
    go_send[...] = product[:, 2 * GROUP_WIDTH :]


ORDER_LA = (4, 2, 1)
ORDER_LB = (2, 4, 1)


HALF = WIDTH // 2
HELD = SLOTS // 2 * SLICE


def flip_kernel(t0, t1, t2, t3, out_ref):
    for slot, t_ref in enumerate((t0, t1, t2, t3)):
        out_ref[:, slot * QUARTER : (slot + 1) * QUARTER] = t_ref[...].T


def qkv_grad_kernel(
    info, tokens_t, gh0, gh1, gh2, go_own, go_near, vec_ref, s0, s1, s2, la_keep, la_send, lb_keep, lb_send, out_scr
):
    quarter, here = info[0], info[3]
    for h, gh_ref in enumerate((gh0, gh1, gh2)):
        product = mm(tokens_t[...], gh_ref[...]).astype(bf16)
        for kind in range(3):
            lo = kind * GROUP_WIDTH + h * HEAD_DIM
            out_scr[:, lo : lo + HEAD_DIM] = product[:, kind * HEAD_DIM : (kind + 1) * HEAD_DIM]
    add_to(out_scr.at[:, 3 * GROUP_WIDTH :], go_own[...], go_near[...])
    for keep, send, order, lo in (
        (la_keep, la_send, ORDER_LA, 0),
        (lb_keep, lb_send, ORDER_LB, HALF),
    ):
        for p in range(SLOTS):
            start = pl.multiple_of((here ^ position_mask(p, order)) * SLICE, SLICE)
            out = send if p >= SLOTS // 2 else keep
            row = p % (SLOTS // 2) * SLICE
            out[row : row + SLICE, :] = out_scr[pl.ds(start, SLICE), lo : lo + HALF]
    placed = []
    for kind in (0, 2):
        cols = slice(kind * HEAD_DIM, (kind + 1) * HEAD_DIM)
        piece = jnp.concatenate([sums[0:1, cols] for sums in (s0, s1, s2)], axis=1)
        placed.append(
            jnp.concatenate([jnp.where(quarter == g, piece, 0.0) for g in range(TP)], axis=1)
        )
    vectors = jnp.concatenate([vec_ref[0:10, :]] + placed + [vec_ref[12:VEC_ROWS, :]], axis=0)
    vectors = vectors.astype(bf16)
    for out in (la_keep, la_send):
        out[HELD : HELD + VEC_ROWS, :] = vectors[:, :HALF]
        out[HELD + VEC_ROWS :, :] = vectors[:, HALF:]


def token_grad_kernel(gh0, gh1, gh2, w_ref, keep_ref, send_ref, all_scr):
    for h, gh_ref in enumerate((gh0, gh1, gh2)):
        for kind in range(3):
            lo = kind * GROUP_WIDTH + h * HEAD_DIM
            all_scr[:, lo : lo + HEAD_DIM] = gh_ref[:, kind * HEAD_DIM : (kind + 1) * HEAD_DIM]
    half = LENGTH // 2
    send_ref[...] = mm_nt(all_scr[half:, :], w_ref[...]).astype(bf16)
    keep_ref[...] = mm_nt(all_scr[:half, :], w_ref[...]).astype(bf16)


def ffn_out_kernel(info, f_ref, f_other, w_in_out, w_back_out, flip_scr):
    mine = info[1]
    for side, ref in enumerate((f_ref, f_other)):
        for place_xy in range(4):
            mask = side | (X_BIT if place_xy & 1 else 0) | (Y_BIT if place_xy & 2 else 0)
            start = pl.multiple_of((mine ^ mask) * SLICE, SLICE)
            w_in_out[pl.ds(start, SLICE), :] = ref[place_xy, 0].astype(f32)
            flip_scr[pl.ds(start, SLICE), :] = ref[place_xy, 1].astype(f32)
    w_back_out[...] = flip_scr[...].T


def qkv_out_kernel(info, c_ref, c_other, qkv_out, out_out, *rest):
    vec_outs, (all_scr, flip_scr) = rest[:9], rest[9:]
    quarter, z_here, here = info[0], info[2], info[3]
    count = 16 * SLICE
    for side, ref in enumerate((c_ref, c_other)):
        for n in range(16):
            all_scr[side * 16 + n] = ref[n * SLICE : (n + 1) * SLICE, :]
    vectors = total(c_ref[count:, :], c_other[count:, :])
    bias_in = jnp.zeros((1, WIDTH), f32)
    for q in range(TP):
        bias_in = jnp.where(z_here == q, vectors[6 + q : 7 + q, :], bias_in)
    for out, n in zip(vec_outs[:8], (0, 1, 2, 3, 4, 5, 10, 11)):
        out[...] = vectors[n]
    vec_outs[8][...] = bias_in[0]
    for block in range(SLOTS):
        pieces = []
        for group in range(TP):
            group_off = quarter ^ group
            block_off = here ^ block
            xy = ((block_off >> 2) & 1) + (block_off & 2)
            z_off = (group_off & 1) + 2 * (block_off & 1)
            slot = (group_off >> 1) * 16 + xy * 4 + z_off
            pieces.append(all_scr[slot])
        rows = slice(block * SLICE, (block + 1) * SLICE)
        for kind in range(4):
            cols = slice(kind * GROUP_WIDTH, (kind + 1) * GROUP_WIDTH)
            joined = jnp.concatenate([piece[:, cols] for piece in pieces], axis=1).astype(f32)
            if kind < 3:
                qkv_out[rows, kind * WIDTH : (kind + 1) * WIDTH] = joined
            else:
                flip_scr[rows, :] = joined
    out_out[...] = flip_scr[...].T


def add_to(out, *terms):
    out[...] = add_low(*terms)


def join_kernel(*refs):
    out, at = refs[-1], 0
    for ref in refs[:-1]:
        out[at : at + ref.shape[0]] = ref[...]
        at += ref.shape[0]


def diag_kernel(by_x, by_y, first, second):
    half = first.shape[0]
    first[...] = by_x[:half]
    second[...] = by_y[half:]


CUT = SLICE


def mix_kernel(by_x, by_y, own, to_x, to_y):
    to_x[:PIECE] = own[...]
    to_y[:PIECE] = own[...]
    for n in range(2):
        to_x[PIECE + n * (PIECE - CUT) : PIECE + (n + 1) * (PIECE - CUT)] = by_y[n * PIECE + CUT : (n + 1) * PIECE]
        to_y[PIECE + n * CUT : PIECE + (n + 1) * CUT] = by_x[n * PIECE : n * PIECE + CUT]


def last_mix_kernel(by_x, by_y, to_x, to_y):
    to_x[...] = by_y[CUT:PIECE]
    to_y[...] = by_x[:CUT]


def level_one_kernel(keep, other, first, second):
    add_to(first, keep[0, 2:], other[0, 2:])
    add_to(second, keep[1, 2:], other[1, 2:])


def level_two_kernel(*refs):
    first, second = refs[-2:]
    for n in range(2):
        keep, other, by_x, by_y = refs[4 * n : 4 * n + 4]
        add_to(first.at[n], keep[0, 1], other[0, 1], by_x[1])
        add_to(second.at[n], keep[1, 1], other[1, 1], by_y[1])


def plane_kernel(*refs):
    by_xy, by_yx, near, kept = refs[-4:]
    for n in range(2):
        keep, other, by_x, by_y = refs[4 * n : 4 * n + 4]
        for q in range(TP):
            order, pair = q // 2, q % 2
            first, second = (by_x, by_xy) if order == 0 else (by_y, by_yx)
            out = near if q % 2 else kept
            add_to(
                out.at[q // 2, n], keep[order, 0, pair], other[order, 0, pair], first[0, pair], second[n, pair]
            )


def far_kernel(kept, near, far):
    add_to(far, kept[1], near[1])


def last_kernel(kept, near, far, out):
    for n in range(2):
        add_to(out.at[n], kept[0, 1 - n], near[0, 1 - n], far[1 - n])


def go_kernel(keep, other, own, send):
    add_to(own, keep[:, :GROUP_WIDTH], other[:, :GROUP_WIDTH])
    add_to(send, keep[:, GROUP_WIDTH:], other[:, GROUP_WIDTH:])


def near_kernel(keep, other, out):
    add_to(out, keep[QUARTER:], other[QUARTER:])


def tokens_kernel(keep, other, near, grad_in, out):
    add_to(out, keep[:QUARTER], other[:QUARTER], near[...], grad_in[...])


TWO = 2 * SLICE


def qkv_two_kernel(la, ra, lb, rb, la_out, lb_out):
    add_to(la_out, la[TWO:], ra[TWO:])
    add_to(lb_out, lb[TWO:], rb[TWO:])


def qkv_three_kernel(la, ra, ra2, lb, rb, rb2, out):
    add_to(out.at[:TWO, :HALF], la[:TWO], ra[:TWO], ra2[:TWO])
    add_to(out.at[:TWO, HALF:], lb[:TWO], rb[:TWO], rb2[...])
    for n in range(2):
        rows = slice(HELD + n * VEC_ROWS, HELD + (n + 1) * VEC_ROWS)
        rows_two = slice(TWO + n * VEC_ROWS, TWO + (n + 1) * VEC_ROWS)
        add_to(out.at[TWO:, n * HALF : (n + 1) * HALF], la[rows], ra[rows], ra2[rows_two])


def qkv_four_kernel(own, other, out):
    add_to(out.at[:SLICE], own[:SLICE], other[SLICE:TWO])
    add_to(out.at[SLICE:TWO], own[SLICE:TWO], other[:SLICE])
    add_to(out.at[TWO:], own[TWO:], other[TWO:])


def mix_l_kernel(by_x, by_y, other, to_x, to_y):
    to_x[:TWO] = other[:TWO]
    to_x[TWO:] = by_y[SLICE:TWO]
    to_y[:TWO] = other[:TWO]
    to_y[TWO:] = by_x[:SLICE]


def diag_l_kernel(by_x, by_y, to_x, to_y):
    to_x[...] = by_y[SLICE:TWO]
    to_y[...] = by_x[:SLICE]


def plane_l_kernel(own, other, x_own, y_own, x_other, y_other, d_x, d_y, out):
    diag_own = (y_other[TWO:], x_other[TWO:])
    diag_other = (d_y[...], d_x[...])
    places = (
        ((own[:SLICE], own[SLICE:TWO]), (other[:SLICE], other[SLICE:TWO])),
        ((x_own[:SLICE], x_own[SLICE:TWO]), (x_other[:SLICE], x_other[SLICE:TWO])),
        ((y_own[:SLICE], y_own[SLICE:TWO]), (y_other[:SLICE], y_other[SLICE:TWO])),
        (diag_own, diag_other),
    )
    for p, (here, there) in enumerate(places):
        for slot in range(TP):
            at = (p * TP + slot) * SLICE
            out[at : at + SLICE] = (there if slot % 2 else here)[slot // 2]
    add_to(out.at[16 * SLICE :], own[TWO:], other[TWO:])


VMEM = pl.BlockSpec(memory_space=pltpu.VMEM)
SMEM = pl.BlockSpec(memory_space=pltpu.SMEM)
HBM = pl.BlockSpec(memory_space=pl.ANY)


def call(kernel, in_specs, outs, scratch, vmem_mib, name, deps=()):
    count, extra = len(in_specs), len(deps)

    def body(*refs):
        kernel(*refs[:count], *refs[count + extra :])

    run = pl.pallas_call(
        body,
        out_shape=[jax.ShapeDtypeStruct(shape, dtype) for shape, dtype in outs],
        in_specs=list(in_specs) + [HBM] * extra,
        out_specs=[VMEM] * len(outs),
        scratch_shapes=scratch,
        compiler_params=pltpu.CompilerParams(vmem_limit_bytes=vmem_mib * 1024 * 1024),
        cost_estimate=pl.CostEstimate(flops=1, bytes_accessed=1, transcendentals=0),
        name=name,
    )
    return lambda *arrays: run(*arrays, *deps)


def step(kernel, name, outs, *arrays, deps=()):
    shapes = [(shape, bf16) for shape in outs]
    result = call(kernel, [VMEM] * len(arrays), shapes, [], 12, name, deps)(*arrays)
    return result[0] if len(outs) == 1 else result


def per_device(
    tokens,
    w_qkv,
    bias_query,
    bias_value,
    w_out,
    bias_out,
    gain_attn,
    shift_attn,
    w_in,
    bias_in,
    w_back,
    bias_back,
    gain_ffn,
    shift_ffn,
    random_blocks,
    cotangent,
):
    dp_count = lax.axis_size("dp")
    d = lax.axis_index("dp")
    z = lax.axis_index("tp")
    core = d & 1
    quarter = (z & 1) + 2 * core
    mine = d & (SLOTS - 1)
    here = ((d >> 1) & 1) * 4 + ((d >> 2) & 1) * 2 + (z >> 1)
    native = (core == z // 2).astype(jnp.int32)
    info = jnp.stack([quarter, mine, z, here, native]).astype(jnp.int32)
    extra_bits = [1 << b for b in range(3, dp_count.bit_length() - 1)]

    own_tokens = place(tokens[0])
    piece = call(
        piece_kernel,
        [SMEM, HBM, VMEM, VMEM],
        [((2 * SLICE + VEC_ROWS, WIDTH), bf16)],
        [pltpu.VMEM((WIDTH, WIDTH), bf16), pltpu.SemaphoreType.DMA],
        8,
        "piece",
    )(info, w_in, w_back, bias_in)[0]
    piece_one = hop(piece, 0, 1)
    piece_two = hop(piece, 0, 2)
    random_own = random_blocks.reshape(-1)
    random_other = hop(random_own, CORE, 0)
    w_group, bias_group = call(
        group_kernel,
        [SMEM, VMEM, VMEM, VMEM],
        [((WIDTH, 3 * GROUP_WIDTH), bf16), ((1, 3 * GROUP_WIDTH), f32)],
        [],
        16,
        "group",
    )(info, w_qkv, bias_query, bias_value)
    near_tokens = hop(own_tokens, 0, 1)
    core_tokens = hop(own_tokens, CORE, 0)
    far_tokens = hop(near_tokens, CORE, 0)
    part_one = step(
        join_kernel, "pair", [(2 * PIECE, WIDTH)], piece_one, piece_two, deps=(own_tokens, w_group)
    )
    x_one = hop(part_one, X_BIT, 0)
    y_one = hop(part_one, Y_BIT, 0)
    piece_three = hop(piece_two, 0, 1)
    cot = place(cotangent[0])
    to_x, to_y = step(
        mix_kernel,
        "mix",
        [(3 * PIECE - 2 * CUT, WIDTH), (PIECE + 2 * CUT, WIDTH)],
        x_one,
        y_one,
        piece_three,
        deps=(near_tokens,),
    )
    x_three = hop(to_x, X_BIT, 0)
    y_three = hop(to_y, Y_BIT, 0)

    packed = ((PACKED, 2 * HEAD_DIM), bf16)
    double = ((2 * PACKED, 2 * HEAD_DIM), bf16)
    per_head = ((LENGTH, HEAD_DIM), bf16)
    token_slots = (own_tokens, near_tokens, core_tokens, far_tokens)
    a0, a13, a2, *heads = call(
        attention_kernel,
        [SMEM] * 3 + [VMEM] * 6,
        [packed, double, packed] + [per_head] * 9 + [((16, QUARTER), f32)],
        [pltpu.VMEM((GROUP, LENGTH, HEAD_DIM), bf16)],
        24,
        "attention",
        (to_x, core_tokens),
    )(info, random_own, random_other, *token_slots, w_group, bias_group)
    heads, lse = heads[:9], heads[9]
    a1 = hop(a13, 0, 1)
    a2 = hop(a2, CORE, 0)
    a3 = hop(a1[PACKED:], CORE, 0)
    to_x, to_y = step(
        last_mix_kernel,
        "mix_last",
        [(PIECE - CUT, WIDTH), (CUT, WIDTH)],
        x_three,
        y_three,
        deps=(a0, cot),
    )
    last_back = hop(to_x, X_BIT, 0)
    last_in = hop(to_y, Y_BIT, 0)
    held = step(
        held_kernel,
        "held",
        [(11 * PIECE, WIDTH)],
        part_one,
        x_one,
        y_one,
        piece_three,
        x_three,
        y_three,
        deps=(a2, cot),
    )
    tokens_t = call(flip_kernel, [VMEM] * 4, [((WIDTH, LENGTH), bf16)], [], 8, "flip_tokens", (a1, held))(
        *token_slots
    )[0]
    last = step(join_kernel, "last_piece", [(PIECE, WIDTH)], last_in, last_back, deps=(tokens_t,))
    quarters = ((TP - 1, WIDTH, WIDTH), bf16)
    w_in_s, w_back_s, w_out_s, bias_s = call(
        assemble_kernel,
        [SMEM] + [VMEM] * 6,
        [quarters, quarters, ((WIDTH, WIDTH), bf16), ((TP - 1, VEC_ROWS, WIDTH), bf16)],
        [],
        20,
        "assemble",
    )(info, held, hop(held, CORE, 0), last_in, last_back, hop(last, CORE, 0), w_out)

    rows = ((QUARTER, WIDTH), bf16)
    wide = ((QUARTER, TP * WIDTH), bf16)
    rows_f32 = ((QUARTER, WIDTH), f32)
    vec_rows = ((VEC_ROWS, WIDTH), f32)
    out_here, first_in, grad_second, ffn_input, grad_branch, activated, gelu_slope, attended, vectors = call(
        ffn_kernel,
        [SMEM] + [VMEM] * 19,
        [rows, rows_f32, rows_f32, rows, rows, wide, ((QUARTER, TP * WIDTH), f32), rows, vec_rows],
        [],
        20,
        "ffn",
        (tokens_t,),
    )(
        info,
        own_tokens,
        a0,
        a1,
        a2,
        a3,
        bias_out,
        gain_attn,
        shift_attn,
        bias_back,
        gain_ffn,
        shift_ffn,
        bias_in,
        cot,
        w_out_s,
        w_in,
        w_back,
        w_in_s,
        w_back_s,
        bias_s,
    )
    pairs = ((2, SLOTS // 2, 2, SLICE, WIDTH), bf16)
    halves = ((WIDTH, 2 * GROUP_WIDTH), bf16)
    flips = [pltpu.VMEM((WIDTH, QUARTER), bf16), pltpu.VMEM((WIDTH, QUARTER), bf16)]
    back_keep, back_send = call(
        weight_grads, [SMEM] + [VMEM] * 2, [pairs] * 2, flips, 12, "back_grads"
    )(info, grad_branch, activated)
    back_other = hop(back_send, CORE, 0)

    g0, g13, g2, grad_in, vectors, in_keep, in_send, go_keep, go_send = call(
        ffn_back_kernel,
        [SMEM] + [VMEM] * 13,
        [packed, double, packed, rows_f32, vec_rows] + [pairs] * 2 + [halves] * 2,
        [pltpu.VMEM((QUARTER, TP * WIDTH), bf16)] + flips,
        20,
        "ffn_back",
        (back_keep,),
    )(
        info,
        first_in,
        grad_second,
        grad_branch,
        gelu_slope,
        gain_attn,
        vectors,
        w_out_s,
        w_in,
        w_back,
        w_in_s,
        w_back_s,
        ffn_input,
        attended,
    )
    g1 = hop(g13, 0, 1)
    g2 = hop(g2, CORE, 0)
    g3 = hop(g1[PACKED:], CORE, 0)

    first_level = [(2, 2, SLICE, WIDTH)] * 2
    def hop_pair(pair, first, second):
        return hop(pair[0], first, 0), hop(pair[1], second, 0)

    back_sums = step(level_one_kernel, "back_one", first_level, back_keep, back_other, deps=(g13,))
    back_x, back_y = hop_pair(back_sums, X_BIT, Y_BIT)
    in_other = hop(in_send, CORE, 0)
    go_other = hop(go_send, CORE, 0)

    def head_back(h, deps):
        return call(
            functools.partial(attention_back_kernel, h),
            [SMEM] * 3 + [VMEM] * 8,
            [((LENGTH, 3 * HEAD_DIM), bf16), ((8, 3 * HEAD_DIM), f32)],
            [
                pltpu.VMEM((LENGTH, HEAD_DIM), bf16),
                pltpu.VMEM((LENGTH, HEAD_DIM), f32),
                pltpu.VMEM((LENGTH, HEAD_DIM), f32),
                pltpu.VMEM((LENGTH, HEAD_DIM), f32),
            ],
            12,
            f"attention_back_{h}",
            deps,
        )(info, random_own, random_other, *heads[3 * h : 3 * h + 3], lse, g0, g1, g2, g3)

    go_own, go_send = step(go_kernel, "go", [(WIDTH, GROUP_WIDTH)] * 2, go_keep, go_other)
    go_near = hop(go_send, 0, 1)
    gh0, s0 = head_back(0, (go_own, back_sums[0]))
    sums = step(level_one_kernel, "in_one", first_level, in_keep, in_other, deps=(gh0, back_x, back_y, go_near))
    in_x, in_y = hop_pair(sums, X_BIT, Y_BIT)
    gh1, s1 = head_back(1, (sums[0],))
    gh2, s2 = head_back(2, (gh1,))
    back_parts = [back_keep, back_other, back_x, back_y]
    in_parts = [in_keep, in_other, in_x, in_y]
    sums = step(
        level_two_kernel, "two", [(2, 2, SLICE, WIDTH)] * 2, *back_parts, *in_parts, deps=(gh2,)
    )
    by_xy, by_yx = hop_pair(sums, Y_BIT, X_BIT)
    layer_out = place(out_here)[None]

    la_keep, la_send, lb_keep, lb_send = call(
        qkv_grad_kernel,
        [SMEM] + [VMEM] * 10,
        [((HELD + 2 * VEC_ROWS, HALF), bf16)] * 2 + [((HELD, HALF), bf16)] * 2,
        [pltpu.VMEM((WIDTH, 4 * GROUP_WIDTH), bf16)],
        16,
        "qkv_grads",
        (layer_out, sums[0]),
    )(info, tokens_t, gh0, gh1, gh2, go_own, go_near, vectors, s0, s1, s2)
    ra = hop(la_send, X_BIT, 0)
    rb = hop(lb_send, Y_BIT, 0)

    keep, send = call(
        token_grad_kernel,
        [VMEM] * 4,
        [((LENGTH // 2, WIDTH), bf16)] * 2,
        [pltpu.VMEM((LENGTH, 3 * GROUP_WIDTH), bf16)],
        16,
        "token_grad",
        (la_keep,),
    )(gh0, gh1, gh2, w_group)
    other = hop(send, CORE, 0)
    near_low = step(near_kernel, "near", [(QUARTER, WIDTH)], keep, other)
    near = hop(near_low, 0, 1)

    la2, lb2 = step(
        qkv_two_kernel,
        "qkv_two",
        [(TWO + 2 * VEC_ROWS, HALF), (TWO, HALF)],
        la_keep,
        ra,
        lb_keep,
        rb,
        deps=(near,),
    )
    ra2 = hop(la2, Y_BIT, 0)
    rb2 = hop(lb2, X_BIT, 0)
    rows_l = (TWO + VEC_ROWS, WIDTH)
    partial = step(qkv_three_kernel, "qkv_three", [rows_l], la_keep, ra, ra2, lb_keep, rb, rb2)
    near_sum, kept = step(
        plane_kernel,
        "plane_sum",
        [(2, 2, SLICE, WIDTH)] * 2,
        *back_parts,
        *in_parts,
        by_xy,
        by_yx,
        deps=(la2,),
    )
    near_f = hop(near_sum, 0, 1)
    far_low = step(far_kernel, "far", [(2, SLICE, WIDTH)], kept, near_f, deps=(partial,))
    far_f = hop(far_low, 0, 2)
    low_tokens = step(
        tokens_kernel, "tokens", [(QUARTER, WIDTH)], keep, other, near, grad_in, deps=(partial,)
    )
    sum_l = step(
        qkv_four_kernel, "qkv_four", [rows_l], partial, hop(partial, 0, 2), deps=(far_low, low_tokens)
    )
    for bit in extra_bits:
        sum_l = add_low(sum_l, hop(sum_l, bit, 0))
    grad_tokens = place(low_tokens)[None]

    own_l = sum_l[:TWO]
    x_own = hop(own_l, X_BIT, 0)
    y_own = hop(own_l, Y_BIT, 0)
    other_l = hop(sum_l, 0, 1)
    to_x, to_y = step(
        mix_l_kernel, "mix_l", [(TWO + SLICE, WIDTH)] * 2, x_own, y_own, other_l
    )
    x_other = hop(to_x, X_BIT, 0)
    y_other = hop(to_y, Y_BIT, 0)
    sum_f = step(last_kernel, "last", [(2, SLICE, WIDTH)], kept, near_f, far_f, deps=(to_x,))
    for bit in extra_bits:
        sum_f = add_low(sum_f, hop(sum_f, bit, 0))
    f_x = hop(sum_f, X_BIT, 0)
    f_y = hop(sum_f, Y_BIT, 0)
    diag_l = step(
        diag_l_kernel, "diag_l", [(SLICE, WIDTH)] * 2, x_other, y_other, deps=(sum_f, grad_tokens)
    )
    d_x, d_y = hop_pair(diag_l, X_BIT, Y_BIT)
    diag_f = step(diag_kernel, "diag_f", [(1, SLICE, WIDTH)] * 2, f_x, f_y, deps=(diag_l[0],))
    f_d0, f_d1 = hop_pair(diag_f, Y_BIT, X_BIT)
    f_all = step(join_kernel, "join_f", [(8, SLICE, WIDTH)], sum_f, f_x, f_y, f_d0, f_d1)
    f_all = f_all.reshape(4, 2, SLICE, WIDTH)
    grad_w_in, grad_w_back = call(
        ffn_out_kernel,
        [SMEM, VMEM, VMEM],
        [((WIDTH, WIDTH), f32)] * 2,
        [pltpu.VMEM((WIDTH, WIDTH), f32)],
        24,
        "ffn_out",
    )(info, f_all, hop(f_all, CORE, 0))
    plane = step(
        plane_l_kernel,
        "join_l",
        [(16 * SLICE + VEC_ROWS, WIDTH)],
        sum_l,
        other_l,
        x_own,
        y_own,
        x_other,
        y_other,
        d_x,
        d_y,
        deps=(f_all,),
    )
    grad_w_qkv, grad_w_out, *vec_outs = call(
        qkv_out_kernel,
        [SMEM, VMEM, VMEM],
        [((WIDTH, 3 * WIDTH), f32), ((WIDTH, WIDTH), f32)] + [((WIDTH,), f32)] * 9,
        [pltpu.VMEM((32, SLICE, WIDTH), bf16), pltpu.VMEM((WIDTH, WIDTH), f32)],
        24,
        "qkv_out",
        (grad_w_in,),
    )(info, plane, hop(plane, CORE, 0))
    (
        grad_shift_ffn,
        grad_gain_ffn,
        grad_bias_back,
        grad_shift_attn,
        grad_gain_attn,
        grad_bias_out,
        grad_bias_query,
        grad_bias_value,
        grad_bias_in,
    ) = vec_outs
    return (
        layer_out,
        grad_tokens,
        grad_w_qkv,
        grad_bias_query,
        grad_bias_value,
        grad_w_out,
        grad_bias_out,
        grad_gain_attn,
        grad_shift_attn,
        grad_w_in,
        grad_bias_in,
        grad_w_back,
        grad_bias_back,
        grad_gain_ffn,
        grad_shift_ffn,
    )


def solution(mesh):
    in_specs = (
        P("dp", "tp", None),
        P(),
        P(),
        P(),
        P(),
        P(),
        P(),
        P(),
        P(None, "tp"),
        P("tp"),
        P("tp", None),
        P(),
        P(),
        P(),
        P("dp", None, None, None),
        P("dp", "tp", None),
    )
    out_specs = (
        P("dp", "tp", None),
        P("dp", "tp", None),
        P(),
        P(),
        P(),
        P(),
        P(),
        P(),
        P(),
        P(None, "tp"),
        P("tp"),
        P("tp", None),
        P(),
        P(),
        P(),
    )
    return jax.shard_map(
        per_device, mesh=mesh, in_specs=in_specs, out_specs=out_specs, check_vma=False
    )
```

time: 359 us -> 244 us (0.68)
  starting transfers between devices: 116 us -> 73.3 us
  waiting for transfers between devices: 127 us -> 92 us
  Pallas kernels: 77.9 us -> 63.1 us
  other arithmetic: 13.5 us -> 0 us
  local copies, waits for them, and re-layouts: 22 us -> 10.5 us
    ppermute x58 -> x53, starting transfers between devices: 93.4 us -> 51.8 us  [hop(): return lax.ppermute(array, ('dp', 'tp'), pairs)]
    ppermute x58 -> x53, waiting for transfers between devices: 107 us -> 83.7 us  [hop(): return lax.ppermute(array, ('dp', 'tp'), pairs)]
    pallas_call x9 -> x37, Pallas kernels: 77.9 us -> 63.1 us  [call(): return lambda *arrays: run(*arrays, *deps)]
    ppermute x5 -> x4, waiting for transfers between devices: 19.8 us -> 8.32 us  [place(): return lax.ppermute(array, ('dp', 'tp'), pairs)]
    convert_element_type x15 -> x0, other arithmetic: 7.37 us -> none  [the longest x12 4.87 us: add_low(): return total(*terms).astype(bf16)]
    another operation x9 -> x1, local copies, waits for them, and re-layouts: 4.82 us -> 0.08 us  [per_device(): info = jnp.stack([quarter, mine, z, here, native]).astype(jnp.int32)]
    another operation x15 -> x0, other arithmetic: 4.68 us -> none
    ppermute x5 -> x4, starting transfers between devices: 22.7 us -> 21.4 us  [place(): return lax.ppermute(array, ('dp', 'tp'), pairs)]
  transfers between devices with their start and end apart: 63 -> 57, of which waited for: 28 -> 23; matrix products, arithmetic and copies ran while one was open for 8% -> 1% of each run, Pallas kernels for 14% -> 17%
where the time goes in v2:
time: 244 us; the launch traced here: 240 us
  waiting for transfers between devices  92 us (38%)
  starting transfers between devices  73.3 us (30%)
  Pallas kernels  63.1 us (26%)
  local copies, waits for them, and re-layouts  10.5 us (4%)
    ppermute x53, waiting for transfers between devices, hop(): return lax.ppermute(array, ('dp', 'tp'), pairs)  83.7 us
    pallas_call x37, Pallas kernels, call(): return lambda *arrays: run(*arrays, *deps)  63.1 us
    ppermute x53, starting transfers between devices, hop(): return lax.ppermute(array, ('dp', 'tp'), pairs)  51.8 us
    ppermute x4, starting transfers between devices, place(): return lax.ppermute(array, ('dp', 'tp'), pairs)  21.4 us
    unnamed x51, local copies, waits for them, and re-layouts  9.29 us
    ppermute x4, waiting for transfers between devices, place(): return lax.ppermute(array, ('dp', 'tp'), pairs)  8.32 us
  transfers between devices with their start and end apart: 57, of which 23 were waited for; matrix products, arithmetic and copies ran while one was open for 1% of the time, Pallas kernels for 17%

profile of v2, /device:TPU:1, one launch (start us, length us, event | category | flops | bytes accessed | tf_op | source)
XLA Modules:
  0.0 240.5 jit_solution(10007166429092994285)
XLA Ops:
  0.7 5.7 %collective-permute-start = (bf16[256,768]{1,0:T(8,128)(2,1)}, bf16[256,768]{1,0:T(8,128)(2,1)S(1)}, u32[]{:S(2)}, u32[]{:S(2)}) collective-permute-start(bf16[256,768]{1,0:T(8,128)(2,1)} %bitcast.19), channel_id=1, source_target_pairs={{0,0},{1,1},{2,4},{3,5},{4,2},{5,3},{6,6},{7,7},{8,8},{9,9},{10,12... | collective-permute-start | bytes 1179656 | tf_op jit(solution)/shard_map/ppermute | solution.py:67
  10.9 1.4 collective-permute-start.5
  12.3 2.0 copy-done.4
  15.2 12.1 %collective-permute-done.6.refs_1_ = bf16[208,768]{1,0:T(8,128)(2,1)S(1)} collective-permute-done((bf16[208,768]{1,0:T(8,128)(2,1)S(1)}, bf16[208,768]{1,0:T(8,128)(2,1)S(1)}, u32[]{:S(2)}, u32[]{:S(2)}) %collective-permute-start.6) | collective-permute-done | bytes 319520 | tf_op jit(solution)/shard_map/ppermute | solution.py:56
  27.4 1.3 collective-permute-start.7
  29.9 3.1 %collective-permute-start.2 = (bf16[256,768]{1,0:T(8,128)(2,1)S(1)}, bf16[256,768]{1,0:T(8,128)(2,1)S(1)}, u32[]{:S(2)}, u32[]{:S(2)}) collective-permute-start(bf16[256,768]{1,0:T(8,128)(2,1)S(1)} %collective-permute-done.refs_2_.refs_3_.refs_0_.refs_1_), channel_id=1, source_target_pairs={{0,1},{1,0},{2,3},{3,2},{4,5},{5,4},{6,7},{7,6},{8,9},{9,8},{10,11... | collective-permute-start | bytes 1179656 | tf_op jit(solution)/shard_map/ppermute | solution.py:56
  33.0 14.5 %collective-permute-done.9.refs_2_.refs_3_ = bf16[208,768]{1,0:T(8,128)(2,1)S(1)} collective-permute-done((bf16[208,768]{1,0:T(8,128)(2,1)S(1)}, bf16[208,768]{1,0:T(8,128)(2,1)S(1)}, u32[]{:S(2)}, u32[]{:S(2)}) %collective-permute-start.9) | collective-permute-done | bytes 319520 | tf_op jit(solution)/shard_map/ppermute | solution.py:56
  49.3 2.9 %collective-permute-start.3 = (bf16[256,768]{1,0:T(8,128)(2,1)S(1)}, bf16[256,768]{1,0:T(8,128)(2,1)S(1)}, u32[]{:S(2)}, u32[]{:S(2)}) collective-permute-start(bf16[256,768]{1,0:T(8,128)(2,1)S(1)} %collective-permute-done.refs_2_.refs_3_.refs_0_.refs_1_), channel_id=1, source_target_pairs={{0,4},{1,5},{2,6},{3,7},{4,0},{5,1},{6,2},{7,3},{8,12},{9,13},{10,... | collective-permute-start | bytes 1179656 | tf_op jit(solution)/shard_map/ppermute | solution.py:56
  55.5 3.6 %collective-permute-start.13 = (bf16[256,768]{1,0:T(8,128)(2,1)}, bf16[256,768]{1,0:T(8,128)(2,1)S(1)}, u32[]{:S(2)}, u32[]{:S(2)}) collective-permute-start(bf16[256,768]{1,0:T(8,128)(2,1)} %bitcast.20), channel_id=1, source_target_pairs={{0,0},{1,1},{2,4},{3,5},{4,2},{5,3},{6,6},{7,7},{8,8},{9,9},{10,12... | collective-permute-start | bytes 1179656 | tf_op jit(solution)/shard_map/ppermute | solution.py:67
  59.2 10.7 %attention.1 = (bf16[384,128]{1,0:T(8,128)(2,1)S(1)}, bf16[768,128]{1,0:T(8,128)(2,1)S(1)}, bf16[384,128]{1,0:T(8,128)(2,1)S(1)}, bf16[1024,64]{1,0:T(8,128)(2,1...) custom-call(s32[5]{0:T(128)S(1)} %stack.27.refs_0_, ...), custom_call_target="tpu_custom_call" | custom-call | flops 1 | bytes 1 | tf_op jit(solution)/shard_map/attention/pallas_call | solution.py:623
  70.0 1.3 collective-permute-done.11.refs_6_.refs_4_
  71.3 1.3 held.1.refs_5_.refs_1_
  74.1 1.3 collective-permute-start.18
  76.6 2.4 collective-permute-done.10.refs_4_.refs_3_
  79.0 1.5 flip_tokens.1.refs_2_.refs_20_.refs_1_
  84.2 6.4 %ffn.1 = (bf16[256,768]{1,0:T(8,128)(2,1)S(1)}, f32[256,768]{1,0:T(8,128)S(1)}, f32[256,768]{1,0:T(8,128)S(1)}, bf16[256,768]{1,0:T(8,128)(2,1)S(1)}, bf16[256,7...) custom-call(s32[5]{0:T(128)S(1)} %stack.27.refs_0_, ...), custom_call_target="tpu_custom_call" | custom-call | flops 1 | bytes 1 | tf_op jit(solution)/shard_map/ffn/pallas_call | solution.py:623
  90.7 2.1 back_grads.1
  93.2 5.7 %ffn_back.1 = (bf16[384,128]{1,0:T(8,128)(2,1)S(1)}, bf16[768,128]{1,0:T(8,128)(2,1)S(1)}, bf16[384,128]{1,0:T(8,128)(2,1)S(1)}, f32[256,768]{1,0:T(8,128)S(1)},...) custom-call(s32[5]{0:T(128)S(1)} %stack.27.refs_0_, ...), custom_call_target="tpu_custom_call" | custom-call | flops 1 | bytes 1 | tf_op jit(solution)/shard_map/ffn_back/pallas_call | solution.py:623
  99.8 1.3 collective-permute-start.27
  102.9 1.5 collective-permute-done.24.refs_1_
  104.7 1.3 collective-permute-start.29
  106.0 2.0 collective-permute-done.21.refs_8_
  108.1 2.8 %collective-permute-start.22 = (bf16[384,128]{1,0:T(8,128)(2,1)S(1)}, bf16[384,128]{1,0:T(8,128)(2,1)S(1)}, u32[]{:S(2)}, u32[]{:S(2)}) collective-permute-start(bf16[384,128]{1,0:T(8,128)(2,1)S(1)} %get-tuple-element.130), channel_id=1, source_target_pairs={{0,4},{1,5},{2,6},{3,7},{4,0},{5,1},{6,2},{7,3},{8,12},{9,13},{10,... | collective-permute-start | bytes 294920 | tf_op jit(solution)/shard_map/ppermute | solution.py:56
  113.1 4.7 %attention_back_0.1 = (bf16[1024,192]{1,0:T(8,128)(2,1)S(1)}, f32[8,192]{1,0:T(8,128)S(1)}) custom-call(s32[5]{0:T(128)S(1)} %stack.27.refs_0_, s32[576]{0:T(1024)S(1)} %reshape.36.refs_1_, s32[576]{0:T(1024)S(1)} %collective-permute-done.1.refs_2_, bf16[1024,64]{1,0:T(8,128)(2,1)S(1)} %get-tuple-element.115.refs_3_, ...), custom_call_target="tpu_custom_call" | custom-call | flops 1 | bytes 1 | tf_op jit(solution)/shard_map/attention_back_0/pallas_call | solution.py:623
  118.2 5.3 %collective-permute-start.20 = (bf16[256,768]{1,0:T(8,128)(2,1)S(1)}, bf16[256,768]{1,0:T(8,128)(2,1)S(1)}, u32[]{:S(2)}, u32[]{:S(2)}) collective-permute-start(bf16[256,768]{1,0:T(8,128)(2,1)S(1)} %get-tuple-element.114), channel_id=1, source_target_pairs={{0,0},{1,1},{2,4},{3,5},{4,2},{5,3},{6,6},{7,7},{8,8},{9,9},{10,12... | collective-permute-start | bytes 1179656 | tf_op jit(solution)/shard_map/ppermute | solution.py:67
  123.6 4.5 %attention_back_1.1 = (bf16[1024,192]{1,0:T(8,128)(2,1)S(1)}, f32[8,192]{1,0:T(8,128)S(1)}) custom-call(s32[5]{0:T(128)S(1)} %stack.27.refs_0_, s32[576]{0:T(1024)S(1)} %reshape.36.refs_1_, s32[576]{0:T(1024)S(1)} %collective-permute-done.1.refs_2_, bf16[1024,64]{1,0:T(8,128)(2,1)S(1)} %get-tuple-element.137.refs_3_, ...), custom_call_target="tpu_custom_call" | custom-call | flops 1 | bytes 1 | tf_op jit(solution)/shard_map/attention_back_1/pallas_call | solution.py:623
  128.1 4.5 %attention_back_2.1 = (bf16[1024,192]{1,0:T(8,128)(2,1)S(1)}, f32[8,192]{1,0:T(8,128)S(1)}) custom-call(s32[5]{0:T(128)S(1)} %stack.27.refs_0_, s32[576]{0:T(1024)S(1)} %reshape.36.refs_1_, s32[576]{0:T(1024)S(1)} %collective-permute-done.1.refs_2_, bf16[1024,64]{1,0:T(8,128)(2,1)S(1)} %get-tuple-element.146.refs_3_, ...), custom_call_target="tpu_custom_call" | custom-call | flops 1 | bytes 1 | tf_op jit(solution)/shard_map/attention_back_2/pallas_call | solution.py:623
  133.2 2.1 qkv_grads.1
  135.4 1.5 token_grad.1
  140.1 1.5 collective-permute-start.33
  142.7 16.7 %collective-permute-done.35.refs_3_.refs_4_ = bf16[384,384]{1,0:T(8,128)(2,1)S(1)} collective-permute-done((bf16[384,384]{1,0:T(8,128)(2,1)S(1)}, bf16[384,384]{1,0:T(8,128)(2,1)S(1)}, u32[]{:S(2)}, u32[]{:S(2)}) %collective-permute-start.35) | collective-permute-done | bytes 294944 | tf_op jit(solution)/shard_map/ppermute | solution.py:56
  160.1 1.7 collective-permute-start.42
  161.8 1.5 collective-permute-start.36
  163.6 3.9 %collective-permute-done.37.refs_5_ = bf16[192,384]{1,0:T(8,128)(2,1)S(1)} collective-permute-done((bf16[192,384]{1,0:T(8,128)(2,1)S(1)}, bf16[192,384]{1,0:T(8,128)(2,1)S(1)}, u32[]{:S(2)}, u32[]{:S(2)}) %collective-permute-start.37) | collective-permute-done | bytes 147488 | tf_op jit(solution)/shard_map/ppermute | solution.py:56
  169.2 11.1 %collective-permute-done.42.refs_1_ = bf16[2,2,96,768]{3,2,1,0:T(8,128)(2,1)S(1)} collective-permute-done((bf16[2,2,96,768]{3,2,1,0:T(8,128)(2,1)S(1)}, bf16[2,2,96,768]{3,2,1,0:T(8,128)(2,1)S(1)}, u32[]{:S(2)}, u32[]{:S(2)}) %collective-permute-start.42) | collective-permute-done | bytes 589856 | tf_op jit(solution)/shard_map/ppermute | solution.py:56
  180.5 3.0 %collective-permute-start.43 = (bf16[208,768]{1,0:T(8,128)(2,1)S(1)}, bf16[208,768]{1,0:T(8,128)(2,1)S(1)}, u32[]{:S(2)}, u32[]{:S(2)}) collective-permute-start(bf16[208,768]{1,0:T(8,128)(2,1)S(1)} %qkv_four.1.refs_0_), channel_id=1, source_target_pairs={{0,1},{1,0},{2,3},{3,2},{4,5},{5,4},{6,7},{7,6},{8,9},{9,8},{10,11... | collective-permute-start | bytes 958472 | tf_op jit(solution)/shard_map/ppermute | solution.py:56
  184.0 1.4 collective-permute-start.45
  186.3 3.4 %collective-permute-done.44.refs_0_.refs_2_ = bf16[192,768]{1,0:T(8,128)(2,1)S(1)} collective-permute-done((bf16[192,768]{1,0:T(8,128)(2,1)S(1)}, bf16[192,768]{1,0:T(8,128)(2,1)S(1)}, u32[]{:S(2)}, u32[]{:S(2)}) %collective-permute-start.44) | collective-permute-done | bytes 294944 | tf_op jit(solution)/shard_map/ppermute | solution.py:56
  191.1 3.7 %collective-permute-start.47 = (bf16[288,768]{1,0:T(8,128)(2,1)S(1)}, bf16[288,768]{1,0:T(8,128)(2,1)S(1)}, u32[]{:S(2)}, u32[]{:S(2)}) collective-permute-start(bf16[288,768]{1,0:T(8,128)(2,1)S(1)} %get-tuple-element.169), channel_id=1, source_target_pairs={{0,16},{1,17},{2,18},{3,19},{4,20},{5,21},{6,22},{7,23},{8,24},{9,... | collective-permute-start | bytes 1327112 | tf_op jit(solution)/shard_map/ppermute | solution.py:56
  194.8 6.7 %collective-permute-start.38 = (bf16[256,768]{1,0:T(8,128)(2,1)S(1)}, bf16[256,768]{1,0:T(8,128)(2,1)S(1)}, u32[]{:S(2)}, u32[]{:S(2)}) collective-permute-start(bf16[256,768]{1,0:T(8,128)(2,1)S(1)} %tokens.1.refs_3_), channel_id=1, source_target_pairs={{0,0},{1,1},{2,4},{3,5},{4,2},{5,3},{6,6},{7,7},{8,8},{9,9},{10,12... | collective-permute-start | bytes 1179656 | tf_op jit(solution)/shard_map/ppermute | solution.py:67
  203.0 8.2 %collective-permute-done.38 = bf16[256,768]{1,0:T(8,128)(2,1)S(1)} collective-permute-done((bf16[256,768]{1,0:T(8,128)(2,1)S(1)}, bf16[256,768]{1,0:T(8,128)(2,1)S(1)}, u32[]{:S(2)}, u32[]{:S(2)}) %collective-permute-start.38) | collective-permute-done | bytes 393248 | tf_op jit(solution)/shard_map/ppermute | solution.py:67
  214.3 1.4 collective-permute-done.53.refs_3_
  216.5 2.2 collective-permute-done.49.refs_6_
  218.9 2.9 %collective-permute-start.55 = (bf16[1552,768]{1,0:T(8,128)(2,1)S(1)}, bf16[1552,768]{1,0:T(8,128)(2,1)S(1)}, u32[]{:S(2)}, u32[]{:S(2)}) collective-permute-start(bf16[1552,768]{1,0:T(8,128)(2,1)S(1)} %join_l.1.refs_1_), channel_id=1, source_target_pairs={{0,4},{1,5},{2,6},{3,7},{4,0},{5,1},{6,2},{7,3},{8,12},{9,13},{10,... | collective-permute-start | bytes 7151624 | tf_op jit(solution)/shard_map/ppermute | solution.py:56
  221.9 5.8 %collective-permute-done.56.refs_2_ = bf16[4,2,96,768]{3,2,1,0:T(8,128)(2,1)S(1)} collective-permute-done((bf16[4,2,96,768]{3,2,1,0:T(8,128)(2,1)S(1)}, bf16[4,2,96,768]{3,2,1,0:T(8,128)(2,1)S(1)}, u32[]{:S(2)}, u32[]{:S(2)}) %collective-permute-start.56) | collective-permute-done | bytes 1179680 | tf_op jit(solution)/shard_map/ppermute | solution.py:56
  227.7 3.6 %ffn_out.1 = (f32[768,768]{1,0:T(8,128)}, f32[768,768]{1,0:T(8,128)}) custom-call(s32[5]{0:T(128)S(1)} %stack.27.refs_0_, bf16[4,2,96,768]{3,2,1,0:T(8,128)(2,1)S(1)} %bitcast.14, bf16[4,2,96,768]{3,2,1,0:T(8,128)(2,1)S(1)} %collective-permute-done.56.refs_2_), custom_call_target="tpu_custom_call" | custom-call | flops 1 | bytes 1 | tf_op jit(solution)/shard_map/ffn_out/pallas_call | solution.py:623
  231.3 1.7 copy-done.9
  233.0 5.7 %qkv_out.1 = (f32[768,2304]{1,0:T(8,128)}, f32[768,768]{1,0:T(8,128)}, f32[768]{0:T(1024)}, f32[768]{0:T(1024)}, f32[768]{0:T(1024)}, /*index=5*/f32[768]{0:T(10...) custom-call(s32[5]{0:T(128)S(1)} %stack.27.refs_0_, ...), custom_call_target="tpu_custom_call" | custom-call | flops 1 | bytes 1 | tf_op jit(solution)/shard_map/qkv_out/pallas_call | solution.py:623
  (159 shorter events, 41.9 us)
Async XLA Ops:
  0.7 26.7 %collective-permute-start = (bf16[256,768]{1,0:T(8,128)(2,1)}, bf16[256,768]{1,0:T(8,128)(2,1)S(1)}, u32[]{:S(2)}, u32[]{:S(2)}) collective-permute-start(bf16[256,768]{1,0:T(8,128)(2,1)} %bitcast.19), channel_id=1, source_target_pairs={{0,0},{1,1},{2,4},{3,5},{4,2},{5,3},{6,6},{7,7},{8,8},{9,9},{10,12... | collective-permute-start | bytes 1179656 | tf_op jit(solution)/shard_map/ppermute | solution.py:67
  10.9 16.5 %collective-permute-start.6 = (bf16[208,768]{1,0:T(8,128)(2,1)S(1)}, bf16[208,768]{1,0:T(8,128)(2,1)S(1)}, u32[]{:S(2)}, u32[]{:S(2)}) collective-permute-start(bf16[208,768]{1,0:T(8,128)(2,1)S(1)} %piece.1), channel_id=1, source_target_pairs={{0,2},{1,3},{2,0},{3,1},{4,6},{5,7},{6,4},{7,5},{8,10},{9,11},{10,... | collective-permute-start | bytes 958472 | tf_op jit(solution)/shard_map/ppermute | solution.py:56
  10.9 16.4 %collective-permute-start.5 = (bf16[208,768]{1,0:T(8,128)(2,1)S(1)}, bf16[208,768]{1,0:T(8,128)(2,1)S(1)}, u32[]{:S(2)}, u32[]{:S(2)}) collective-permute-start(bf16[208,768]{1,0:T(8,128)(2,1)S(1)} %piece.1), channel_id=1, source_target_pairs={{0,1},{1,0},{2,3},{3,2},{4,5},{5,4},{6,7},{7,6},{8,9},{9,8},{10,11... | collective-permute-start | bytes 958472 | tf_op jit(solution)/shard_map/ppermute | solution.py:56
  27.4 20.2 %collective-permute-start.7 = (bf16[416,768]{1,0:T(8,128)(2,1)S(1)}, bf16[416,768]{1,0:T(8,128)(2,1)S(1)}, u32[]{:S(2)}, u32[]{:S(2)}) collective-permute-start(bf16[416,768]{1,0:T(8,128)(2,1)S(1)} %pair.1.refs_0_), channel_id=1, source_target_pairs={{0,8},{1,9},{2,10},{3,11},{4,12},{5,13},{6,14},{7,15},{8,0},{9,1},... | collective-permute-start | bytes 1916936 | tf_op jit(solution)/shard_map/ppermute | solution.py:56
  28.7 18.9 %collective-permute-start.8 = (bf16[416,768]{1,0:T(8,128)(2,1)S(1)}, bf16[416,768]{1,0:T(8,128)(2,1)S(1)}, u32[]{:S(2)}, u32[]{:S(2)}) collective-permute-start(bf16[416,768]{1,0:T(8,128)(2,1)S(1)} %pair.1.refs_0_), channel_id=1, source_target_pairs={{0,16},{1,17},{2,18},{3,19},{4,20},{5,21},{6,22},{7,23},{8,24},{9,... | collective-permute-start | bytes 1916936 | tf_op jit(solution)/shard_map/ppermute | solution.py:56
  29.9 17.7 %collective-permute-start.2 = (bf16[256,768]{1,0:T(8,128)(2,1)S(1)}, bf16[256,768]{1,0:T(8,128)(2,1)S(1)}, u32[]{:S(2)}, u32[]{:S(2)}) collective-permute-start(bf16[256,768]{1,0:T(8,128)(2,1)S(1)} %collective-permute-done.refs_2_.refs_3_.refs_0_.refs_1_), channel_id=1, source_target_pairs={{0,1},{1,0},{2,3},{3,2},{4,5},{5,4},{6,7},{7,6},{8,9},{9,8},{10,11... | collective-permute-start | bytes 1179656 | tf_op jit(solution)/shard_map/ppermute | solution.py:56
  33.0 14.6 %collective-permute-start.9 = (bf16[208,768]{1,0:T(8,128)(2,1)S(1)}, bf16[208,768]{1,0:T(8,128)(2,1)S(1)}, u32[]{:S(2)}, u32[]{:S(2)}) collective-permute-start(bf16[208,768]{1,0:T(8,128)(2,1)S(1)} %collective-permute-done.6.refs_1_), channel_id=1, source_target_pairs={{0,1},{1,0},{2,3},{3,2},{4,5},{5,4},{6,7},{7,6},{8,9},{9,8},{10,11... | collective-permute-start | bytes 958472 | tf_op jit(solution)/shard_map/ppermute | solution.py:56
  48.8 22.5 %collective-permute-start.14 = (bf16[432,768]{1,0:T(8,128)(2,1)}, bf16[432,768]{1,0:T(8,128)(2,1)S(1)}, u32[]{:S(2)}, u32[]{:S(2)}) collective-permute-start(bf16[432,768]{1,0:T(8,128)(2,1)} %get-tuple-element.103.refs_9_), channel_id=1, source_target_pairs={{0,8},{1,9},{2,10},{3,11},{4,12},{5,13},{6,14},{7,15},{8,0},{9,1},... | collective-permute-start | bytes 1990664 | tf_op jit(solution)/shard_map/ppermute | solution.py:56
  49.1 22.2 %collective-permute-start.15 = (bf16[400,768]{1,0:T(8,128)(2,1)}, bf16[400,768]{1,0:T(8,128)(2,1)}, u32[]{:S(2)}, u32[]{:S(2)}) collective-permute-start(bf16[400,768]{1,0:T(8,128)(2,1)} %get-tuple-element.107), channel_id=1, source_target_pairs={{0,16},{1,17},{2,18},{3,19},{4,20},{5,21},{6,22},{7,23},{8,24},{9,... | collective-permute-start | bytes 1843208 | tf_op jit(solution)/shard_map/ppermute | solution.py:56
  49.3 9.9 %collective-permute-start.3 = (bf16[256,768]{1,0:T(8,128)(2,1)S(1)}, bf16[256,768]{1,0:T(8,128)(2,1)S(1)}, u32[]{:S(2)}, u32[]{:S(2)}) collective-permute-start(bf16[256,768]{1,0:T(8,128)(2,1)S(1)} %collective-permute-done.refs_2_.refs_3_.refs_0_.refs_1_), channel_id=1, source_target_pairs={{0,4},{1,5},{2,6},{3,7},{4,0},{5,1},{6,2},{7,3},{8,12},{9,13},{10,... | collective-permute-start | bytes 1179656 | tf_op jit(solution)/shard_map/ppermute | solution.py:56
  52.2 7.0 %collective-permute-start.4 = (bf16[256,768]{1,0:T(8,128)(2,1)S(1)}, bf16[256,768]{1,0:T(8,128)(2,1)}, u32[]{:S(2)}, u32[]{:S(2)}) collective-permute-start(bf16[256,768]{1,0:T(8,128)(2,1)S(1)} %collective-permute-done.2.refs_3_.refs_4_.refs_1_), channel_id=1, source_target_pairs={{0,4},{1,5},{2,6},{3,7},{4,0},{5,1},{6,2},{7,3},{8,12},{9,13},{10,... | collective-permute-start | bytes 1179656 | tf_op jit(solution)/shard_map/ppermute | solution.py:56
  55.5 14.5 %collective-permute-start.13 = (bf16[256,768]{1,0:T(8,128)(2,1)}, bf16[256,768]{1,0:T(8,128)(2,1)S(1)}, u32[]{:S(2)}, u32[]{:S(2)}) collective-permute-start(bf16[256,768]{1,0:T(8,128)(2,1)} %bitcast.20), channel_id=1, source_target_pairs={{0,0},{1,1},{2,4},{3,5},{4,2},{5,3},{6,6},{7,7},{8,8},{9,9},{10,12... | collective-permute-start | bytes 1179656 | tf_op jit(solution)/shard_map/ppermute | solution.py:67
  72.6 10.4 %collective-permute-start.16 = (bf16[2288,768]{1,0:T(8,128)(2,1)S(1)}, bf16[2288,768]{1,0:T(8,128)(2,1)S(1)}, u32[]{:S(2)}, u32[]{:S(2)}) collective-permute-start(bf16[2288,768]{1,0:T(8,128)(2,1)S(1)} %held.1.refs_5_.refs_1_), channel_id=1, source_target_pairs={{0,4},{1,5},{2,6},{3,7},{4,0},{5,1},{6,2},{7,3},{8,12},{9,13},{10,... | collective-permute-start | bytes 10543112 | tf_op jit(solution)/shard_map/ppermute | solution.py:56
  72.9 6.1 %collective-permute-start.10 = (bf16[768,128]{1,0:T(8,128)(2,1)S(1)}, bf16[768,128]{1,0:T(8,128)(2,1)S(1)}, u32[]{:S(2)}, u32[]{:S(2)}) collective-permute-start(bf16[768,128]{1,0:T(8,128)(2,1)S(1)} %get-tuple-element.105), channel_id=1, source_target_pairs={{0,1},{1,0},{2,3},{3,2},{4,5},{5,4},{6,7},{7,6},{8,9},{9,8},{10,11... | collective-permute-start | bytes 589832 | tf_op jit(solution)/shard_map/ppermute | solution.py:56
  74.1 6.4 %collective-permute-start.18 = (bf16[112,768]{1,0:T(8,128)(2,1)S(1)}, bf16[112,768]{1,0:T(8,128)(2,1)S(1)}, u32[]{:S(2)}, u32[]{:S(2)}) collective-permute-start(bf16[112,768]{1,0:T(8,128)(2,1)S(1)} %get-tuple-element.109), channel_id=1, source_target_pairs={{0,8},{1,9},{2,10},{3,11},{4,12},{5,13},{6,14},{7,15},{8,0},{9,1},... | collective-permute-start | bytes 516104 | tf_op jit(solution)/shard_map/ppermute | solution.py:56
  75.4 5.1 %collective-permute-start.17 = (bf16[96,768]{1,0:T(8,128)(2,1)S(1)}, bf16[96,768]{1,0:T(8,128)(2,1)S(1)}, u32[]{:S(2)}, u32[]{:S(2)}) collective-permute-start(bf16[96,768]{1,0:T(8,128)(2,1)S(1)} %get-tuple-element.108), channel_id=1, source_target_pairs={{0,16},{1,17},{2,18},{3,19},{4,20},{5,21},{6,22},{7,23},{8,24},{9,... | collective-permute-start | bytes 442376 | tf_op jit(solution)/shard_map/ppermute | solution.py:56
  92.8 6.8 %collective-permute-start.25 = (bf16[2,4,2,96,768]{4,3,2,1,0:T(8,128)(2,1)S(1)}, bf16[2,4,2,96,768]{4,3,2,1,0:T(8,128)(2,1)S(1)}, u32[]{:S(2)}, u32[]{:S(2)}) collective-permute-start(bf16[2,4,2,96,768]{4,3,2,1,0:T(8,128)(2,1)S(1)} %get-tuple-element.134), channel_id=1, source_target_pairs={{0,4},{1,5},{2,6},{3,7},{4,0},{5,1},{6,2},{7,3},{8,12},{9,13},{10,... | collective-permute-start | bytes 7077896 | tf_op jit(solution)/shard_map/ppermute | solution.py:56
  98.9 18.8 %collective-permute-start.26 = (bf16[2,4,2,96,768]{4,3,2,1,0:T(8,128)(2,1)S(1)}, bf16[2,4,2,96,768]{4,3,2,1,0:T(8,128)(2,1)S(1)}, u32[]{:S(2)}, u32[]{:S(2)}) collective-permute-start(bf16[2,4,2,96,768]{4,3,2,1,0:T(8,128)(2,1)S(1)} %get-tuple-element.141), channel_id=1, source_target_pairs={{0,4},{1,5},{2,6},{3,7},{4,0},{5,1},{6,2},{7,3},{8,12},{9,13},{10,... | collective-permute-start | bytes 7077896 | tf_op jit(solution)/shard_map/ppermute | solution.py:56
  99.1 5.2 %collective-permute-start.24 = (bf16[768,384]{1,0:T(8,128)(2,1)S(1)}, bf16[768,384]{1,0:T(8,128)(2,1)S(1)}, u32[]{:S(2)}, u32[]{:S(2)}) collective-permute-start(bf16[768,384]{1,0:T(8,128)(2,1)S(1)} %get-tuple-element.132), channel_id=1, source_target_pairs={{0,4},{1,5},{2,6},{3,7},{4,0},{5,1},{6,2},{7,3},{8,12},{9,13},{10,... | collective-permute-start | bytes 1769480 | tf_op jit(solution)/shard_map/ppermute | solution.py:56
  99.8 18.0 %collective-permute-start.27 = (bf16[2,2,96,768]{3,2,1,0:T(8,128)(2,1)S(1)}, bf16[2,2,96,768]{3,2,1,0:T(8,128)(2,1)S(1)}, u32[]{:S(2)}, u32[]{:S(2)}) collective-permute-start(bf16[2,2,96,768]{3,2,1,0:T(8,128)(2,1)S(1)} %get-tuple-element.135.refs_12_), channel_id=1, source_target_pairs={{0,8},{1,9},{2,10},{3,11},{4,12},{5,13},{6,14},{7,15},{8,0},{9,1},... | collective-permute-start | bytes 1769480 | tf_op jit(solution)/shard_map/ppermute | solution.py:56
  101.1 16.7 %collective-permute-start.28 = (bf16[2,2,96,768]{3,2,1,0:T(8,128)(2,1)S(1)}, bf16[2,2,96,768]{3,2,1,0:T(8,128)(2,1)S(1)}, u32[]{:S(2)}, u32[]{:S(2)}) collective-permute-start(bf16[2,2,96,768]{3,2,1,0:T(8,128)(2,1)S(1)} %get-tuple-element.142), channel_id=1, source_target_pairs={{0,16},{1,17},{2,18},{3,19},{4,20},{5,21},{6,22},{7,23},{8,24},{9,... | collective-permute-start | bytes 1769480 | tf_op jit(solution)/shard_map/ppermute | solution.py:56
  102.3 5.7 %collective-permute-start.21 = (bf16[768,128]{1,0:T(8,128)(2,1)S(1)}, bf16[768,128]{1,0:T(8,128)(2,1)S(1)}, u32[]{:S(2)}, u32[]{:S(2)}) collective-permute-start(bf16[768,128]{1,0:T(8,128)(2,1)S(1)} %get-tuple-element.129.refs_2_), channel_id=1, source_target_pairs={{0,1},{1,0},{2,3},{3,2},{4,5},{5,4},{6,7},{7,6},{8,9},{9,8},{10,11... | collective-permute-start | bytes 589832 | tf_op jit(solution)/shard_map/ppermute | solution.py:56
  104.7 13.0 %collective-permute-start.29 = (bf16[768,192]{1,0:T(8,128)(2,1)S(1)}, bf16[768,192]{1,0:T(8,128)(2,1)S(1)}, u32[]{:S(2)}, u32[]{:S(2)}) collective-permute-start(bf16[768,192]{1,0:T(8,128)(2,1)S(1)} %get-tuple-element.143), channel_id=1, source_target_pairs={{0,1},{1,0},{2,3},{3,2},{4,5},{5,4},{6,7},{7,6},{8,9},{9,8},{10,11... | collective-permute-start | bytes 884744 | tf_op jit(solution)/shard_map/ppermute | solution.py:56
  118.1 14.6 %collective-permute-start.30 = (bf16[2,2,96,768]{3,2,1,0:T(8,128)(2,1)S(1)}, bf16[2,2,96,768]{3,2,1,0:T(8,128)(2,1)S(1)}, u32[]{:S(2)}, u32[]{:S(2)}) collective-permute-start(bf16[2,2,96,768]{3,2,1,0:T(8,128)(2,1)S(1)} %get-tuple-element.144.refs_11_), channel_id=1, source_target_pairs={{0,8},{1,9},{2,10},{3,11},{4,12},{5,13},{6,14},{7,15},{8,0},{9,1},... | collective-permute-start | bytes 1769480 | tf_op jit(solution)/shard_map/ppermute | solution.py:56
  118.2 14.5 %collective-permute-start.31 = (bf16[2,2,96,768]{3,2,1,0:T(8,128)(2,1)S(1)}, bf16[2,2,96,768]{3,2,1,0:T(8,128)(2,1)S(1)}, u32[]{:S(2)}, u32[]{:S(2)}) collective-permute-start(bf16[2,2,96,768]{3,2,1,0:T(8,128)(2,1)S(1)} %get-tuple-element.154), channel_id=1, source_target_pairs={{0,16},{1,17},{2,18},{3,19},{4,20},{5,21},{6,22},{7,23},{8,24},{9,... | collective-permute-start | bytes 1769480 | tf_op jit(solution)/shard_map/ppermute | solution.py:56
  118.2 15.0 %collective-permute-start.20 = (bf16[256,768]{1,0:T(8,128)(2,1)S(1)}, bf16[256,768]{1,0:T(8,128)(2,1)S(1)}, u32[]{:S(2)}, u32[]{:S(2)}) collective-permute-start(bf16[256,768]{1,0:T(8,128)(2,1)S(1)} %get-tuple-element.114), channel_id=1, source_target_pairs={{0,0},{1,1},{2,4},{3,5},{4,2},{5,3},{6,6},{7,7},{8,8},{9,9},{10,12... | collective-permute-start | bytes 1179656 | tf_op jit(solution)/shard_map/ppermute | solution.py:67
  138.1 21.3 %collective-permute-start.40 = (bf16[2,2,96,768]{3,2,1,0:T(8,128)(2,1)S(1)}, bf16[2,2,96,768]{3,2,1,0:T(8,128)(2,1)S(1)}, u32[]{:S(2)}, u32[]{:S(2)}) collective-permute-start(bf16[2,2,96,768]{3,2,1,0:T(8,128)(2,1)S(1)} %get-tuple-element.155.refs_12_), channel_id=1, source_target_pairs={{0,16},{1,17},{2,18},{3,19},{4,20},{5,21},{6,22},{7,23},{8,24},{9,... | collective-permute-start | bytes 1769480 | tf_op jit(solution)/shard_map/ppermute | solution.py:56
  138.3 21.1 %collective-permute-start.41 = (bf16[2,2,96,768]{3,2,1,0:T(8,128)(2,1)S(1)}, bf16[2,2,96,768]{3,2,1,0:T(8,128)(2,1)S(1)}, u32[]{:S(2)}, u32[]{:S(2)}) collective-permute-start(bf16[2,2,96,768]{3,2,1,0:T(8,128)(2,1)S(1)} %get-tuple-element.165), channel_id=1, source_target_pairs={{0,8},{1,9},{2,10},{3,11},{4,12},{5,13},{6,14},{7,15},{8,0},{9,1},... | collective-permute-start | bytes 1769480 | tf_op jit(solution)/shard_map/ppermute | solution.py:56
  140.1 19.2 %collective-permute-start.33 = (bf16[256,768]{1,0:T(8,128)(2,1)S(1)}, bf16[256,768]{1,0:T(8,128)(2,1)S(1)}, u32[]{:S(2)}, u32[]{:S(2)}) collective-permute-start(bf16[256,768]{1,0:T(8,128)(2,1)S(1)} %near.1), channel_id=1, source_target_pairs={{0,1},{1,0},{2,3},{3,2},{4,5},{5,4},{6,7},{7,6},{8,9},{9,8},{10,11... | collective-permute-start | bytes 1179656 | tf_op jit(solution)/shard_map/ppermute | solution.py:56
  141.6 17.7 %collective-permute-start.34 = (bf16[416,384]{1,0:T(8,128)(2,1)S(1)}, bf16[416,384]{1,0:T(8,128)(2,1)S(1)}, u32[]{:S(2)}, u32[]{:S(2)}) collective-permute-start(bf16[416,384]{1,0:T(8,128)(2,1)S(1)} %get-tuple-element.160), channel_id=1, source_target_pairs={{0,8},{1,9},{2,10},{3,11},{4,12},{5,13},{6,14},{7,15},{8,0},{9,1},... | collective-permute-start | bytes 958472 | tf_op jit(solution)/shard_map/ppermute | solution.py:56
  142.0 17.3 %collective-permute-start.35 = (bf16[384,384]{1,0:T(8,128)(2,1)S(1)}, bf16[384,384]{1,0:T(8,128)(2,1)S(1)}, u32[]{:S(2)}, u32[]{:S(2)}) collective-permute-start(bf16[384,384]{1,0:T(8,128)(2,1)S(1)} %get-tuple-element.162), channel_id=1, source_target_pairs={{0,16},{1,17},{2,18},{3,19},{4,20},{5,21},{6,22},{7,23},{8,24},{9,... | collective-permute-start | bytes 884744 | tf_op jit(solution)/shard_map/ppermute | solution.py:56
  160.1 20.3 %collective-permute-start.42 = (bf16[2,2,96,768]{3,2,1,0:T(8,128)(2,1)S(1)}, bf16[2,2,96,768]{3,2,1,0:T(8,128)(2,1)S(1)}, u32[]{:S(2)}, u32[]{:S(2)}) collective-permute-start(bf16[2,2,96,768]{3,2,1,0:T(8,128)(2,1)S(1)} %get-tuple-element.167), channel_id=1, source_target_pairs={{0,1},{1,0},{2,3},{3,2},{4,5},{5,4},{6,7},{7,6},{8,9},{9,8},{10,11... | collective-permute-start | bytes 1769480 | tf_op jit(solution)/shard_map/ppermute | solution.py:56
  161.8 5.8 %collective-permute-start.36 = (bf16[224,384]{1,0:T(8,128)(2,1)S(1)}, bf16[224,384]{1,0:T(8,128)(2,1)S(1)}, u32[]{:S(2)}, u32[]{:S(2)}) collective-permute-start(bf16[224,384]{1,0:T(8,128)(2,1)S(1)} %get-tuple-element.163.refs_10_), channel_id=1, source_target_pairs={{0,16},{1,17},{2,18},{3,19},{4,20},{5,21},{6,22},{7,23},{8,24},{9,... | collective-permute-start | bytes 516104 | tf_op jit(solution)/shard_map/ppermute | solution.py:56
  167.7 12.8 %collective-permute-start.39 = (bf16[208,768]{1,0:T(8,128)(2,1)S(1)}, bf16[208,768]{1,0:T(8,128)(2,1)S(1)}, u32[]{:S(2)}, u32[]{:S(2)}) collective-permute-start(bf16[208,768]{1,0:T(8,128)(2,1)S(1)} %qkv_three.1.refs_4_.refs_2_.refs_0_), channel_id=1, source_target_pairs={{0,2},{1,3},{2,0},{3,1},{4,6},{5,7},{6,4},{7,5},{8,10},{9,11},{10,... | collective-permute-start | bytes 958472 | tf_op jit(solution)/shard_map/ppermute | solution.py:56
  180.5 9.3 %collective-permute-start.43 = (bf16[208,768]{1,0:T(8,128)(2,1)S(1)}, bf16[208,768]{1,0:T(8,128)(2,1)S(1)}, u32[]{:S(2)}, u32[]{:S(2)}) collective-permute-start(bf16[208,768]{1,0:T(8,128)(2,1)S(1)} %qkv_four.1.refs_0_), channel_id=1, source_target_pairs={{0,1},{1,0},{2,3},{3,2},{4,5},{5,4},{6,7},{7,6},{8,9},{9,8},{10,11... | collective-permute-start | bytes 958472 | tf_op jit(solution)/shard_map/ppermute | solution.py:56
  183.5 6.1 %collective-permute-start.44 = (bf16[192,768]{1,0:T(8,128)(2,1)S(1)}, bf16[192,768]{1,0:T(8,128)(2,1)S(1)}, u32[]{:S(2)}, u32[]{:S(2)}) collective-permute-start(bf16[192,768]{1,0:T(8,128)(2,1)S(1)} %slice.14), channel_id=1, source_target_pairs={{0,8},{1,9},{2,10},{3,11},{4,12},{5,13},{6,14},{7,15},{8,0},{9,1},... | collective-permute-start | bytes 884744 | tf_op jit(solution)/shard_map/ppermute | solution.py:56
  184.0 5.9 %collective-permute-start.45 = (bf16[192,768]{1,0:T(8,128)(2,1)S(1)}, bf16[192,768]{1,0:T(8,128)(2,1)S(1)}, u32[]{:S(2)}, u32[]{:S(2)}) collective-permute-start(bf16[192,768]{1,0:T(8,128)(2,1)S(1)} %slice.14), channel_id=1, source_target_pairs={{0,16},{1,17},{2,18},{3,19},{4,20},{5,21},{6,22},{7,23},{8,24},{9,... | collective-permute-start | bytes 884744 | tf_op jit(solution)/shard_map/ppermute | solution.py:56
  185.4 16.1 %collective-permute-start.48 = (bf16[2,96,768]{2,1,0:T(8,128)(2,1)S(1)}, bf16[2,96,768]{2,1,0:T(8,128)(2,1)S(1)}, u32[]{:S(2)}, u32[]{:S(2)}) collective-permute-start(bf16[2,96,768]{2,1,0:T(8,128)(2,1)S(1)} %far.1.refs_2_), channel_id=1, source_target_pairs={{0,2},{1,3},{2,0},{3,1},{4,6},{5,7},{6,4},{7,5},{8,10},{9,11},{10,... | collective-permute-start | bytes 884744 | tf_op jit(solution)/shard_map/ppermute | solution.py:56
  189.9 21.3 %collective-permute-start.46 = (bf16[288,768]{1,0:T(8,128)(2,1)S(1)}, bf16[288,768]{1,0:T(8,128)(2,1)S(1)}, u32[]{:S(2)}, u32[]{:S(2)}) collective-permute-start(bf16[288,768]{1,0:T(8,128)(2,1)S(1)} %get-tuple-element.168.refs_3_), channel_id=1, source_target_pairs={{0,8},{1,9},{2,10},{3,11},{4,12},{5,13},{6,14},{7,15},{8,0},{9,1},... | collective-permute-start | bytes 1327112 | tf_op jit(solution)/shard_map/ppermute | solution.py:56
  191.1 20.1 %collective-permute-start.47 = (bf16[288,768]{1,0:T(8,128)(2,1)S(1)}, bf16[288,768]{1,0:T(8,128)(2,1)S(1)}, u32[]{:S(2)}, u32[]{:S(2)}) collective-permute-start(bf16[288,768]{1,0:T(8,128)(2,1)S(1)} %get-tuple-element.169), channel_id=1, source_target_pairs={{0,16},{1,17},{2,18},{3,19},{4,20},{5,21},{6,22},{7,23},{8,24},{9,... | collective-permute-start | bytes 1327112 | tf_op jit(solution)/shard_map/ppermute | solution.py:56
  194.8 16.4 %collective-permute-start.38 = (bf16[256,768]{1,0:T(8,128)(2,1)S(1)}, bf16[256,768]{1,0:T(8,128)(2,1)S(1)}, u32[]{:S(2)}, u32[]{:S(2)}) collective-permute-start(bf16[256,768]{1,0:T(8,128)(2,1)S(1)} %tokens.1.refs_3_), channel_id=1, source_target_pairs={{0,0},{1,1},{2,4},{3,5},{4,2},{5,3},{6,6},{7,7},{8,8},{9,9},{10,12... | collective-permute-start | bytes 1179656 | tf_op jit(solution)/shard_map/ppermute | solution.py:67
  201.6 9.6 %collective-permute-start.51 = (bf16[2,96,768]{2,1,0:T(8,128)(2,1)S(1)}, bf16[2,96,768]{2,1,0:T(8,128)(2,1)S(1)}, u32[]{:S(2)}, u32[]{:S(2)}) collective-permute-start(bf16[2,96,768]{2,1,0:T(8,128)(2,1)S(1)} %last.1.refs_2_.refs_0_), channel_id=1, source_target_pairs={{0,8},{1,9},{2,10},{3,11},{4,12},{5,13},{6,14},{7,15},{8,0},{9,1},... | collective-permute-start | bytes 884744 | tf_op jit(solution)/shard_map/ppermute | solution.py:56
  202.4 8.8 %collective-permute-start.52 = (bf16[2,96,768]{2,1,0:T(8,128)(2,1)S(1)}, bf16[2,96,768]{2,1,0:T(8,128)(2,1)S(1)}, u32[]{:S(2)}, u32[]{:S(2)}) collective-permute-start(bf16[2,96,768]{2,1,0:T(8,128)(2,1)S(1)} %last.1.refs_2_.refs_0_), channel_id=1, source_target_pairs={{0,16},{1,17},{2,18},{3,19},{4,20},{5,21},{6,22},{7,23},{8,24},{9,... | collective-permute-start | bytes 884744 | tf_op jit(solution)/shard_map/ppermute | solution.py:56
  211.3 4.4 %collective-permute-start.53 = (bf16[1,96,768]{2,1,0:T(8,128)(2,1)S(1)}, bf16[1,96,768]{2,1,0:T(8,128)(2,1)S(1)}, u32[]{:S(2)}, u32[]{:S(2)}) collective-permute-start(bf16[1,96,768]{2,1,0:T(8,128)(2,1)S(1)} %get-tuple-element.172), channel_id=1, source_target_pairs={{0,16},{1,17},{2,18},{3,19},{4,20},{5,21},{6,22},{7,23},{8,24},{9,... | collective-permute-start | bytes 442376 | tf_op jit(solution)/shard_map/ppermute | solution.py:56
  212.6 6.2 %collective-permute-start.49 = (bf16[96,768]{1,0:T(8,128)(2,1)S(1)}, bf16[96,768]{1,0:T(8,128)(2,1)S(1)}, u32[]{:S(2)}, u32[]{:S(2)}) collective-permute-start(bf16[96,768]{1,0:T(8,128)(2,1)S(1)} %get-tuple-element.170.refs_2_), channel_id=1, source_target_pairs={{0,8},{1,9},{2,10},{3,11},{4,12},{5,13},{6,14},{7,15},{8,0},{9,1},... | collective-permute-start | bytes 442376 | tf_op jit(solution)/shard_map/ppermute | solution.py:56
  213.6 5.1 %collective-permute-start.50 = (bf16[96,768]{1,0:T(8,128)(2,1)S(1)}, bf16[96,768]{1,0:T(8,128)(2,1)S(1)}, u32[]{:S(2)}, u32[]{:S(2)}) collective-permute-start(bf16[96,768]{1,0:T(8,128)(2,1)S(1)} %get-tuple-element.171), channel_id=1, source_target_pairs={{0,16},{1,17},{2,18},{3,19},{4,20},{5,21},{6,22},{7,23},{8,24},{9,... | collective-permute-start | bytes 442376 | tf_op jit(solution)/shard_map/ppermute | solution.py:56
  218.9 12.4 %collective-permute-start.55 = (bf16[1552,768]{1,0:T(8,128)(2,1)S(1)}, bf16[1552,768]{1,0:T(8,128)(2,1)S(1)}, u32[]{:S(2)}, u32[]{:S(2)}) collective-permute-start(bf16[1552,768]{1,0:T(8,128)(2,1)S(1)} %join_l.1.refs_1_), channel_id=1, source_target_pairs={{0,4},{1,5},{2,6},{3,7},{4,0},{5,1},{6,2},{7,3},{8,12},{9,13},{10,... | collective-permute-start | bytes 7151624 | tf_op jit(solution)/shard_map/ppermute | solution.py:56
  221.8 5.9 %collective-permute-start.56 = (bf16[4,2,96,768]{3,2,1,0:T(8,128)(2,1)S(1)}, bf16[4,2,96,768]{3,2,1,0:T(8,128)(2,1)S(1)}, u32[]{:S(2)}, u32[]{:S(2)}) collective-permute-start(bf16[4,2,96,768]{3,2,1,0:T(8,128)(2,1)S(1)} %bitcast.13), channel_id=1, source_target_pairs={{0,4},{1,5},{2,6},{3,7},{4,0},{5,1},{6,2},{7,3},{8,12},{9,13},{10,... | collective-permute-start | bytes 3538952 | tf_op jit(solution)/shard_map/ppermute | solution.py:56
  (33 other events, 174.2 us)

commit v3 on v2

--- a/solution.py
+++ b/solution.py
@@ -407,7 +407,7 @@
         )
     vectors = jnp.concatenate([vec_ref[0:10, :]] + placed + [vec_ref[12:VEC_ROWS, :]], axis=0)
     vectors = vectors.astype(bf16)
-    for out in (la_keep, la_send):
+    for out in (la_keep, la_send, lb_keep, lb_send):
         out[HELD : HELD + VEC_ROWS, :] = vectors[:, :HALF]
         out[HELD + VEC_ROWS :, :] = vectors[:, HALF:]
 
@@ -422,49 +422,54 @@
     keep_ref[...] = mm_nt(all_scr[:half, :], w_ref[...]).astype(bf16)
 
 
-def ffn_out_kernel(info, f_ref, f_other, w_in_out, w_back_out, flip_scr):
-    mine = info[1]
-    for side, ref in enumerate((f_ref, f_other)):
-        for place_xy in range(4):
-            mask = side | (X_BIT if place_xy & 1 else 0) | (Y_BIT if place_xy & 2 else 0)
-            start = pl.multiple_of((mine ^ mask) * SLICE, SLICE)
-            w_in_out[pl.ds(start, SLICE), :] = ref[place_xy, 0].astype(f32)
-            flip_scr[pl.ds(start, SLICE), :] = ref[place_xy, 1].astype(f32)
-    w_back_out[...] = flip_scr[...].T
-
-
-def qkv_out_kernel(info, c_ref, c_other, qkv_out, out_out, *rest):
-    vec_outs, (all_scr, flip_scr) = rest[:9], rest[9:]
-    quarter, z_here, here = info[0], info[2], info[3]
+def final_kernel(info, c_ref, c_other, f_ref, f_other, low_tokens, low_out, *rest):
+    qkv_out, out_out, w_in_out, w_back_out, layer_out, token_out = rest[:6]
+    vec_outs, (all_scr, flip_scr, out_scr, back_scr) = rest[6:15], rest[15:]
+    quarter, mine, z_here, here = info[0], info[1], info[2], info[3]
+    block = pl.program_id(0)
     count = 16 * SLICE
-    for side, ref in enumerate((c_ref, c_other)):
-        for n in range(16):
-            all_scr[side * 16 + n] = ref[n * SLICE : (n + 1) * SLICE, :]
-    vectors = total(c_ref[count:, :], c_other[count:, :])
-    bias_in = jnp.zeros((1, WIDTH), f32)
-    for q in range(TP):
-        bias_in = jnp.where(z_here == q, vectors[6 + q : 7 + q, :], bias_in)
-    for out, n in zip(vec_outs[:8], (0, 1, 2, 3, 4, 5, 10, 11)):
-        out[...] = vectors[n]
-    vec_outs[8][...] = bias_in[0]
-    for block in range(SLOTS):
-        pieces = []
-        for group in range(TP):
-            group_off = quarter ^ group
-            block_off = here ^ block
-            xy = ((block_off >> 2) & 1) + (block_off & 2)
-            z_off = (group_off & 1) + 2 * (block_off & 1)
-            slot = (group_off >> 1) * 16 + xy * 4 + z_off
-            pieces.append(all_scr[slot])
-        rows = slice(block * SLICE, (block + 1) * SLICE)
-        for kind in range(4):
-            cols = slice(kind * GROUP_WIDTH, (kind + 1) * GROUP_WIDTH)
-            joined = jnp.concatenate([piece[:, cols] for piece in pieces], axis=1).astype(f32)
-            if kind < 3:
-                qkv_out[rows, kind * WIDTH : (kind + 1) * WIDTH] = joined
-            else:
-                flip_scr[rows, :] = joined
-    out_out[...] = flip_scr[...].T
+
+    def piece(group, at):
+        group_off, block_off = quarter ^ group, here ^ at
+        xy = ((block_off >> 2) & 1) + (block_off & 2)
+        return all_scr[(group_off >> 1) * 16 + xy * 4 + (group_off & 1) + 2 * (block_off & 1)]
+
+    def ffn_piece(at, part):
+        mask = mine ^ at
+        nth = (((mask >> 1) & 1) + ((mask >> 2) & 1) * 2) * 2 + part
+        return jnp.where((mask & 1) == 1, f_other[nth].astype(f32), f_ref[nth].astype(f32))
+
+    @pl.when(block == 0)
+    def _():
+        for side, ref in enumerate((c_ref, c_other)):
+            for n in range(16):
+                all_scr[side * 16 + n] = ref[n * SLICE : (n + 1) * SLICE, :]
+        vectors = total(c_ref[count:, :], c_other[count:, :])
+        bias_in = jnp.zeros((1, WIDTH), f32)
+        for q in range(TP):
+            bias_in = jnp.where(z_here == q, vectors[6 + q : 7 + q, :], bias_in)
+        for out, n in zip(vec_outs[:8], (0, 1, 2, 3, 4, 5, 10, 11)):
+            out[...] = vectors[n]
+        vec_outs[8][...] = bias_in[0]
+        for at in range(SLOTS):
+            rows = slice(at * SLICE, (at + 1) * SLICE)
+            last = [piece(group, at)[:, 3 * GROUP_WIDTH :] for group in range(TP)]
+            flip_scr[rows, :] = jnp.concatenate(last, axis=1).astype(f32)
+            back_scr[rows, :] = ffn_piece(at, 1)
+        out_scr[...] = flip_scr[...].T
+        flip_scr[...] = back_scr[...].T
+
+    rows = pl.ds(pl.multiple_of(block * SLICE, SLICE), SLICE)
+    pieces = [piece(group, block) for group in range(TP)]
+    for kind in range(3):
+        cols = slice(kind * GROUP_WIDTH, (kind + 1) * GROUP_WIDTH)
+        joined = jnp.concatenate([part[:, cols] for part in pieces], axis=1)
+        qkv_out[:, kind * WIDTH : (kind + 1) * WIDTH] = joined.astype(f32)
+    out_out[...] = out_scr[rows, :]
+    w_back_out[...] = flip_scr[rows, :]
+    w_in_out[...] = ffn_piece(block, 0)
+    layer_out[...] = low_out[...]
+    token_out[...] = low_tokens[...]
 
 
 def add_to(out, *terms):
@@ -505,34 +510,46 @@
     add_to(second, keep[1, 2:], other[1, 2:])
 
 
-def level_two_kernel(*refs):
-    first, second = refs[-2:]
+def middle_kernel(in_keep, in_other, back_keep, back_other, back_x, back_y, to_x, to_y):
     for n in range(2):
-        keep, other, by_x, by_y = refs[4 * n : 4 * n + 4]
-        add_to(first.at[n], keep[0, 1], other[0, 1], by_x[1])
-        add_to(second.at[n], keep[1, 1], other[1, 1], by_y[1])
-
-
-def plane_kernel(*refs):
-    by_xy, by_yx, near, kept = refs[-4:]
-    for n in range(2):
-        keep, other, by_x, by_y = refs[4 * n : 4 * n + 4]
-        for q in range(TP):
-            order, pair = q // 2, q % 2
-            first, second = (by_x, by_xy) if order == 0 else (by_y, by_yx)
-            out = near if q % 2 else kept
-            add_to(
-                out.at[q // 2, n], keep[order, 0, pair], other[order, 0, pair], first[0, pair], second[n, pair]
-            )
+        out = to_y if n else to_x
+        for p in range(2):
+            for pair in range(2):
+                add_to(out.at[2 * p + pair], in_keep[n, 2 + p, pair], in_other[n, 2 + p, pair])
+    for pair in range(2):
+        add_to(to_y.at[4 + pair], back_keep[0, 1, pair], back_other[0, 1, pair], back_x[1, pair])
+        add_to(to_x.at[4 + pair], back_keep[1, 1, pair], back_other[1, 1, pair], back_y[1, pair])
+
+
+def in_two_kernel(keep, other, by_x, by_y, first, second):
+    for pair in range(2):
+        add_to(first.at[pair], keep[0, 1, pair], other[0, 1, pair], by_x[2 + pair])
+        add_to(second.at[pair], keep[1, 1, pair], other[1, 1, pair], by_y[2 + pair])
+
+
+def in_plane_kernel(keep, other, by_x, by_y, by_xy, by_yx, near, kept):
+    for q in range(TP):
+        order, pair = q // 2, q % 2
+        first, second = (by_x, by_xy) if order == 0 else (by_y, by_yx)
+        out = near if q % 2 else kept
+        add_to(out.at[q // 2], keep[order, 0, pair], other[order, 0, pair], first[pair], second[pair])
+
+
+def back_plane_kernel(keep, other, by_x, by_y, mid_x, mid_y, near, kept):
+    for q in range(TP):
+        order, pair = q // 2, q % 2
+        first, second = (by_x, mid_y) if order == 0 else (by_y, mid_x)
+        out = near if q % 2 else kept
+        add_to(out.at[q // 2], keep[order, 0, pair], other[order, 0, pair], first[0, pair], second[4 + pair])
 
 
 def far_kernel(kept, near, far):
     add_to(far, kept[1], near[1])
 
 
-def last_kernel(kept, near, far, out):
-    for n in range(2):
-        add_to(out.at[n], kept[0, 1 - n], near[0, 1 - n], far[1 - n])
+def last_kernel(kept_a, near_a, far_a, kept_b, near_b, far_b, out):
+    add_to(out.at[0], kept_a[0], near_a[0], far_a[...])
+    add_to(out.at[1], kept_b[0], near_b[0], far_b[...])
 
 
 def go_kernel(keep, other, own, send):
@@ -544,8 +561,9 @@
     add_to(out, keep[QUARTER:], other[QUARTER:])
 
 
-def tokens_kernel(keep, other, near, grad_in, out):
-    add_to(out, keep[:QUARTER], other[:QUARTER], near[...], grad_in[...])
+def tokens_kernel(keep, other, near, grad_in, out_here, tokens, again):
+    add_to(tokens, keep[:QUARTER], other[:QUARTER], near[...], grad_in[...])
+    again[...] = out_here[...]
 
 
 TWO = 2 * SLICE
@@ -553,7 +571,7 @@
 
 def qkv_two_kernel(la, ra, lb, rb, la_out, lb_out):
     add_to(la_out, la[TWO:], ra[TWO:])
-    add_to(lb_out, lb[TWO:], rb[TWO:])
+    add_to(lb_out, lb[TWO:HELD], rb[TWO:HELD])
 
 
 def qkv_three_kernel(la, ra, ra2, lb, rb, rb2, out):
@@ -852,26 +870,30 @@
     go_own, go_send = step(go_kernel, "go", [(WIDTH, GROUP_WIDTH)] * 2, go_keep, go_other)
     go_near = hop(go_send, 0, 1)
     gh0, s0 = head_back(0, (go_own, back_sums[0]))
-    sums = step(level_one_kernel, "in_one", first_level, in_keep, in_other, deps=(gh0, back_x, back_y, go_near))
-    in_x, in_y = hop_pair(sums, X_BIT, Y_BIT)
-    gh1, s1 = head_back(1, (sums[0],))
+    back_parts = [back_keep, back_other, back_x, back_y]
+    to_x, to_y = step(
+        middle_kernel,
+        "middle",
+        [(6, SLICE, WIDTH)] * 2,
+        in_keep,
+        in_other,
+        *back_parts,
+        deps=(gh0,),
+    )
+    mid_x, mid_y = hop(to_x, X_BIT, 0), hop(to_y, Y_BIT, 0)
+    in_parts = [in_keep, in_other, mid_x, mid_y]
+    z_level = [(2, SLICE, WIDTH)] * 2
+    gh1, s1 = head_back(1, (to_x,))
     gh2, s2 = head_back(2, (gh1,))
-    back_parts = [back_keep, back_other, back_x, back_y]
-    in_parts = [in_keep, in_other, in_x, in_y]
-    sums = step(
-        level_two_kernel, "two", [(2, 2, SLICE, WIDTH)] * 2, *back_parts, *in_parts, deps=(gh2,)
-    )
-    by_xy, by_yx = hop_pair(sums, Y_BIT, X_BIT)
-    layer_out = place(out_here)[None]
 
     la_keep, la_send, lb_keep, lb_send = call(
         qkv_grad_kernel,
         [SMEM] + [VMEM] * 10,
-        [((HELD + 2 * VEC_ROWS, HALF), bf16)] * 2 + [((HELD, HALF), bf16)] * 2,
+        [((HELD + 2 * VEC_ROWS, HALF), bf16)] * 4,
         [pltpu.VMEM((WIDTH, 4 * GROUP_WIDTH), bf16)],
         16,
         "qkv_grads",
-        (layer_out, sums[0]),
+        (gh2,),
     )(info, tokens_t, gh0, gh1, gh2, go_own, go_near, vectors, s0, s1, s2)
     ra = hop(la_send, X_BIT, 0)
     rb = hop(lb_send, Y_BIT, 0)
@@ -886,9 +908,16 @@
         (la_keep,),
     )(gh0, gh1, gh2, w_group)
     other = hop(send, CORE, 0)
-    near_low = step(near_kernel, "near", [(QUARTER, WIDTH)], keep, other)
+    near_b, kept_b = step(
+        back_plane_kernel, "back_plane", z_level, *back_parts, mid_x, mid_y, deps=(keep,)
+    )
+    near_b = hop(near_b, 0, 1)
+    sums = step(in_two_kernel, "in_two", z_level, *in_parts, deps=(kept_b,))
+    in_parts += hop_pair(sums, Y_BIT, X_BIT)
+    near_low = step(near_kernel, "near", [(QUARTER, WIDTH)], keep, other, deps=(sums[0],))
     near = hop(near_low, 0, 1)
-
+    far_b = step(far_kernel, "far_back", [(SLICE, WIDTH)], kept_b, near_b, deps=(near_low,))
+    far_hop_b = hop(far_b, 0, 2)
     la2, lb2 = step(
         qkv_two_kernel,
         "qkv_two",
@@ -897,34 +926,23 @@
         ra,
         lb_keep,
         rb,
-        deps=(near,),
+        deps=(far_b,),
     )
     ra2 = hop(la2, Y_BIT, 0)
     rb2 = hop(lb2, X_BIT, 0)
     rows_l = (TWO + VEC_ROWS, WIDTH)
-    partial = step(qkv_three_kernel, "qkv_three", [rows_l], la_keep, ra, ra2, lb_keep, rb, rb2)
-    near_sum, kept = step(
-        plane_kernel,
-        "plane_sum",
-        [(2, 2, SLICE, WIDTH)] * 2,
-        *back_parts,
-        *in_parts,
-        by_xy,
-        by_yx,
-        deps=(la2,),
-    )
-    near_f = hop(near_sum, 0, 1)
-    far_low = step(far_kernel, "far", [(2, SLICE, WIDTH)], kept, near_f, deps=(partial,))
-    far_f = hop(far_low, 0, 2)
-    low_tokens = step(
-        tokens_kernel, "tokens", [(QUARTER, WIDTH)], keep, other, near, grad_in, deps=(partial,)
-    )
+    near_a, kept_a = step(in_plane_kernel, "in_plane", z_level, *in_parts, deps=(la2,))
+    near_a = hop(near_a, 0, 1)
+    partial = step(
+        qkv_three_kernel, "qkv_three", [rows_l], la_keep, ra, ra2, lb_keep, rb, rb2, deps=(kept_a, far_hop_b)
+    )
+    far_a = step(far_kernel, "far_in", [(SLICE, WIDTH)], kept_a, near_a, deps=(partial, far_hop_b))
+    far_hop_a = hop(far_a, 0, 2)
     sum_l = step(
-        qkv_four_kernel, "qkv_four", [rows_l], partial, hop(partial, 0, 2), deps=(far_low, low_tokens)
+        qkv_four_kernel, "qkv_four", [rows_l], partial, hop(partial, 0, 2), deps=(far_a, near)
     )
     for bit in extra_bits:
         sum_l = add_low(sum_l, hop(sum_l, bit, 0))
-    grad_tokens = place(low_tokens)[None]
 
     own_l = sum_l[:TWO]
     x_own = hop(own_l, X_BIT, 0)
@@ -935,27 +953,41 @@
     )
     x_other = hop(to_x, X_BIT, 0)
     y_other = hop(to_y, Y_BIT, 0)
-    sum_f = step(last_kernel, "last", [(2, SLICE, WIDTH)], kept, near_f, far_f, deps=(to_x,))
+    sum_f = step(
+        last_kernel,
+        "last",
+        [(2, SLICE, WIDTH)],
+        kept_a,
+        near_a,
+        far_hop_a,
+        kept_b,
+        near_b,
+        far_hop_b,
+        deps=(to_x,),
+    )
     for bit in extra_bits:
         sum_f = add_low(sum_f, hop(sum_f, bit, 0))
+    low_outs = step(
+        tokens_kernel,
+        "tokens",
+        [(QUARTER, WIDTH)] * 2,
+        keep,
+        other,
+        near,
+        grad_in,
+        out_here,
+        deps=(sum_f,),
+    )
+    token_grads, layer_out = place(low_outs[0]), place(low_outs[1])
     f_x = hop(sum_f, X_BIT, 0)
     f_y = hop(sum_f, Y_BIT, 0)
+    diag_f = step(diag_kernel, "diag_f", [(1, SLICE, WIDTH)] * 2, f_x, f_y, deps=(to_x,))
+    f_d0, f_d1 = hop_pair(diag_f, Y_BIT, X_BIT)
     diag_l = step(
-        diag_l_kernel, "diag_l", [(SLICE, WIDTH)] * 2, x_other, y_other, deps=(sum_f, grad_tokens)
+        diag_l_kernel, "diag_l", [(SLICE, WIDTH)] * 2, x_other, y_other, deps=(diag_f[0],)
     )
     d_x, d_y = hop_pair(diag_l, X_BIT, Y_BIT)
-    diag_f = step(diag_kernel, "diag_f", [(1, SLICE, WIDTH)] * 2, f_x, f_y, deps=(diag_l[0],))
-    f_d0, f_d1 = hop_pair(diag_f, Y_BIT, X_BIT)
     f_all = step(join_kernel, "join_f", [(8, SLICE, WIDTH)], sum_f, f_x, f_y, f_d0, f_d1)
-    f_all = f_all.reshape(4, 2, SLICE, WIDTH)
-    grad_w_in, grad_w_back = call(
-        ffn_out_kernel,
-        [SMEM, VMEM, VMEM],
-        [((WIDTH, WIDTH), f32)] * 2,
-        [pltpu.VMEM((WIDTH, WIDTH), f32)],
-        24,
-        "ffn_out",
-    )(info, f_all, hop(f_all, CORE, 0))
     plane = step(
         plane_l_kernel,
         "join_l",
@@ -968,17 +1000,32 @@
         y_other,
         d_x,
         d_y,
-        deps=(f_all,),
-    )
-    grad_w_qkv, grad_w_out, *vec_outs = call(
-        qkv_out_kernel,
-        [SMEM, VMEM, VMEM],
-        [((WIDTH, 3 * WIDTH), f32), ((WIDTH, WIDTH), f32)] + [((WIDTH,), f32)] * 9,
-        [pltpu.VMEM((32, SLICE, WIDTH), bf16), pltpu.VMEM((WIDTH, WIDTH), f32)],
-        24,
-        "qkv_out",
-        (grad_w_in,),
-    )(info, plane, hop(plane, CORE, 0))
+        deps=(f_all, token_grads, layer_out),
+    )
+    whole = pl.BlockSpec(memory_space=pltpu.VMEM)
+    piece_rows = QUARTER // SLOTS
+    by_rows = lambda rows, cols: pl.BlockSpec((rows, cols), lambda i: (i, 0))
+    square = ((WIDTH, WIDTH), f32)
+    grad_w_qkv, grad_w_out, grad_w_in, grad_w_back, layer_out, grad_tokens, *vec_outs = pl.pallas_call(
+        final_kernel,
+        grid=(SLOTS,),
+        out_shape=[
+            jax.ShapeDtypeStruct(shape, dtype)
+            for shape, dtype in [((WIDTH, 3 * WIDTH), f32), square, square, square, rows, rows]
+            + [((WIDTH,), f32)] * 9
+        ],
+        in_specs=[SMEM]
+        + [whole] * 4
+        + [by_rows(piece_rows, WIDTH)] * 2,
+        out_specs=[by_rows(SLICE, 3 * WIDTH)]
+        + [by_rows(SLICE, WIDTH)] * 3
+        + [by_rows(piece_rows, WIDTH)] * 2
+        + [pl.BlockSpec((WIDTH,), lambda i: (0,))] * 9,
+        scratch_shapes=[pltpu.VMEM((32, SLICE, WIDTH), bf16)] + [pltpu.VMEM((WIDTH, WIDTH), f32)] * 3,
+        compiler_params=pltpu.CompilerParams(vmem_limit_bytes=36 * 1024 * 1024),
+        cost_estimate=pl.CostEstimate(flops=1, bytes_accessed=1, transcendentals=0),
+        name="final",
+    )(info, plane, hop(plane, CORE, 0), f_all, hop(f_all, CORE, 0), token_grads, layer_out)
     (
         grad_shift_ffn,
         grad_gain_ffn,
@@ -991,8 +1038,8 @@
         grad_bias_in,
     ) = vec_outs
     return (
-        layer_out,
-        grad_tokens,
+        layer_out[None],
+        grad_tokens[None],
         grad_w_qkv,
         grad_bias_query,
         grad_bias_value,

time: 244 us -> 231 us (0.947)
  waiting for transfers between devices: 92 us -> 86.6 us
  local copies, waits for them, and re-layouts: 10.5 us -> 7.35 us
  starting transfers between devices: 73.3 us -> 70.4 us
    pallas_call x37, Pallas kernels: 63.1 us -> 53.7 us  [call(): return lambda *arrays: run(*arrays, *deps)]
    pallas_call x0 -> x1, Pallas kernels: none -> 7.73 us  [per_device(): pl.pallas_call(final_kernel, grid=(SLOTS,), out_shape=[jax.ShapeDtypeStru...]
    ppermute x53 -> x55, starting transfers between devices: 51.8 us -> 46.2 us  [hop(): return lax.ppermute(array, ('dp', 'tp'), pairs)]
    ppermute x53 -> x55, waiting for transfers between devices: 83.7 us -> 79.1 us  [hop(): return lax.ppermute(array, ('dp', 'tp'), pairs)]
    unnamed x51 -> x47, local copies, waits for them, and re-layouts: 9.29 us -> 6.14 us
    ppermute x4, starting transfers between devices: 21.4 us -> 24.2 us  [place(): return lax.ppermute(array, ('dp', 'tp'), pairs)]
  transfers between devices with their start and end apart: 57 -> 59, of which waited for: 23 -> 24; matrix products, arithmetic and copies ran while one was open for 1% -> 1% of each run, Pallas kernels for 17% -> 19%
where the time goes in v3:
time: 231 us; the launch traced here: 227 us
  waiting for transfers between devices  86.6 us (37%)
  starting transfers between devices  70.4 us (30%)
  Pallas kernels  61.4 us (27%)
  local copies, waits for them, and re-layouts  7.35 us (3%)
    ppermute x55, waiting for transfers between devices, hop(): return lax.ppermute(array, ('dp', 'tp'), pairs)  79.1 us
    pallas_call x37, Pallas kernels, call(): return lambda *arrays: run(*arrays, *deps)  53.7 us
    ppermute x55, starting transfers between devices, hop(): return lax.ppermute(array, ('dp', 'tp'), pairs)  46.2 us
    ppermute x4, starting transfers between devices, place(): return lax.ppermute(array, ('dp', 'tp'), pairs)  24.2 us
    pallas_call x1, Pallas kernels, per_device(): pl.pallas_call(final_kernel, grid=(SLOTS,), out_shape=[jax.ShapeDtypeStru...  7.73 us
    ppermute x4, waiting for transfers between devices, place(): return lax.ppermute(array, ('dp', 'tp'), pairs)  7.58 us
    unnamed x47, local copies, waits for them, and re-layouts  6.14 us
  transfers between devices with their start and end apart: 59, of which 24 were waited for; matrix products, arithmetic and copies ran while one was open for 1% of the time, Pallas kernels for 19%

profile of v3, /device:TPU:1, one launch (start us, length us, event | category | flops | bytes accessed | tf_op | source)
XLA Modules:
  0.0 227.3 jit_solution(18398141415945018472)
XLA Ops:
  0.7 5.7 %collective-permute-start = (bf16[256,768]{1,0:T(8,128)(2,1)}, bf16[256,768]{1,0:T(8,128)(2,1)S(1)}, u32[]{:S(2)}, u32[]{:S(2)}) collective-permute-start(bf16[256,768]{1,0:T(8,128)(2,1)} %bitcast.11), channel_id=1, source_target_pairs={{0,0},{1,1},{2,4},{3,5},{4,2},{5,3},{6,6},{7,7},{8,8},{9,9},{10,12... | collective-permute-start | bytes 1179656 | tf_op jit(solution)/shard_map/ppermute | solution.py:67
  6.5 1.3 copy-done
  7.8 1.3 copy-done.2
  10.9 1.4 collective-permute-start.5
  12.3 2.0 copy-done.4
  15.2 12.1 %collective-permute-done.6.refs_1_ = bf16[208,768]{1,0:T(8,128)(2,1)S(1)} collective-permute-done((bf16[208,768]{1,0:T(8,128)(2,1)S(1)}, bf16[208,768]{1,0:T(8,128)(2,1)S(1)}, u32[]{:S(2)}, u32[]{:S(2)}) %collective-permute-start.6) | collective-permute-done | bytes 319520 | tf_op jit(solution)/shard_map/ppermute | solution.py:56
  27.4 1.3 collective-permute-start.8
  29.9 3.1 %collective-permute-start.1 = (bf16[256,768]{1,0:T(8,128)(2,1)S(1)}, bf16[256,768]{1,0:T(8,128)(2,1)S(1)}, u32[]{:S(2)}, u32[]{:S(2)}) collective-permute-start(bf16[256,768]{1,0:T(8,128)(2,1)S(1)} %collective-permute-done.refs_2_.refs_3_.refs_0_.refs_1_), channel_id=1, source_target_pairs={{0,1},{1,0},{2,3},{3,2},{4,5},{5,4},{6,7},{7,6},{8,9},{9,8},{10,11... | collective-permute-start | bytes 1179656 | tf_op jit(solution)/shard_map/ppermute | solution.py:56
  33.0 14.5 %collective-permute-done.9.refs_2_.refs_3_ = bf16[208,768]{1,0:T(8,128)(2,1)S(1)} collective-permute-done((bf16[208,768]{1,0:T(8,128)(2,1)S(1)}, bf16[208,768]{1,0:T(8,128)(2,1)S(1)}, u32[]{:S(2)}, u32[]{:S(2)}) %collective-permute-start.9) | collective-permute-done | bytes 319520 | tf_op jit(solution)/shard_map/ppermute | solution.py:56
  49.3 2.9 %collective-permute-start.2 = (bf16[256,768]{1,0:T(8,128)(2,1)S(1)}, bf16[256,768]{1,0:T(8,128)(2,1)S(1)}, u32[]{:S(2)}, u32[]{:S(2)}) collective-permute-start(bf16[256,768]{1,0:T(8,128)(2,1)S(1)} %collective-permute-done.refs_2_.refs_3_.refs_0_.refs_1_), channel_id=1, source_target_pairs={{0,4},{1,5},{2,6},{3,7},{4,0},{5,1},{6,2},{7,3},{8,12},{9,13},{10,... | collective-permute-start | bytes 1179656 | tf_op jit(solution)/shard_map/ppermute | solution.py:56
  55.5 3.6 %collective-permute-start.14 = (bf16[256,768]{1,0:T(8,128)(2,1)}, bf16[256,768]{1,0:T(8,128)(2,1)S(1)}, u32[]{:S(2)}, u32[]{:S(2)}) collective-permute-start(bf16[256,768]{1,0:T(8,128)(2,1)} %bitcast.12), channel_id=1, source_target_pairs={{0,0},{1,1},{2,4},{3,5},{4,2},{5,3},{6,6},{7,7},{8,8},{9,9},{10,12... | collective-permute-start | bytes 1179656 | tf_op jit(solution)/shard_map/ppermute | solution.py:67
  59.2 10.7 %attention.1 = (bf16[384,128]{1,0:T(8,128)(2,1)S(1)}, bf16[768,128]{1,0:T(8,128)(2,1)S(1)}, bf16[384,128]{1,0:T(8,128)(2,1)S(1)}, bf16[1024,64]{1,0:T(8,128)(2,1...) custom-call(s32[5]{0:T(128)S(1)} %stack.27.refs_0_.info, ...), custom_call_target="tpu_custom_call" | custom-call | flops 1 | bytes 1 | tf_op jit(solution)/shard_map/attention/pallas_call | solution.py:641
  70.0 1.3 collective-permute-done.13.refs_6_.refs_4_
  71.3 1.3 held.1.refs_5_.refs_1_
  74.1 1.3 collective-permute-start.18
  76.6 2.4 %collective-permute-done.10.refs_4_.refs_3_ = bf16[768,128]{1,0:T(8,128)(2,1)S(1)} collective-permute-done((bf16[768,128]{1,0:T(8,128)(2,1)S(1)}, bf16[768,128]{1,0:T(8,128)(2,1)S(1)}, u32[]{:S(2)}, u32[]{:S(2)}) %collective-permute-start.10) | collective-permute-done | bytes 196640 | tf_op jit(solution)/shard_map/ppermute | solution.py:56
  79.0 1.5 flip_tokens.1.refs_2_.refs_20_.refs_1_
  84.2 6.3 %ffn.1 = (bf16[256,768]{1,0:T(8,128)(2,1)S(1)}, f32[256,768]{1,0:T(8,128)S(1)}, f32[256,768]{1,0:T(8,128)S(1)}, bf16[256,768]{1,0:T(8,128)(2,1)S(1)}, bf16[256,7...) custom-call(s32[5]{0:T(128)S(1)} %stack.27.refs_0_.info, ...), custom_call_target="tpu_custom_call" | custom-call | flops 1 | bytes 1 | tf_op jit(solution)/shard_map/ffn/pallas_call | solution.py:641
  90.5 2.1 back_grads.1
  93.0 5.6 %ffn_back.1 = (bf16[384,128]{1,0:T(8,128)(2,1)S(1)}, bf16[768,128]{1,0:T(8,128)(2,1)S(1)}, bf16[384,128]{1,0:T(8,128)(2,1)S(1)}, f32[256,768]{1,0:T(8,128)S(1)},...) custom-call(s32[5]{0:T(128)S(1)} %stack.27.refs_0_.info, ...), custom_call_target="tpu_custom_call" | custom-call | flops 1 | bytes 1 | tf_op jit(solution)/shard_map/ffn_back/pallas_call | solution.py:641
  99.5 1.3 collective-permute-start.27
  102.6 5.2 %collective-permute-done.20.refs_8_ = bf16[768,128]{1,0:T(8,128)(2,1)S(1)} collective-permute-done((bf16[768,128]{1,0:T(8,128)(2,1)S(1)}, bf16[768,128]{1,0:T(8,128)(2,1)S(1)}, u32[]{:S(2)}, u32[]{:S(2)}) %collective-permute-start.20) | collective-permute-done | bytes 196640 | tf_op jit(solution)/shard_map/ppermute | solution.py:56
  107.8 1.6 collective-permute-start.21
  110.9 4.9 %attention_back_0.1 = (bf16[1024,192]{1,0:T(8,128)(2,1)S(1)}, f32[8,192]{1,0:T(8,128)S(1)}) custom-call(s32[5]{0:T(128)S(1)} %stack.27.refs_0_.info, s32[576]{0:T(1024)S(1)} %reshape.33.refs_1_, s32[576]{0:T(1024)S(1)} %collective-permute-done.4.refs_2_, bf16[1024,64]{1,0:T(8,128)(2,1)S(1)} %get-tuple-element.113.refs_3_, ...), custom_call_target="tpu_custom_call" | custom-call | flops 1 | bytes 1 | tf_op jit(solution)/shard_map/attention_back_0/pallas_call | solution.py:641
  117.5 4.5 %attention_back_1.1 = (bf16[1024,192]{1,0:T(8,128)(2,1)S(1)}, f32[8,192]{1,0:T(8,128)S(1)}) custom-call(s32[5]{0:T(128)S(1)} %stack.27.refs_0_.info, s32[576]{0:T(1024)S(1)} %reshape.33.refs_1_, s32[576]{0:T(1024)S(1)} %collective-permute-done.4.refs_2_, bf16[1024,64]{1,0:T(8,128)(2,1)S(1)} %get-tuple-element.142.refs_3_, ...), custom_call_target="tpu_custom_call" | custom-call | flops 1 | bytes 1 | tf_op jit(solution)/shard_map/attention_back_1/pallas_call | solution.py:641
  122.1 4.5 %attention_back_2.1 = (bf16[1024,192]{1,0:T(8,128)(2,1)S(1)}, f32[8,192]{1,0:T(8,128)S(1)}) custom-call(s32[5]{0:T(128)S(1)} %stack.27.refs_0_.info, s32[576]{0:T(1024)S(1)} %reshape.33.refs_1_, s32[576]{0:T(1024)S(1)} %collective-permute-done.4.refs_2_, bf16[1024,64]{1,0:T(8,128)(2,1)S(1)} %get-tuple-element.150.refs_3_, ...), custom_call_target="tpu_custom_call" | custom-call | flops 1 | bytes 1 | tf_op jit(solution)/shard_map/attention_back_2/pallas_call | solution.py:641
  126.6 2.1 qkv_grads.1
  128.7 1.7 token_grad.1
  130.4 1.6 collective-permute-start.34
  133.6 3.2 %collective-permute-done.32.refs_5_.refs_3_ = bf16[6,96,768]{2,1,0:T(8,128)(2,1)S(1)} collective-permute-done((bf16[6,96,768]{2,1,0:T(8,128)(2,1)S(1)}, bf16[6,96,768]{2,1,0:T(8,128)(2,1)S(1)}, u32[]{:S(2)}, u32[]{:S(2)}) %collective-permute-start.32) | collective-permute-done | bytes 884768 | tf_op jit(solution)/shard_map/ppermute | solution.py:56
  139.6 3.4 %collective-permute-done.33.refs_1_.refs_4_ = bf16[2,96,768]{2,1,0:T(8,128)(2,1)S(1)} collective-permute-done((bf16[2,96,768]{2,1,0:T(8,128)(2,1)S(1)}, bf16[2,96,768]{2,1,0:T(8,128)(2,1)S(1)}, u32[]{:S(2)}, u32[]{:S(2)}) %collective-permute-start.33) | collective-permute-done | bytes 294944 | tf_op jit(solution)/shard_map/ppermute | solution.py:56
  144.9 1.5 collective-permute-start.39
  146.9 3.0 %collective-permute-done.38.refs_5_ = bf16[2,96,768]{2,1,0:T(8,128)(2,1)S(1)} collective-permute-done((bf16[2,96,768]{2,1,0:T(8,128)(2,1)S(1)}, bf16[2,96,768]{2,1,0:T(8,128)(2,1)S(1)}, u32[]{:S(2)}, u32[]{:S(2)}) %collective-permute-start.38) | collective-permute-done | bytes 294944 | tf_op jit(solution)/shard_map/ppermute | solution.py:56
  151.4 1.6 collective-permute-done.36.refs_5_
  153.4 1.9 collective-permute-start.40
  156.0 17.1 %collective-permute-done.41.refs_1_ = bf16[2,96,768]{2,1,0:T(8,128)(2,1)S(1)} collective-permute-done((bf16[2,96,768]{2,1,0:T(8,128)(2,1)S(1)}, bf16[2,96,768]{2,1,0:T(8,128)(2,1)S(1)}, u32[]{:S(2)}, u32[]{:S(2)}) %collective-permute-start.41) | collective-permute-done | bytes 294944 | tf_op jit(solution)/shard_map/ppermute | solution.py:56
  173.4 1.6 collective-permute-start.45
  175.3 2.4 %collective-permute-start.48 = (bf16[96,768]{1,0:T(8,128)(2,1)S(1)}, bf16[96,768]{1,0:T(8,128)(2,1)S(1)}, u32[]{:S(2)}, u32[]{:S(2)}) collective-permute-start(bf16[96,768]{1,0:T(8,128)(2,1)S(1)} %far_in.1.refs_2_), channel_id=1, source_target_pairs={{0,2},{1,3},{2,0},{3,1},{4,6},{5,7},{6,4},{7,5},{8,10},{9,11},{10,... | collective-permute-start | bytes 442376 | tf_op jit(solution)/shard_map/ppermute | solution.py:56
  177.7 1.4 collective-permute-done.45.refs_1_.refs_3_
  179.1 1.8 collective-permute-done.44.refs_0_.refs_2_
  181.5 1.8 collective-permute-start.50
  185.1 9.1 %collective-permute-start.55 = (bf16[256,768]{1,0:T(8,128)(2,1)S(1)}, bf16[256,768]{1,0:T(8,128)(2,1)S(1)}, u32[]{:S(2)}, u32[]{:S(2)}) collective-permute-start(bf16[256,768]{1,0:T(8,128)(2,1)S(1)} %get-tuple-element.182), channel_id=1, source_target_pairs={{0,0},{1,1},{2,4},{3,5},{4,2},{5,3},{6,6},{7,7},{8,8},{9,9},{10,12... | collective-permute-start | bytes 1179656 | tf_op jit(solution)/shard_map/ppermute | solution.py:67
  194.2 5.7 %collective-permute-start.56 = (bf16[256,768]{1,0:T(8,128)(2,1)S(1)}, bf16[256,768]{1,0:T(8,128)(2,1)S(1)}, u32[]{:S(2)}, u32[]{:S(2)}) collective-permute-start(bf16[256,768]{1,0:T(8,128)(2,1)S(1)} %get-tuple-element.183), channel_id=1, source_target_pairs={{0,0},{1,1},{2,4},{3,5},{4,2},{5,3},{6,6},{7,7},{8,8},{9,9},{10,12... | collective-permute-start | bytes 1179656 | tf_op jit(solution)/shard_map/ppermute | solution.py:67
  202.2 1.8 collective-permute-done.54.refs_4_
  204.7 3.4 %collective-permute-done.55.refs_9_.low_tokens = bf16[256,768]{1,0:T(8,128)(2,1)S(1)} collective-permute-done((bf16[256,768]{1,0:T(8,128)(2,1)S(1)}, bf16[256,768]{1,0:T(8,128)(2,1)S(1)}, u32[]{:S(2)}, u32[]{:S(2)}) %collective-permute-start.55) | collective-permute-done | bytes 393248 | tf_op jit(solution)/shard_map/ppermute | solution.py:67
  208.1 4.2 %collective-permute-done.56.refs_10_.low_out = bf16[256,768]{1,0:T(8,128)(2,1)S(1)} collective-permute-done((bf16[256,768]{1,0:T(8,128)(2,1)S(1)}, bf16[256,768]{1,0:T(8,128)(2,1)S(1)}, u32[]{:S(2)}, u32[]{:S(2)}) %collective-permute-start.56) | collective-permute-done | bytes 393248 | tf_op jit(solution)/shard_map/ppermute | solution.py:67
  213.5 5.8 %collective-permute-done.58.f_other = bf16[8,96,768]{2,1,0:T(8,128)(2,1)S(1)} collective-permute-done((bf16[8,96,768]{2,1,0:T(8,128)(2,1)S(1)}, bf16[8,96,768]{2,1,0:T(8,128)(2,1)S(1)}, u32[]{:S(2)}, u32[]{:S(2)}) %collective-permute-start.58) | collective-permute-done | bytes 1179680 | tf_op jit(solution)/shard_map/ppermute | solution.py:56
  219.3 7.7 %final.1 = (f32[768,2304]{1,0:T(8,128)}, f32[768,768]{1,0:T(8,128)}, f32[768,768]{1,0:T(8,128)}, f32[768,768]{1,0:T(8,128)}, bf16[256,768]{1,0:T(8,128)(2,1)}, /...) custom-call(s32[5]{0:T(128)S(1)} %stack.27.refs_0_.info, ...), custom_call_target="tpu_custom_call" | custom-call | flops 1 | bytes 1 | tf_op jit(solution)/shard_map/final/pallas_call | solution.py:1009
  (160 shorter events, 38.3 us)
Async XLA Ops:
  0.7 26.7 %collective-permute-start = (bf16[256,768]{1,0:T(8,128)(2,1)}, bf16[256,768]{1,0:T(8,128)(2,1)S(1)}, u32[]{:S(2)}, u32[]{:S(2)}) collective-permute-start(bf16[256,768]{1,0:T(8,128)(2,1)} %bitcast.11), channel_id=1, source_target_pairs={{0,0},{1,1},{2,4},{3,5},{4,2},{5,3},{6,6},{7,7},{8,8},{9,9},{10,12... | collective-permute-start | bytes 1179656 | tf_op jit(solution)/shard_map/ppermute | solution.py:67
  10.9 16.5 %collective-permute-start.6 = (bf16[208,768]{1,0:T(8,128)(2,1)S(1)}, bf16[208,768]{1,0:T(8,128)(2,1)S(1)}, u32[]{:S(2)}, u32[]{:S(2)}) collective-permute-start(bf16[208,768]{1,0:T(8,128)(2,1)S(1)} %piece.1), channel_id=1, source_target_pairs={{0,2},{1,3},{2,0},{3,1},{4,6},{5,7},{6,4},{7,5},{8,10},{9,11},{10,... | collective-permute-start | bytes 958472 | tf_op jit(solution)/shard_map/ppermute | solution.py:56
  10.9 16.4 %collective-permute-start.5 = (bf16[208,768]{1,0:T(8,128)(2,1)S(1)}, bf16[208,768]{1,0:T(8,128)(2,1)S(1)}, u32[]{:S(2)}, u32[]{:S(2)}) collective-permute-start(bf16[208,768]{1,0:T(8,128)(2,1)S(1)} %piece.1), channel_id=1, source_target_pairs={{0,1},{1,0},{2,3},{3,2},{4,5},{5,4},{6,7},{7,6},{8,9},{9,8},{10,11... | collective-permute-start | bytes 958472 | tf_op jit(solution)/shard_map/ppermute | solution.py:56
  27.4 20.2 %collective-permute-start.8 = (bf16[416,768]{1,0:T(8,128)(2,1)S(1)}, bf16[416,768]{1,0:T(8,128)(2,1)S(1)}, u32[]{:S(2)}, u32[]{:S(2)}) collective-permute-start(bf16[416,768]{1,0:T(8,128)(2,1)S(1)} %pair.1.refs_0_), channel_id=1, source_target_pairs={{0,16},{1,17},{2,18},{3,19},{4,20},{5,21},{6,22},{7,23},{8,24},{9,... | collective-permute-start | bytes 1916936 | tf_op jit(solution)/shard_map/ppermute | solution.py:56
  28.7 18.9 %collective-permute-start.7 = (bf16[416,768]{1,0:T(8,128)(2,1)S(1)}, bf16[416,768]{1,0:T(8,128)(2,1)S(1)}, u32[]{:S(2)}, u32[]{:S(2)}) collective-permute-start(bf16[416,768]{1,0:T(8,128)(2,1)S(1)} %pair.1.refs_0_), channel_id=1, source_target_pairs={{0,8},{1,9},{2,10},{3,11},{4,12},{5,13},{6,14},{7,15},{8,0},{9,1},... | collective-permute-start | bytes 1916936 | tf_op jit(solution)/shard_map/ppermute | solution.py:56
  29.9 17.7 %collective-permute-start.1 = (bf16[256,768]{1,0:T(8,128)(2,1)S(1)}, bf16[256,768]{1,0:T(8,128)(2,1)S(1)}, u32[]{:S(2)}, u32[]{:S(2)}) collective-permute-start(bf16[256,768]{1,0:T(8,128)(2,1)S(1)} %collective-permute-done.refs_2_.refs_3_.refs_0_.refs_1_), channel_id=1, source_target_pairs={{0,1},{1,0},{2,3},{3,2},{4,5},{5,4},{6,7},{7,6},{8,9},{9,8},{10,11... | collective-permute-start | bytes 1179656 | tf_op jit(solution)/shard_map/ppermute | solution.py:56
  33.0 14.6 %collective-permute-start.9 = (bf16[208,768]{1,0:T(8,128)(2,1)S(1)}, bf16[208,768]{1,0:T(8,128)(2,1)S(1)}, u32[]{:S(2)}, u32[]{:S(2)}) collective-permute-start(bf16[208,768]{1,0:T(8,128)(2,1)S(1)} %collective-permute-done.6.refs_1_), channel_id=1, source_target_pairs={{0,1},{1,0},{2,3},{3,2},{4,5},{5,4},{6,7},{7,6},{8,9},{9,8},{10,11... | collective-permute-start | bytes 958472 | tf_op jit(solution)/shard_map/ppermute | solution.py:56
  48.8 22.5 %collective-permute-start.11 = (bf16[432,768]{1,0:T(8,128)(2,1)}, bf16[432,768]{1,0:T(8,128)(2,1)S(1)}, u32[]{:S(2)}, u32[]{:S(2)}) collective-permute-start(bf16[432,768]{1,0:T(8,128)(2,1)} %get-tuple-element.109.refs_9_), channel_id=1, source_target_pairs={{0,8},{1,9},{2,10},{3,11},{4,12},{5,13},{6,14},{7,15},{8,0},{9,1},... | collective-permute-start | bytes 1990664 | tf_op jit(solution)/shard_map/ppermute | solution.py:56
  49.1 22.2 %collective-permute-start.12 = (bf16[400,768]{1,0:T(8,128)(2,1)}, bf16[400,768]{1,0:T(8,128)(2,1)}, u32[]{:S(2)}, u32[]{:S(2)}) collective-permute-start(bf16[400,768]{1,0:T(8,128)(2,1)} %get-tuple-element.111), channel_id=1, source_target_pairs={{0,16},{1,17},{2,18},{3,19},{4,20},{5,21},{6,22},{7,23},{8,24},{9,... | collective-permute-start | bytes 1843208 | tf_op jit(solution)/shard_map/ppermute | solution.py:56
  49.3 9.9 %collective-permute-start.2 = (bf16[256,768]{1,0:T(8,128)(2,1)S(1)}, bf16[256,768]{1,0:T(8,128)(2,1)S(1)}, u32[]{:S(2)}, u32[]{:S(2)}) collective-permute-start(bf16[256,768]{1,0:T(8,128)(2,1)S(1)} %collective-permute-done.refs_2_.refs_3_.refs_0_.refs_1_), channel_id=1, source_target_pairs={{0,4},{1,5},{2,6},{3,7},{4,0},{5,1},{6,2},{7,3},{8,12},{9,13},{10,... | collective-permute-start | bytes 1179656 | tf_op jit(solution)/shard_map/ppermute | solution.py:56
  52.2 7.0 %collective-permute-start.3 = (bf16[256,768]{1,0:T(8,128)(2,1)S(1)}, bf16[256,768]{1,0:T(8,128)(2,1)}, u32[]{:S(2)}, u32[]{:S(2)}) collective-permute-start(bf16[256,768]{1,0:T(8,128)(2,1)S(1)} %collective-permute-done.1.refs_3_.refs_4_.refs_1_), channel_id=1, source_target_pairs={{0,4},{1,5},{2,6},{3,7},{4,0},{5,1},{6,2},{7,3},{8,12},{9,13},{10,... | collective-permute-start | bytes 1179656 | tf_op jit(solution)/shard_map/ppermute | solution.py:56
  55.5 14.5 %collective-permute-start.14 = (bf16[256,768]{1,0:T(8,128)(2,1)}, bf16[256,768]{1,0:T(8,128)(2,1)S(1)}, u32[]{:S(2)}, u32[]{:S(2)}) collective-permute-start(bf16[256,768]{1,0:T(8,128)(2,1)} %bitcast.12), channel_id=1, source_target_pairs={{0,0},{1,1},{2,4},{3,5},{4,2},{5,3},{6,6},{7,7},{8,8},{9,9},{10,12... | collective-permute-start | bytes 1179656 | tf_op jit(solution)/shard_map/ppermute | solution.py:67
  72.6 10.4 %collective-permute-start.16 = (bf16[2288,768]{1,0:T(8,128)(2,1)S(1)}, bf16[2288,768]{1,0:T(8,128)(2,1)S(1)}, u32[]{:S(2)}, u32[]{:S(2)}) collective-permute-start(bf16[2288,768]{1,0:T(8,128)(2,1)S(1)} %held.1.refs_5_.refs_1_), channel_id=1, source_target_pairs={{0,4},{1,5},{2,6},{3,7},{4,0},{5,1},{6,2},{7,3},{8,12},{9,13},{10,... | collective-permute-start | bytes 10543112 | tf_op jit(solution)/shard_map/ppermute | solution.py:56
  72.8 6.1 %collective-permute-start.10 = (bf16[768,128]{1,0:T(8,128)(2,1)S(1)}, bf16[768,128]{1,0:T(8,128)(2,1)S(1)}, u32[]{:S(2)}, u32[]{:S(2)}) collective-permute-start(bf16[768,128]{1,0:T(8,128)(2,1)S(1)} %get-tuple-element.110), channel_id=1, source_target_pairs={{0,1},{1,0},{2,3},{3,2},{4,5},{5,4},{6,7},{7,6},{8,9},{9,8},{10,11... | collective-permute-start | bytes 589832 | tf_op jit(solution)/shard_map/ppermute | solution.py:56
  74.1 6.4 %collective-permute-start.18 = (bf16[112,768]{1,0:T(8,128)(2,1)S(1)}, bf16[112,768]{1,0:T(8,128)(2,1)S(1)}, u32[]{:S(2)}, u32[]{:S(2)}) collective-permute-start(bf16[112,768]{1,0:T(8,128)(2,1)S(1)} %get-tuple-element.119), channel_id=1, source_target_pairs={{0,8},{1,9},{2,10},{3,11},{4,12},{5,13},{6,14},{7,15},{8,0},{9,1},... | collective-permute-start | bytes 516104 | tf_op jit(solution)/shard_map/ppermute | solution.py:56
  92.6 6.6 %collective-permute-start.24 = (bf16[2,4,2,96,768]{4,3,2,1,0:T(8,128)(2,1)S(1)}, bf16[2,4,2,96,768]{4,3,2,1,0:T(8,128)(2,1)S(1)}, u32[]{:S(2)}, u32[]{:S(2)}) collective-permute-start(bf16[2,4,2,96,768]{4,3,2,1,0:T(8,128)(2,1)S(1)} %get-tuple-element.139), channel_id=1, source_target_pairs={{0,4},{1,5},{2,6},{3,7},{4,0},{5,1},{6,2},{7,3},{8,12},{9,13},{10,... | collective-permute-start | bytes 7077896 | tf_op jit(solution)/shard_map/ppermute | solution.py:56
  98.7 17.1 %collective-permute-start.25 = (bf16[2,4,2,96,768]{4,3,2,1,0:T(8,128)(2,1)S(1)}, bf16[2,4,2,96,768]{4,3,2,1,0:T(8,128)(2,1)S(1)}, u32[]{:S(2)}, u32[]{:S(2)}) collective-permute-start(bf16[2,4,2,96,768]{4,3,2,1,0:T(8,128)(2,1)S(1)} %get-tuple-element.146), channel_id=1, source_target_pairs={{0,4},{1,5},{2,6},{3,7},{4,0},{5,1},{6,2},{7,3},{8,12},{9,13},{10,... | collective-permute-start | bytes 7077896 | tf_op jit(solution)/shard_map/ppermute | solution.py:56
  98.8 10.5 %collective-permute-start.23 = (bf16[768,384]{1,0:T(8,128)(2,1)S(1)}, bf16[768,384]{1,0:T(8,128)(2,1)S(1)}, u32[]{:S(2)}, u32[]{:S(2)}) collective-permute-start(bf16[768,384]{1,0:T(8,128)(2,1)S(1)} %get-tuple-element.137), channel_id=1, source_target_pairs={{0,4},{1,5},{2,6},{3,7},{4,0},{5,1},{6,2},{7,3},{8,12},{9,13},{10,... | collective-permute-start | bytes 1769480 | tf_op jit(solution)/shard_map/ppermute | solution.py:56
  99.5 16.3 %collective-permute-start.27 = (bf16[2,2,96,768]{3,2,1,0:T(8,128)(2,1)S(1)}, bf16[2,2,96,768]{3,2,1,0:T(8,128)(2,1)S(1)}, u32[]{:S(2)}, u32[]{:S(2)}) collective-permute-start(bf16[2,2,96,768]{3,2,1,0:T(8,128)(2,1)S(1)} %get-tuple-element.147), channel_id=1, source_target_pairs={{0,16},{1,17},{2,18},{3,19},{4,20},{5,21},{6,22},{7,23},{8,24},{9,... | collective-permute-start | bytes 1769480 | tf_op jit(solution)/shard_map/ppermute | solution.py:56
  100.8 15.0 %collective-permute-start.26 = (bf16[2,2,96,768]{3,2,1,0:T(8,128)(2,1)S(1)}, bf16[2,2,96,768]{3,2,1,0:T(8,128)(2,1)S(1)}, u32[]{:S(2)}, u32[]{:S(2)}) collective-permute-start(bf16[2,2,96,768]{3,2,1,0:T(8,128)(2,1)S(1)} %get-tuple-element.140.refs_12_), channel_id=1, source_target_pairs={{0,8},{1,9},{2,10},{3,11},{4,12},{5,13},{6,14},{7,15},{8,0},{9,1},... | collective-permute-start | bytes 1769480 | tf_op jit(solution)/shard_map/ppermute | solution.py:56
  110.3 16.3 %collective-permute-start.28 = (bf16[768,192]{1,0:T(8,128)(2,1)S(1)}, bf16[768,192]{1,0:T(8,128)(2,1)S(1)}, u32[]{:S(2)}, u32[]{:S(2)}) collective-permute-start(bf16[768,192]{1,0:T(8,128)(2,1)S(1)} %get-tuple-element.154), channel_id=1, source_target_pairs={{0,1},{1,0},{2,3},{3,2},{4,5},{5,4},{6,7},{7,6},{8,9},{9,8},{10,11... | collective-permute-start | bytes 884744 | tf_op jit(solution)/shard_map/ppermute | solution.py:56
  116.3 20.5 %collective-permute-start.32 = (bf16[6,96,768]{2,1,0:T(8,128)(2,1)S(1)}, bf16[6,96,768]{2,1,0:T(8,128)(2,1)S(1)}, u32[]{:S(2)}, u32[]{:S(2)}) collective-permute-start(bf16[6,96,768]{2,1,0:T(8,128)(2,1)S(1)} %get-tuple-element.163), channel_id=1, source_target_pairs={{0,16},{1,17},{2,18},{3,19},{4,20},{5,21},{6,22},{7,23},{8,24},{9,... | collective-permute-start | bytes 2654216 | tf_op jit(solution)/shard_map/ppermute | solution.py:56
  116.6 20.2 %collective-permute-start.31 = (bf16[6,96,768]{2,1,0:T(8,128)(2,1)S(1)}, bf16[6,96,768]{2,1,0:T(8,128)(2,1)S(1)}, u32[]{:S(2)}, u32[]{:S(2)}) collective-permute-start(bf16[6,96,768]{2,1,0:T(8,128)(2,1)S(1)} %get-tuple-element.148.refs_11_), channel_id=1, source_target_pairs={{0,8},{1,9},{2,10},{3,11},{4,12},{5,13},{6,14},{7,15},{8,0},{9,1},... | collective-permute-start | bytes 2654216 | tf_op jit(solution)/shard_map/ppermute | solution.py:56
  130.4 7.9 %collective-permute-start.34 = (bf16[512,768]{1,0:T(8,128)(2,1)S(1)}, bf16[512,768]{1,0:T(8,128)(2,1)S(1)}, u32[]{:S(2)}, u32[]{:S(2)}) collective-permute-start(bf16[512,768]{1,0:T(8,128)(2,1)S(1)} %get-tuple-element.167), channel_id=1, source_target_pairs={{0,4},{1,5},{2,6},{3,7},{4,0},{5,1},{6,2},{7,3},{8,12},{9,13},{10,... | collective-permute-start | bytes 2359304 | tf_op jit(solution)/shard_map/ppermute | solution.py:56
  132.1 11.5 %collective-permute-start.29 = (bf16[416,384]{1,0:T(8,128)(2,1)S(1)}, bf16[416,384]{1,0:T(8,128)(2,1)S(1)}, u32[]{:S(2)}, u32[]{:S(2)}) collective-permute-start(bf16[416,384]{1,0:T(8,128)(2,1)S(1)} %get-tuple-element.160), channel_id=1, source_target_pairs={{0,8},{1,9},{2,10},{3,11},{4,12},{5,13},{6,14},{7,15},{8,0},{9,1},... | collective-permute-start | bytes 958472 | tf_op jit(solution)/shard_map/ppermute | solution.py:56
  132.3 11.3 %collective-permute-start.30 = (bf16[416,384]{1,0:T(8,128)(2,1)S(1)}, bf16[416,384]{1,0:T(8,128)(2,1)S(1)}, u32[]{:S(2)}, u32[]{:S(2)}) collective-permute-start(bf16[416,384]{1,0:T(8,128)(2,1)S(1)} %get-tuple-element.162), channel_id=1, source_target_pairs={{0,16},{1,17},{2,18},{3,19},{4,20},{5,21},{6,22},{7,23},{8,24},{9,... | collective-permute-start | bytes 958472 | tf_op jit(solution)/shard_map/ppermute | solution.py:56
  137.1 5.9 %collective-permute-start.33 = (bf16[2,96,768]{2,1,0:T(8,128)(2,1)S(1)}, bf16[2,96,768]{2,1,0:T(8,128)(2,1)S(1)}, u32[]{:S(2)}, u32[]{:S(2)}) collective-permute-start(bf16[2,96,768]{2,1,0:T(8,128)(2,1)S(1)} %get-tuple-element.166), channel_id=1, source_target_pairs={{0,1},{1,0},{2,3},{3,2},{4,5},{5,4},{6,7},{7,6},{8,9},{9,8},{10,11... | collective-permute-start | bytes 884744 | tf_op jit(solution)/shard_map/ppermute | solution.py:56
  137.8 12.0 %collective-permute-start.38 = (bf16[2,96,768]{2,1,0:T(8,128)(2,1)S(1)}, bf16[2,96,768]{2,1,0:T(8,128)(2,1)S(1)}, u32[]{:S(2)}, u32[]{:S(2)}) collective-permute-start(bf16[2,96,768]{2,1,0:T(8,128)(2,1)S(1)} %get-tuple-element.171), channel_id=1, source_target_pairs={{0,8},{1,9},{2,10},{3,11},{4,12},{5,13},{6,14},{7,15},{8,0},{9,1},... | collective-permute-start | bytes 884744 | tf_op jit(solution)/shard_map/ppermute | solution.py:56
  138.3 12.0 %collective-permute-start.37 = (bf16[2,96,768]{2,1,0:T(8,128)(2,1)S(1)}, bf16[2,96,768]{2,1,0:T(8,128)(2,1)S(1)}, u32[]{:S(2)}, u32[]{:S(2)}) collective-permute-start(bf16[2,96,768]{2,1,0:T(8,128)(2,1)S(1)} %get-tuple-element.168.refs_2_), channel_id=1, source_target_pairs={{0,16},{1,17},{2,18},{3,19},{4,20},{5,21},{6,22},{7,23},{8,24},{9,... | collective-permute-start | bytes 884744 | tf_op jit(solution)/shard_map/ppermute | solution.py:56
  143.7 9.6 %collective-permute-start.35 = (bf16[224,384]{1,0:T(8,128)(2,1)S(1)}, bf16[224,384]{1,0:T(8,128)(2,1)S(1)}, u32[]{:S(2)}, u32[]{:S(2)}) collective-permute-start(bf16[224,384]{1,0:T(8,128)(2,1)S(1)} %get-tuple-element.169.refs_6_), channel_id=1, source_target_pairs={{0,16},{1,17},{2,18},{3,19},{4,20},{5,21},{6,22},{7,23},{8,24},{9,... | collective-permute-start | bytes 516104 | tf_op jit(solution)/shard_map/ppermute | solution.py:56
  144.9 6.5 %collective-permute-start.39 = (bf16[96,768]{1,0:T(8,128)(2,1)S(1)}, bf16[96,768]{1,0:T(8,128)(2,1)S(1)}, u32[]{:S(2)}, u32[]{:S(2)}) collective-permute-start(bf16[96,768]{1,0:T(8,128)(2,1)S(1)} %far_back.1.refs_4_), channel_id=1, source_target_pairs={{0,2},{1,3},{2,0},{3,1},{4,6},{5,7},{6,4},{7,5},{8,10},{9,11},{10,... | collective-permute-start | bytes 442376 | tf_op jit(solution)/shard_map/ppermute | solution.py:56
  146.5 6.5 %collective-permute-start.36 = (bf16[192,384]{1,0:T(8,128)(2,1)S(1)}, bf16[192,384]{1,0:T(8,128)(2,1)S(1)}, u32[]{:S(2)}, u32[]{:S(2)}) collective-permute-start(bf16[192,384]{1,0:T(8,128)(2,1)S(1)} %get-tuple-element.170), channel_id=1, source_target_pairs={{0,8},{1,9},{2,10},{3,11},{4,12},{5,13},{6,14},{7,15},{8,0},{9,1},... | collective-permute-start | bytes 442376 | tf_op jit(solution)/shard_map/ppermute | solution.py:56
  149.9 23.3 %collective-permute-start.42 = (bf16[256,768]{1,0:T(8,128)(2,1)S(1)}, bf16[256,768]{1,0:T(8,128)(2,1)S(1)}, u32[]{:S(2)}, u32[]{:S(2)}) collective-permute-start(bf16[256,768]{1,0:T(8,128)(2,1)S(1)} %near.1.refs_2_), channel_id=1, source_target_pairs={{0,1},{1,0},{2,3},{3,2},{4,5},{5,4},{6,7},{7,6},{8,9},{9,8},{10,11... | collective-permute-start | bytes 1179656 | tf_op jit(solution)/shard_map/ppermute | solution.py:56
  153.4 19.7 %collective-permute-start.40 = (bf16[208,768]{1,0:T(8,128)(2,1)S(1)}, bf16[208,768]{1,0:T(8,128)(2,1)S(1)}, u32[]{:S(2)}, u32[]{:S(2)}) collective-permute-start(bf16[208,768]{1,0:T(8,128)(2,1)S(1)} %qkv_three.1.refs_2_.refs_0_), channel_id=1, source_target_pairs={{0,2},{1,3},{2,0},{3,1},{4,6},{5,7},{6,4},{7,5},{8,10},{9,11},{10,... | collective-permute-start | bytes 958472 | tf_op jit(solution)/shard_map/ppermute | solution.py:56
  155.3 17.8 %collective-permute-start.41 = (bf16[2,96,768]{2,1,0:T(8,128)(2,1)S(1)}, bf16[2,96,768]{2,1,0:T(8,128)(2,1)S(1)}, u32[]{:S(2)}, u32[]{:S(2)}) collective-permute-start(bf16[2,96,768]{2,1,0:T(8,128)(2,1)S(1)} %get-tuple-element.173), channel_id=1, source_target_pairs={{0,1},{1,0},{2,3},{3,2},{4,5},{5,4},{6,7},{7,6},{8,9},{9,8},{10,11... | collective-permute-start | bytes 884744 | tf_op jit(solution)/shard_map/ppermute | solution.py:56
  173.3 8.1 %collective-permute-start.43 = (bf16[208,768]{1,0:T(8,128)(2,1)S(1)}, bf16[208,768]{1,0:T(8,128)(2,1)S(1)}, u32[]{:S(2)}, u32[]{:S(2)}) collective-permute-start(bf16[208,768]{1,0:T(8,128)(2,1)S(1)} %qkv_four.1.refs_0_), channel_id=1, source_target_pairs={{0,1},{1,0},{2,3},{3,2},{4,5},{5,4},{6,7},{7,6},{8,9},{9,8},{10,11... | collective-permute-start | bytes 958472 | tf_op jit(solution)/shard_map/ppermute | solution.py:56
  175.0 5.9 %collective-permute-start.44 = (bf16[192,768]{1,0:T(8,128)(2,1)S(1)}, bf16[192,768]{1,0:T(8,128)(2,1)S(1)}, u32[]{:S(2)}, u32[]{:S(2)}) collective-permute-start(bf16[192,768]{1,0:T(8,128)(2,1)S(1)} %slice.14), channel_id=1, source_target_pairs={{0,8},{1,9},{2,10},{3,11},{4,12},{5,13},{6,14},{7,15},{8,0},{9,1},... | collective-permute-start | bytes 884744 | tf_op jit(solution)/shard_map/ppermute | solution.py:56
  175.3 6.1 %collective-permute-start.48 = (bf16[96,768]{1,0:T(8,128)(2,1)S(1)}, bf16[96,768]{1,0:T(8,128)(2,1)S(1)}, u32[]{:S(2)}, u32[]{:S(2)}) collective-permute-start(bf16[96,768]{1,0:T(8,128)(2,1)S(1)} %far_in.1.refs_2_), channel_id=1, source_target_pairs={{0,2},{1,3},{2,0},{3,1},{4,6},{5,7},{6,4},{7,5},{8,10},{9,11},{10,... | collective-permute-start | bytes 442376 | tf_op jit(solution)/shard_map/ppermute | solution.py:56
  181.5 12.7 %collective-permute-start.50 = (bf16[2,96,768]{2,1,0:T(8,128)(2,1)S(1)}, bf16[2,96,768]{2,1,0:T(8,128)(2,1)S(1)}, u32[]{:S(2)}, u32[]{:S(2)}) collective-permute-start(bf16[2,96,768]{2,1,0:T(8,128)(2,1)S(1)} %last.1.refs_0_.refs_5_), channel_id=1, source_target_pairs={{0,16},{1,17},{2,18},{3,19},{4,20},{5,21},{6,22},{7,23},{8,24},{9,... | collective-permute-start | bytes 884744 | tf_op jit(solution)/shard_map/ppermute | solution.py:56
  183.4 17.1 %collective-permute-start.47 = (bf16[288,768]{1,0:T(8,128)(2,1)S(1)}, bf16[288,768]{1,0:T(8,128)(2,1)S(1)}, u32[]{:S(2)}, u32[]{:S(2)}) collective-permute-start(bf16[288,768]{1,0:T(8,128)(2,1)S(1)} %get-tuple-element.175), channel_id=1, source_target_pairs={{0,16},{1,17},{2,18},{3,19},{4,20},{5,21},{6,22},{7,23},{8,24},{9,... | collective-permute-start | bytes 1327112 | tf_op jit(solution)/shard_map/ppermute | solution.py:56
  183.4 18.3 %collective-permute-start.46 = (bf16[288,768]{1,0:T(8,128)(2,1)S(1)}, bf16[288,768]{1,0:T(8,128)(2,1)S(1)}, u32[]{:S(2)}, u32[]{:S(2)}) collective-permute-start(bf16[288,768]{1,0:T(8,128)(2,1)S(1)} %get-tuple-element.174.refs_6_.refs_2_), channel_id=1, source_target_pairs={{0,8},{1,9},{2,10},{3,11},{4,12},{5,13},{6,14},{7,15},{8,0},{9,1},... | collective-permute-start | bytes 1327112 | tf_op jit(solution)/shard_map/ppermute | solution.py:56
  184.1 15.9 %collective-permute-start.49 = (bf16[2,96,768]{2,1,0:T(8,128)(2,1)S(1)}, bf16[2,96,768]{2,1,0:T(8,128)(2,1)S(1)}, u32[]{:S(2)}, u32[]{:S(2)}) collective-permute-start(bf16[2,96,768]{2,1,0:T(8,128)(2,1)S(1)} %last.1.refs_0_.refs_5_), channel_id=1, source_target_pairs={{0,8},{1,9},{2,10},{3,11},{4,12},{5,13},{6,14},{7,15},{8,0},{9,1},... | collective-permute-start | bytes 884744 | tf_op jit(solution)/shard_map/ppermute | solution.py:56
  185.1 23.0 %collective-permute-start.55 = (bf16[256,768]{1,0:T(8,128)(2,1)S(1)}, bf16[256,768]{1,0:T(8,128)(2,1)S(1)}, u32[]{:S(2)}, u32[]{:S(2)}) collective-permute-start(bf16[256,768]{1,0:T(8,128)(2,1)S(1)} %get-tuple-element.182), channel_id=1, source_target_pairs={{0,0},{1,1},{2,4},{3,5},{4,2},{5,3},{6,6},{7,7},{8,8},{9,9},{10,12... | collective-permute-start | bytes 1179656 | tf_op jit(solution)/shard_map/ppermute | solution.py:67
  194.2 18.1 %collective-permute-start.56 = (bf16[256,768]{1,0:T(8,128)(2,1)S(1)}, bf16[256,768]{1,0:T(8,128)(2,1)S(1)}, u32[]{:S(2)}, u32[]{:S(2)}) collective-permute-start(bf16[256,768]{1,0:T(8,128)(2,1)S(1)} %get-tuple-element.183), channel_id=1, source_target_pairs={{0,0},{1,1},{2,4},{3,5},{4,2},{5,3},{6,6},{7,7},{8,8},{9,9},{10,12... | collective-permute-start | bytes 1179656 | tf_op jit(solution)/shard_map/ppermute | solution.py:67
  201.8 10.6 %collective-permute-start.51 = (bf16[96,768]{1,0:T(8,128)(2,1)S(1)}, bf16[96,768]{1,0:T(8,128)(2,1)S(1)}, u32[]{:S(2)}, u32[]{:S(2)}) collective-permute-start(bf16[96,768]{1,0:T(8,128)(2,1)S(1)} %get-tuple-element.177), channel_id=1, source_target_pairs={{0,8},{1,9},{2,10},{3,11},{4,12},{5,13},{6,14},{7,15},{8,0},{9,1},... | collective-permute-start | bytes 442376 | tf_op jit(solution)/shard_map/ppermute | solution.py:56
  204.0 8.3 %collective-permute-start.52 = (bf16[96,768]{1,0:T(8,128)(2,1)S(1)}, bf16[96,768]{1,0:T(8,128)(2,1)S(1)}, u32[]{:S(2)}, u32[]{:S(2)}) collective-permute-start(bf16[96,768]{1,0:T(8,128)(2,1)S(1)} %get-tuple-element.178), channel_id=1, source_target_pairs={{0,16},{1,17},{2,18},{3,19},{4,20},{5,21},{6,22},{7,23},{8,24},{9,... | collective-permute-start | bytes 442376 | tf_op jit(solution)/shard_map/ppermute | solution.py:56
  212.5 6.9 %collective-permute-start.57 = (bf16[1552,768]{1,0:T(8,128)(2,1)S(1)}, bf16[1552,768]{1,0:T(8,128)(2,1)S(1)}, u32[]{:S(2)}, u32[]{:S(2)}) collective-permute-start(bf16[1552,768]{1,0:T(8,128)(2,1)S(1)} %join_l.1.c_ref), channel_id=1, source_target_pairs={{0,4},{1,5},{2,6},{3,7},{4,0},{5,1},{6,2},{7,3},{8,12},{9,13},{10,... | collective-permute-start | bytes 7151624 | tf_op jit(solution)/shard_map/ppermute | solution.py:56
  213.5 5.9 %collective-permute-start.58 = (bf16[8,96,768]{2,1,0:T(8,128)(2,1)S(1)}, bf16[8,96,768]{2,1,0:T(8,128)(2,1)S(1)}, u32[]{:S(2)}, u32[]{:S(2)}) collective-permute-start(bf16[8,96,768]{2,1,0:T(8,128)(2,1)S(1)} %join_f.1.refs_8_.f_ref), channel_id=1, source_target_pairs={{0,4},{1,5},{2,6},{3,7},{4,0},{5,1},{6,2},{7,3},{8,12},{9,13},{10,... | collective-permute-start | bytes 3538952 | tf_op jit(solution)/shard_map/ppermute | solution.py:56
  (34 other events, 184.5 us)

commit v4 on v3

--- a/solution.py
+++ b/solution.py
@@ -422,6 +422,9 @@
     keep_ref[...] = mm_nt(all_scr[:half, :], w_ref[...]).astype(bf16)
 
 
+AT_ONCE = 2
+
+
 def final_kernel(info, c_ref, c_other, f_ref, f_other, low_tokens, low_out, *rest):
     qkv_out, out_out, w_in_out, w_back_out, layer_out, token_out = rest[:6]
     vec_outs, (all_scr, flip_scr, out_scr, back_scr) = rest[6:15], rest[15:]
@@ -459,15 +462,18 @@
         out_scr[...] = flip_scr[...].T
         flip_scr[...] = back_scr[...].T
 
-    rows = pl.ds(pl.multiple_of(block * SLICE, SLICE), SLICE)
-    pieces = [piece(group, block) for group in range(TP)]
-    for kind in range(3):
-        cols = slice(kind * GROUP_WIDTH, (kind + 1) * GROUP_WIDTH)
-        joined = jnp.concatenate([part[:, cols] for part in pieces], axis=1)
-        qkv_out[:, kind * WIDTH : (kind + 1) * WIDTH] = joined.astype(f32)
+    for n in range(AT_ONCE):
+        here_block = block * AT_ONCE + n
+        rows = slice(n * SLICE, (n + 1) * SLICE)
+        pieces = [piece(group, here_block) for group in range(TP)]
+        for kind in range(3):
+            cols = slice(kind * GROUP_WIDTH, (kind + 1) * GROUP_WIDTH)
+            joined = jnp.concatenate([part[:, cols] for part in pieces], axis=1)
+            qkv_out[rows, kind * WIDTH : (kind + 1) * WIDTH] = joined.astype(f32)
+        w_in_out[rows, :] = ffn_piece(here_block, 0)
+    rows = pl.ds(pl.multiple_of(block * AT_ONCE * SLICE, SLICE), AT_ONCE * SLICE)
     out_out[...] = out_scr[rows, :]
     w_back_out[...] = flip_scr[rows, :]
-    w_in_out[...] = ffn_piece(block, 0)
     layer_out[...] = low_out[...]
     token_out[...] = low_tokens[...]
 
@@ -701,7 +707,7 @@
     core_tokens = hop(own_tokens, CORE, 0)
     far_tokens = hop(near_tokens, CORE, 0)
     part_one = step(
-        join_kernel, "pair", [(2 * PIECE, WIDTH)], piece_one, piece_two, deps=(own_tokens, w_group)
+        join_kernel, "pair", [(2 * PIECE, WIDTH)], piece_one, piece_two, deps=(own_tokens, w_group, random_other)
     )
     x_one = hop(part_one, X_BIT, 0)
     y_one = hop(part_one, Y_BIT, 0)
@@ -1003,12 +1009,13 @@
         deps=(f_all, token_grads, layer_out),
     )
     whole = pl.BlockSpec(memory_space=pltpu.VMEM)
-    piece_rows = QUARTER // SLOTS
+    piece_rows = QUARTER // SLOTS * AT_ONCE
+    block_rows = SLICE * AT_ONCE
     by_rows = lambda rows, cols: pl.BlockSpec((rows, cols), lambda i: (i, 0))
     square = ((WIDTH, WIDTH), f32)
     grad_w_qkv, grad_w_out, grad_w_in, grad_w_back, layer_out, grad_tokens, *vec_outs = pl.pallas_call(
         final_kernel,
-        grid=(SLOTS,),
+        grid=(SLOTS // AT_ONCE,),
         out_shape=[
             jax.ShapeDtypeStruct(shape, dtype)
             for shape, dtype in [((WIDTH, 3 * WIDTH), f32), square, square, square, rows, rows]
@@ -1017,8 +1024,8 @@
         in_specs=[SMEM]
         + [whole] * 4
         + [by_rows(piece_rows, WIDTH)] * 2,
-        out_specs=[by_rows(SLICE, 3 * WIDTH)]
-        + [by_rows(SLICE, WIDTH)] * 3
+        out_specs=[by_rows(block_rows, 3 * WIDTH)]
+        + [by_rows(block_rows, WIDTH)] * 3
         + [by_rows(piece_rows, WIDTH)] * 2
         + [pl.BlockSpec((WIDTH,), lambda i: (0,))] * 9,
         scratch_shapes=[pltpu.VMEM((32, SLICE, WIDTH), bf16)] + [pltpu.VMEM((WIDTH, WIDTH), f32)] * 3,

time: 231 us -> 224 us (0.970)
  Pallas kernels: 61.4 us -> 56.3 us
    pallas_call x37, Pallas kernels: 53.7 us -> 49 us  [call(): return lambda *arrays: run(*arrays, *deps)]
    unnamed x47 -> x37, local copies, waits for them, and re-layouts: 6.14 us -> 5.45 us
  transfers between devices with their start and end apart: 59 -> 59, of which waited for: 24 -> 23; matrix products, arithmetic and copies ran while one was open for 1% -> 0% of each run, Pallas kernels for 19% -> 18%
where the time goes in v4:
time: 224 us; the launch traced here: 220 us
  waiting for transfers between devices  85 us (38%)
  starting transfers between devices  71 us (32%)
  Pallas kernels  56.3 us (25%)
  local copies, waits for them, and re-layouts  5.77 us (3%)
    ppermute x55, waiting for transfers between devices, hop(): return lax.ppermute(array, ('dp', 'tp'), pairs)  77.8 us
    pallas_call x37, Pallas kernels, call(): return lambda *arrays: run(*arrays, *deps)  49 us
    ppermute x55, starting transfers between devices, hop(): return lax.ppermute(array, ('dp', 'tp'), pairs)  46.9 us
    ppermute x4, starting transfers between devices, place(): return lax.ppermute(array, ('dp', 'tp'), pairs)  24.2 us
    pallas_call x1, Pallas kernels, per_device(): pl.pallas_call(final_kernel, grid=(SLOTS // AT_ONCE,), out_shape=[jax.Sha...  7.32 us
    ppermute x4, waiting for transfers between devices, place(): return lax.ppermute(array, ('dp', 'tp'), pairs)  7.15 us
    unnamed x37, local copies, waits for them, and re-layouts  5.45 us
  transfers between devices with their start and end apart: 59, of which 23 were waited for; matrix products, arithmetic and copies ran while one was open for 0% of the time, Pallas kernels for 18%

profile of v4, /device:TPU:1, one launch (start us, length us, event | category | flops | bytes accessed | tf_op | source)
XLA Modules:
  0.0 219.6 jit_solution(3892946979668474780)
XLA Ops:
  0.7 5.7 %collective-permute-start = (bf16[256,768]{1,0:T(8,128)(2,1)}, bf16[256,768]{1,0:T(8,128)(2,1)S(1)}, u32[]{:S(2)}, u32[]{:S(2)}) collective-permute-start(bf16[256,768]{1,0:T(8,128)(2,1)} %bitcast.11), channel_id=1, source_target_pairs={{0,0},{1,1},{2,4},{3,5},{4,2},{5,3},{6,6},{7,7},{8,8},{9,9},{10,12... | collective-permute-start | bytes 1179656 | tf_op jit(solution)/shard_map/ppermute | solution.py:67
  6.5 1.3 copy-done
  7.8 1.3 copy-done.2
  11.0 1.4 collective-permute-start.5
  13.3 2.0 copy-done.4
  16.2 11.1 %collective-permute-done.6.refs_1_ = bf16[208,768]{1,0:T(8,128)(2,1)S(1)} collective-permute-done((bf16[208,768]{1,0:T(8,128)(2,1)S(1)}, bf16[208,768]{1,0:T(8,128)(2,1)S(1)}, u32[]{:S(2)}, u32[]{:S(2)}) %collective-permute-start.6) | collective-permute-done | bytes 319520 | tf_op jit(solution)/shard_map/ppermute | solution.py:56
  27.4 1.3 collective-permute-start.8
  29.9 3.1 %collective-permute-start.1 = (bf16[256,768]{1,0:T(8,128)(2,1)S(1)}, bf16[256,768]{1,0:T(8,128)(2,1)S(1)}, u32[]{:S(2)}, u32[]{:S(2)}) collective-permute-start(bf16[256,768]{1,0:T(8,128)(2,1)S(1)} %collective-permute-done.refs_2_.refs_3_.refs_0_.refs_1_), channel_id=1, source_target_pairs={{0,1},{1,0},{2,3},{3,2},{4,5},{5,4},{6,7},{7,6},{8,9},{9,8},{10,11... | collective-permute-start | bytes 1179656 | tf_op jit(solution)/shard_map/ppermute | solution.py:56
  33.0 14.5 %collective-permute-done.9.refs_2_.refs_3_ = bf16[208,768]{1,0:T(8,128)(2,1)S(1)} collective-permute-done((bf16[208,768]{1,0:T(8,128)(2,1)S(1)}, bf16[208,768]{1,0:T(8,128)(2,1)S(1)}, u32[]{:S(2)}, u32[]{:S(2)}) %collective-permute-start.9) | collective-permute-done | bytes 319520 | tf_op jit(solution)/shard_map/ppermute | solution.py:56
  48.2 2.9 %collective-permute-start.2 = (bf16[256,768]{1,0:T(8,128)(2,1)S(1)}, bf16[256,768]{1,0:T(8,128)(2,1)S(1)}, u32[]{:S(2)}, u32[]{:S(2)}) collective-permute-start(bf16[256,768]{1,0:T(8,128)(2,1)S(1)} %collective-permute-done.refs_2_.refs_3_.refs_0_.refs_1_), channel_id=1, source_target_pairs={{0,4},{1,5},{2,6},{3,7},{4,0},{5,1},{6,2},{7,3},{8,12},{9,13},{10,... | collective-permute-start | bytes 1179656 | tf_op jit(solution)/shard_map/ppermute | solution.py:56
  51.1 3.8 %collective-permute-start.14 = (bf16[256,768]{1,0:T(8,128)(2,1)S(1)}, bf16[256,768]{1,0:T(8,128)(2,1)S(1)}, u32[]{:S(2)}, u32[]{:S(2)}) collective-permute-start(bf16[256,768]{1,0:T(8,128)(2,1)S(1)} %bitcast.12), channel_id=1, source_target_pairs={{0,0},{1,1},{2,4},{3,5},{4,2},{5,3},{6,6},{7,7},{8,8},{9,9},{10,12... | collective-permute-start | bytes 1179656 | tf_op jit(solution)/shard_map/ppermute | solution.py:67
  54.9 10.3 %attention.1 = (bf16[384,128]{1,0:T(8,128)(2,1)S(1)}, bf16[768,128]{1,0:T(8,128)(2,1)S(1)}, bf16[384,128]{1,0:T(8,128)(2,1)S(1)}, bf16[1024,64]{1,0:T(8,128)(2,1...) custom-call(s32[5]{0:T(128)S(1)} %stack.27.refs_0_.info, ...), custom_call_target="tpu_custom_call" | custom-call | flops 1 | bytes 1 | tf_op jit(solution)/shard_map/attention/pallas_call | solution.py:647
  65.4 1.3 collective-permute-done.13.refs_6_.refs_4_
  68.4 1.2 collective-permute-start.17
  69.6 3.6 %collective-permute-done.10.refs_4_.refs_3_ = bf16[768,128]{1,0:T(8,128)(2,1)S(1)} collective-permute-done((bf16[768,128]{1,0:T(8,128)(2,1)S(1)}, bf16[768,128]{1,0:T(8,128)(2,1)S(1)}, u32[]{:S(2)}, u32[]{:S(2)}) %collective-permute-start.10) | collective-permute-done | bytes 196640 | tf_op jit(solution)/shard_map/ppermute | solution.py:56
  73.8 1.2 collective-permute-start.19
  77.5 6.3 %ffn.1 = (bf16[256,768]{1,0:T(8,128)(2,1)S(1)}, f32[256,768]{1,0:T(8,128)S(1)}, f32[256,768]{1,0:T(8,128)S(1)}, bf16[256,768]{1,0:T(8,128)(2,1)S(1)}, bf16[256,7...) custom-call(s32[5]{0:T(128)S(1)} %stack.27.refs_0_.info, ...), custom_call_target="tpu_custom_call" | custom-call | flops 1 | bytes 1 | tf_op jit(solution)/shard_map/ffn/pallas_call | solution.py:647
  83.8 2.0 back_grads.1
  86.3 5.6 %ffn_back.1 = (bf16[384,128]{1,0:T(8,128)(2,1)S(1)}, bf16[768,128]{1,0:T(8,128)(2,1)S(1)}, bf16[384,128]{1,0:T(8,128)(2,1)S(1)}, f32[256,768]{1,0:T(8,128)S(1)},...) custom-call(s32[5]{0:T(128)S(1)} %stack.27.refs_0_.info, ...), custom_call_target="tpu_custom_call" | custom-call | flops 1 | bytes 1 | tf_op jit(solution)/shard_map/ffn_back/pallas_call | solution.py:647
  92.8 1.3 collective-permute-start.27
  95.8 5.3 %collective-permute-done.20.refs_8_ = bf16[768,128]{1,0:T(8,128)(2,1)S(1)} collective-permute-done((bf16[768,128]{1,0:T(8,128)(2,1)S(1)}, bf16[768,128]{1,0:T(8,128)(2,1)S(1)}, u32[]{:S(2)}, u32[]{:S(2)}) %collective-permute-start.20) | collective-permute-done | bytes 196640 | tf_op jit(solution)/shard_map/ppermute | solution.py:56
  101.0 1.6 collective-permute-start.21
  104.1 4.9 %attention_back_0.1 = (bf16[1024,192]{1,0:T(8,128)(2,1)S(1)}, f32[8,192]{1,0:T(8,128)S(1)}) custom-call(s32[5]{0:T(128)S(1)} %stack.27.refs_0_.info, s32[576]{0:T(1024)S(1)} %reshape.33.refs_1_, s32[576]{0:T(1024)S(1)} %collective-permute-done.4.refs_4_.refs_2_, bf16[1024,64]{1,0:T(8,128)(2,1)S(1)} %get-tuple-element.113.refs_3_, ...), custom_call_target="tpu_custom_call" | custom-call | flops 1 | bytes 1 | tf_op jit(solution)/shard_map/attention_back_0/pallas_call | solution.py:647
  110.7 4.5 %attention_back_1.1 = (bf16[1024,192]{1,0:T(8,128)(2,1)S(1)}, f32[8,192]{1,0:T(8,128)S(1)}) custom-call(s32[5]{0:T(128)S(1)} %stack.27.refs_0_.info, s32[576]{0:T(1024)S(1)} %reshape.33.refs_1_, s32[576]{0:T(1024)S(1)} %collective-permute-done.4.refs_4_.refs_2_, bf16[1024,64]{1,0:T(8,128)(2,1)S(1)} %get-tuple-element.142.refs_3_, ...), custom_call_target="tpu_custom_call" | custom-call | flops 1 | bytes 1 | tf_op jit(solution)/shard_map/attention_back_1/pallas_call | solution.py:647
  115.3 4.5 %attention_back_2.1 = (bf16[1024,192]{1,0:T(8,128)(2,1)S(1)}, f32[8,192]{1,0:T(8,128)S(1)}) custom-call(s32[5]{0:T(128)S(1)} %stack.27.refs_0_.info, s32[576]{0:T(1024)S(1)} %reshape.33.refs_1_, s32[576]{0:T(1024)S(1)} %collective-permute-done.4.refs_4_.refs_2_, bf16[1024,64]{1,0:T(8,128)(2,1)S(1)} %get-tuple-element.150.refs_3_, ...), custom_call_target="tpu_custom_call" | custom-call | flops 1 | bytes 1 | tf_op jit(solution)/shard_map/attention_back_2/pallas_call | solution.py:647
  119.8 2.1 qkv_grads.1
  121.9 1.7 token_grad.1
  123.6 1.7 collective-permute-start.34
  126.8 3.0 %collective-permute-done.32.refs_5_.refs_3_ = bf16[6,96,768]{2,1,0:T(8,128)(2,1)S(1)} collective-permute-done((bf16[6,96,768]{2,1,0:T(8,128)(2,1)S(1)}, bf16[6,96,768]{2,1,0:T(8,128)(2,1)S(1)}, u32[]{:S(2)}, u32[]{:S(2)}) %collective-permute-start.32) | collective-permute-done | bytes 884768 | tf_op jit(solution)/shard_map/ppermute | solution.py:56
  132.8 3.3 %collective-permute-done.33.refs_1_.refs_4_ = bf16[2,96,768]{2,1,0:T(8,128)(2,1)S(1)} collective-permute-done((bf16[2,96,768]{2,1,0:T(8,128)(2,1)S(1)}, bf16[2,96,768]{2,1,0:T(8,128)(2,1)S(1)}, u32[]{:S(2)}, u32[]{:S(2)}) %collective-permute-start.33) | collective-permute-done | bytes 294944 | tf_op jit(solution)/shard_map/ppermute | solution.py:56
  138.0 1.6 collective-permute-start.39
  140.0 3.0 %collective-permute-done.38.refs_5_ = bf16[2,96,768]{2,1,0:T(8,128)(2,1)S(1)} collective-permute-done((bf16[2,96,768]{2,1,0:T(8,128)(2,1)S(1)}, bf16[2,96,768]{2,1,0:T(8,128)(2,1)S(1)}, u32[]{:S(2)}, u32[]{:S(2)}) %collective-permute-start.38) | collective-permute-done | bytes 294944 | tf_op jit(solution)/shard_map/ppermute | solution.py:56
  144.5 1.6 collective-permute-done.36.refs_5_
  146.6 1.9 collective-permute-start.40
  149.0 17.2 %collective-permute-done.41.refs_1_ = bf16[2,96,768]{2,1,0:T(8,128)(2,1)S(1)} collective-permute-done((bf16[2,96,768]{2,1,0:T(8,128)(2,1)S(1)}, bf16[2,96,768]{2,1,0:T(8,128)(2,1)S(1)}, u32[]{:S(2)}, u32[]{:S(2)}) %collective-permute-start.41) | collective-permute-done | bytes 294944 | tf_op jit(solution)/shard_map/ppermute | solution.py:56
  166.5 1.9 collective-permute-start.45
  168.6 2.0 collective-permute-start.48
  170.6 2.0 collective-permute-done.45.refs_1_.refs_3_
  172.6 1.8 collective-permute-done.44.refs_0_.refs_2_
  176.2 1.8 collective-permute-start.46
  178.2 9.2 %collective-permute-start.55 = (bf16[256,768]{1,0:T(8,128)(2,1)S(1)}, bf16[256,768]{1,0:T(8,128)(2,1)S(1)}, u32[]{:S(2)}, u32[]{:S(2)}) collective-permute-start(bf16[256,768]{1,0:T(8,128)(2,1)S(1)} %get-tuple-element.182), channel_id=1, source_target_pairs={{0,0},{1,1},{2,4},{3,5},{4,2},{5,3},{6,6},{7,7},{8,8},{9,9},{10,12... | collective-permute-start | bytes 1179656 | tf_op jit(solution)/shard_map/ppermute | solution.py:67
  187.4 5.5 %collective-permute-start.56 = (bf16[256,768]{1,0:T(8,128)(2,1)S(1)}, bf16[256,768]{1,0:T(8,128)(2,1)S(1)}, u32[]{:S(2)}, u32[]{:S(2)}) collective-permute-start(bf16[256,768]{1,0:T(8,128)(2,1)S(1)} %get-tuple-element.183), channel_id=1, source_target_pairs={{0,0},{1,1},{2,4},{3,5},{4,2},{5,3},{6,6},{7,7},{8,8},{9,9},{10,12... | collective-permute-start | bytes 1179656 | tf_op jit(solution)/shard_map/ppermute | solution.py:67
  194.4 1.4 collective-permute-start.51
  197.0 1.3 collective-permute-start.52
  198.3 2.9 %collective-permute-done.55.refs_9_.low_tokens = bf16[256,768]{1,0:T(8,128)(2,1)S(1)} collective-permute-done((bf16[256,768]{1,0:T(8,128)(2,1)S(1)}, bf16[256,768]{1,0:T(8,128)(2,1)S(1)}, u32[]{:S(2)}, u32[]{:S(2)}) %collective-permute-start.55) | collective-permute-done | bytes 393248 | tf_op jit(solution)/shard_map/ppermute | solution.py:67
  201.3 4.2 %collective-permute-done.56.refs_10_.low_out = bf16[256,768]{1,0:T(8,128)(2,1)S(1)} collective-permute-done((bf16[256,768]{1,0:T(8,128)(2,1)S(1)}, bf16[256,768]{1,0:T(8,128)(2,1)S(1)}, u32[]{:S(2)}, u32[]{:S(2)}) %collective-permute-start.56) | collective-permute-done | bytes 393248 | tf_op jit(solution)/shard_map/ppermute | solution.py:67
  206.3 5.8 %collective-permute-done.58.f_other = bf16[8,96,768]{2,1,0:T(8,128)(2,1)S(1)} collective-permute-done((bf16[8,96,768]{2,1,0:T(8,128)(2,1)S(1)}, bf16[8,96,768]{2,1,0:T(8,128)(2,1)S(1)}, u32[]{:S(2)}, u32[]{:S(2)}) %collective-permute-start.58) | collective-permute-done | bytes 1179680 | tf_op jit(solution)/shard_map/ppermute | solution.py:56
  212.1 7.3 %final.1 = (f32[768,2304]{1,0:T(8,128)}, f32[768,768]{1,0:T(8,128)}, f32[768,768]{1,0:T(8,128)}, f32[768,768]{1,0:T(8,128)}, bf16[256,768]{1,0:T(8,128)(2,1)}, /...) custom-call(s32[5]{0:T(128)S(1)} %stack.27.refs_0_.info, ...), custom_call_target="tpu_custom_call" | custom-call | flops 1 | bytes 1 | tf_op jit(solution)/shard_map/final/pallas_call | solution.py:1016
  (150 shorter events, 31.7 us)
Async XLA Ops:
  0.7 26.7 %collective-permute-start = (bf16[256,768]{1,0:T(8,128)(2,1)}, bf16[256,768]{1,0:T(8,128)(2,1)S(1)}, u32[]{:S(2)}, u32[]{:S(2)}) collective-permute-start(bf16[256,768]{1,0:T(8,128)(2,1)} %bitcast.11), channel_id=1, source_target_pairs={{0,0},{1,1},{2,4},{3,5},{4,2},{5,3},{6,6},{7,7},{8,8},{9,9},{10,12... | collective-permute-start | bytes 1179656 | tf_op jit(solution)/shard_map/ppermute | solution.py:67
  10.9 16.5 %collective-permute-start.6 = (bf16[208,768]{1,0:T(8,128)(2,1)S(1)}, bf16[208,768]{1,0:T(8,128)(2,1)S(1)}, u32[]{:S(2)}, u32[]{:S(2)}) collective-permute-start(bf16[208,768]{1,0:T(8,128)(2,1)S(1)} %piece.1), channel_id=1, source_target_pairs={{0,2},{1,3},{2,0},{3,1},{4,6},{5,7},{6,4},{7,5},{8,10},{9,11},{10,... | collective-permute-start | bytes 958472 | tf_op jit(solution)/shard_map/ppermute | solution.py:56
  11.0 16.4 %collective-permute-start.5 = (bf16[208,768]{1,0:T(8,128)(2,1)S(1)}, bf16[208,768]{1,0:T(8,128)(2,1)S(1)}, u32[]{:S(2)}, u32[]{:S(2)}) collective-permute-start(bf16[208,768]{1,0:T(8,128)(2,1)S(1)} %piece.1), channel_id=1, source_target_pairs={{0,1},{1,0},{2,3},{3,2},{4,5},{5,4},{6,7},{7,6},{8,9},{9,8},{10,11... | collective-permute-start | bytes 958472 | tf_op jit(solution)/shard_map/ppermute | solution.py:56
  27.4 20.2 %collective-permute-start.8 = (bf16[416,768]{1,0:T(8,128)(2,1)S(1)}, bf16[416,768]{1,0:T(8,128)(2,1)S(1)}, u32[]{:S(2)}, u32[]{:S(2)}) collective-permute-start(bf16[416,768]{1,0:T(8,128)(2,1)S(1)} %pair.1.refs_0_), channel_id=1, source_target_pairs={{0,16},{1,17},{2,18},{3,19},{4,20},{5,21},{6,22},{7,23},{8,24},{9,... | collective-permute-start | bytes 1916936 | tf_op jit(solution)/shard_map/ppermute | solution.py:56
  28.7 18.9 %collective-permute-start.7 = (bf16[416,768]{1,0:T(8,128)(2,1)S(1)}, bf16[416,768]{1,0:T(8,128)(2,1)S(1)}, u32[]{:S(2)}, u32[]{:S(2)}) collective-permute-start(bf16[416,768]{1,0:T(8,128)(2,1)S(1)} %pair.1.refs_0_), channel_id=1, source_target_pairs={{0,8},{1,9},{2,10},{3,11},{4,12},{5,13},{6,14},{7,15},{8,0},{9,1},... | collective-permute-start | bytes 1916936 | tf_op jit(solution)/shard_map/ppermute | solution.py:56
  29.9 17.7 %collective-permute-start.1 = (bf16[256,768]{1,0:T(8,128)(2,1)S(1)}, bf16[256,768]{1,0:T(8,128)(2,1)S(1)}, u32[]{:S(2)}, u32[]{:S(2)}) collective-permute-start(bf16[256,768]{1,0:T(8,128)(2,1)S(1)} %collective-permute-done.refs_2_.refs_3_.refs_0_.refs_1_), channel_id=1, source_target_pairs={{0,1},{1,0},{2,3},{3,2},{4,5},{5,4},{6,7},{7,6},{8,9},{9,8},{10,11... | collective-permute-start | bytes 1179656 | tf_op jit(solution)/shard_map/ppermute | solution.py:56
  33.0 14.6 %collective-permute-start.9 = (bf16[208,768]{1,0:T(8,128)(2,1)S(1)}, bf16[208,768]{1,0:T(8,128)(2,1)S(1)}, u32[]{:S(2)}, u32[]{:S(2)}) collective-permute-start(bf16[208,768]{1,0:T(8,128)(2,1)S(1)} %collective-permute-done.6.refs_1_), channel_id=1, source_target_pairs={{0,1},{1,0},{2,3},{3,2},{4,5},{5,4},{6,7},{7,6},{8,9},{9,8},{10,11... | collective-permute-start | bytes 958472 | tf_op jit(solution)/shard_map/ppermute | solution.py:56
  47.7 19.0 %collective-permute-start.11 = (bf16[432,768]{1,0:T(8,128)(2,1)S(1)}, bf16[432,768]{1,0:T(8,128)(2,1)S(1)}, u32[]{:S(2)}, u32[]{:S(2)}) collective-permute-start(bf16[432,768]{1,0:T(8,128)(2,1)S(1)} %get-tuple-element.109.refs_9_), channel_id=1, source_target_pairs={{0,8},{1,9},{2,10},{3,11},{4,12},{5,13},{6,14},{7,15},{8,0},{9,1},... | collective-permute-start | bytes 1990664 | tf_op jit(solution)/shard_map/ppermute | solution.py:56
  48.0 18.6 %collective-permute-start.12 = (bf16[400,768]{1,0:T(8,128)(2,1)S(1)}, bf16[400,768]{1,0:T(8,128)(2,1)S(1)}, u32[]{:S(2)}, u32[]{:S(2)}) collective-permute-start(bf16[400,768]{1,0:T(8,128)(2,1)S(1)} %get-tuple-element.111), channel_id=1, source_target_pairs={{0,16},{1,17},{2,18},{3,19},{4,20},{5,21},{6,22},{7,23},{8,24},{9,... | collective-permute-start | bytes 1843208 | tf_op jit(solution)/shard_map/ppermute | solution.py:56
  48.2 6.7 %collective-permute-start.2 = (bf16[256,768]{1,0:T(8,128)(2,1)S(1)}, bf16[256,768]{1,0:T(8,128)(2,1)S(1)}, u32[]{:S(2)}, u32[]{:S(2)}) collective-permute-start(bf16[256,768]{1,0:T(8,128)(2,1)S(1)} %collective-permute-done.refs_2_.refs_3_.refs_0_.refs_1_), channel_id=1, source_target_pairs={{0,4},{1,5},{2,6},{3,7},{4,0},{5,1},{6,2},{7,3},{8,12},{9,13},{10,... | collective-permute-start | bytes 1179656 | tf_op jit(solution)/shard_map/ppermute | solution.py:56
  51.1 14.2 %collective-permute-start.14 = (bf16[256,768]{1,0:T(8,128)(2,1)S(1)}, bf16[256,768]{1,0:T(8,128)(2,1)S(1)}, u32[]{:S(2)}, u32[]{:S(2)}) collective-permute-start(bf16[256,768]{1,0:T(8,128)(2,1)S(1)} %bitcast.12), channel_id=1, source_target_pairs={{0,0},{1,1},{2,4},{3,5},{4,2},{5,3},{6,6},{7,7},{8,8},{9,9},{10,12... | collective-permute-start | bytes 1179656 | tf_op jit(solution)/shard_map/ppermute | solution.py:67
  66.9 9.4 %collective-permute-start.16 = (bf16[2288,768]{1,0:T(8,128)(2,1)S(1)}, bf16[2288,768]{1,0:T(8,128)(2,1)S(1)}, u32[]{:S(2)}, u32[]{:S(2)}) collective-permute-start(bf16[2288,768]{1,0:T(8,128)(2,1)S(1)} %held.1.refs_5_.refs_1_), channel_id=1, source_target_pairs={{0,4},{1,5},{2,6},{3,7},{4,0},{5,1},{6,2},{7,3},{8,12},{9,13},{10,... | collective-permute-start | bytes 10543112 | tf_op jit(solution)/shard_map/ppermute | solution.py:56
  67.1 6.1 %collective-permute-start.10 = (bf16[768,128]{1,0:T(8,128)(2,1)S(1)}, bf16[768,128]{1,0:T(8,128)(2,1)S(1)}, u32[]{:S(2)}, u32[]{:S(2)}) collective-permute-start(bf16[768,128]{1,0:T(8,128)(2,1)S(1)} %get-tuple-element.110), channel_id=1, source_target_pairs={{0,1},{1,0},{2,3},{3,2},{4,5},{5,4},{6,7},{7,6},{8,9},{9,8},{10,11... | collective-permute-start | bytes 589832 | tf_op jit(solution)/shard_map/ppermute | solution.py:56
  67.6 6.1 %collective-permute-start.18 = (bf16[112,768]{1,0:T(8,128)(2,1)S(1)}, bf16[112,768]{1,0:T(8,128)(2,1)S(1)}, u32[]{:S(2)}, u32[]{:S(2)}) collective-permute-start(bf16[112,768]{1,0:T(8,128)(2,1)S(1)} %get-tuple-element.119), channel_id=1, source_target_pairs={{0,8},{1,9},{2,10},{3,11},{4,12},{5,13},{6,14},{7,15},{8,0},{9,1},... | collective-permute-start | bytes 516104 | tf_op jit(solution)/shard_map/ppermute | solution.py:56
  85.8 6.7 %collective-permute-start.24 = (bf16[2,4,2,96,768]{4,3,2,1,0:T(8,128)(2,1)S(1)}, bf16[2,4,2,96,768]{4,3,2,1,0:T(8,128)(2,1)S(1)}, u32[]{:S(2)}, u32[]{:S(2)}) collective-permute-start(bf16[2,4,2,96,768]{4,3,2,1,0:T(8,128)(2,1)S(1)} %get-tuple-element.139), channel_id=1, source_target_pairs={{0,4},{1,5},{2,6},{3,7},{4,0},{5,1},{6,2},{7,3},{8,12},{9,13},{10,... | collective-permute-start | bytes 7077896 | tf_op jit(solution)/shard_map/ppermute | solution.py:56
  91.9 17.0 %collective-permute-start.25 = (bf16[2,4,2,96,768]{4,3,2,1,0:T(8,128)(2,1)S(1)}, bf16[2,4,2,96,768]{4,3,2,1,0:T(8,128)(2,1)S(1)}, u32[]{:S(2)}, u32[]{:S(2)}) collective-permute-start(bf16[2,4,2,96,768]{4,3,2,1,0:T(8,128)(2,1)S(1)} %get-tuple-element.146), channel_id=1, source_target_pairs={{0,4},{1,5},{2,6},{3,7},{4,0},{5,1},{6,2},{7,3},{8,12},{9,13},{10,... | collective-permute-start | bytes 7077896 | tf_op jit(solution)/shard_map/ppermute | solution.py:56
  92.1 10.5 %collective-permute-start.23 = (bf16[768,384]{1,0:T(8,128)(2,1)S(1)}, bf16[768,384]{1,0:T(8,128)(2,1)S(1)}, u32[]{:S(2)}, u32[]{:S(2)}) collective-permute-start(bf16[768,384]{1,0:T(8,128)(2,1)S(1)} %get-tuple-element.137), channel_id=1, source_target_pairs={{0,4},{1,5},{2,6},{3,7},{4,0},{5,1},{6,2},{7,3},{8,12},{9,13},{10,... | collective-permute-start | bytes 1769480 | tf_op jit(solution)/shard_map/ppermute | solution.py:56
  92.8 16.2 %collective-permute-start.27 = (bf16[2,2,96,768]{3,2,1,0:T(8,128)(2,1)S(1)}, bf16[2,2,96,768]{3,2,1,0:T(8,128)(2,1)S(1)}, u32[]{:S(2)}, u32[]{:S(2)}) collective-permute-start(bf16[2,2,96,768]{3,2,1,0:T(8,128)(2,1)S(1)} %get-tuple-element.147), channel_id=1, source_target_pairs={{0,16},{1,17},{2,18},{3,19},{4,20},{5,21},{6,22},{7,23},{8,24},{9,... | collective-permute-start | bytes 1769480 | tf_op jit(solution)/shard_map/ppermute | solution.py:56
  94.1 14.9 %collective-permute-start.26 = (bf16[2,2,96,768]{3,2,1,0:T(8,128)(2,1)S(1)}, bf16[2,2,96,768]{3,2,1,0:T(8,128)(2,1)S(1)}, u32[]{:S(2)}, u32[]{:S(2)}) collective-permute-start(bf16[2,2,96,768]{3,2,1,0:T(8,128)(2,1)S(1)} %get-tuple-element.140.refs_12_), channel_id=1, source_target_pairs={{0,8},{1,9},{2,10},{3,11},{4,12},{5,13},{6,14},{7,15},{8,0},{9,1},... | collective-permute-start | bytes 1769480 | tf_op jit(solution)/shard_map/ppermute | solution.py:56
  103.6 16.2 %collective-permute-start.28 = (bf16[768,192]{1,0:T(8,128)(2,1)S(1)}, bf16[768,192]{1,0:T(8,128)(2,1)S(1)}, u32[]{:S(2)}, u32[]{:S(2)}) collective-permute-start(bf16[768,192]{1,0:T(8,128)(2,1)S(1)} %get-tuple-element.154), channel_id=1, source_target_pairs={{0,1},{1,0},{2,3},{3,2},{4,5},{5,4},{6,7},{7,6},{8,9},{9,8},{10,11... | collective-permute-start | bytes 884744 | tf_op jit(solution)/shard_map/ppermute | solution.py:56
  109.5 20.4 %collective-permute-start.32 = (bf16[6,96,768]{2,1,0:T(8,128)(2,1)S(1)}, bf16[6,96,768]{2,1,0:T(8,128)(2,1)S(1)}, u32[]{:S(2)}, u32[]{:S(2)}) collective-permute-start(bf16[6,96,768]{2,1,0:T(8,128)(2,1)S(1)} %get-tuple-element.163), channel_id=1, source_target_pairs={{0,16},{1,17},{2,18},{3,19},{4,20},{5,21},{6,22},{7,23},{8,24},{9,... | collective-permute-start | bytes 2654216 | tf_op jit(solution)/shard_map/ppermute | solution.py:56
  109.8 20.1 %collective-permute-start.31 = (bf16[6,96,768]{2,1,0:T(8,128)(2,1)S(1)}, bf16[6,96,768]{2,1,0:T(8,128)(2,1)S(1)}, u32[]{:S(2)}, u32[]{:S(2)}) collective-permute-start(bf16[6,96,768]{2,1,0:T(8,128)(2,1)S(1)} %get-tuple-element.148.refs_11_), channel_id=1, source_target_pairs={{0,8},{1,9},{2,10},{3,11},{4,12},{5,13},{6,14},{7,15},{8,0},{9,1},... | collective-permute-start | bytes 2654216 | tf_op jit(solution)/shard_map/ppermute | solution.py:56
  123.6 7.9 %collective-permute-start.34 = (bf16[512,768]{1,0:T(8,128)(2,1)S(1)}, bf16[512,768]{1,0:T(8,128)(2,1)S(1)}, u32[]{:S(2)}, u32[]{:S(2)}) collective-permute-start(bf16[512,768]{1,0:T(8,128)(2,1)S(1)} %get-tuple-element.167), channel_id=1, source_target_pairs={{0,4},{1,5},{2,6},{3,7},{4,0},{5,1},{6,2},{7,3},{8,12},{9,13},{10,... | collective-permute-start | bytes 2359304 | tf_op jit(solution)/shard_map/ppermute | solution.py:56
  125.3 11.3 %collective-permute-start.29 = (bf16[416,384]{1,0:T(8,128)(2,1)S(1)}, bf16[416,384]{1,0:T(8,128)(2,1)S(1)}, u32[]{:S(2)}, u32[]{:S(2)}) collective-permute-start(bf16[416,384]{1,0:T(8,128)(2,1)S(1)} %get-tuple-element.160), channel_id=1, source_target_pairs={{0,8},{1,9},{2,10},{3,11},{4,12},{5,13},{6,14},{7,15},{8,0},{9,1},... | collective-permute-start | bytes 958472 | tf_op jit(solution)/shard_map/ppermute | solution.py:56
  125.6 11.1 %collective-permute-start.30 = (bf16[416,384]{1,0:T(8,128)(2,1)S(1)}, bf16[416,384]{1,0:T(8,128)(2,1)S(1)}, u32[]{:S(2)}, u32[]{:S(2)}) collective-permute-start(bf16[416,384]{1,0:T(8,128)(2,1)S(1)} %get-tuple-element.162), channel_id=1, source_target_pairs={{0,16},{1,17},{2,18},{3,19},{4,20},{5,21},{6,22},{7,23},{8,24},{9,... | collective-permute-start | bytes 958472 | tf_op jit(solution)/shard_map/ppermute | solution.py:56
  130.2 5.9 %collective-permute-start.33 = (bf16[2,96,768]{2,1,0:T(8,128)(2,1)S(1)}, bf16[2,96,768]{2,1,0:T(8,128)(2,1)S(1)}, u32[]{:S(2)}, u32[]{:S(2)}) collective-permute-start(bf16[2,96,768]{2,1,0:T(8,128)(2,1)S(1)} %get-tuple-element.166), channel_id=1, source_target_pairs={{0,1},{1,0},{2,3},{3,2},{4,5},{5,4},{6,7},{7,6},{8,9},{9,8},{10,11... | collective-permute-start | bytes 884744 | tf_op jit(solution)/shard_map/ppermute | solution.py:56
  131.2 11.7 %collective-permute-start.38 = (bf16[2,96,768]{2,1,0:T(8,128)(2,1)S(1)}, bf16[2,96,768]{2,1,0:T(8,128)(2,1)S(1)}, u32[]{:S(2)}, u32[]{:S(2)}) collective-permute-start(bf16[2,96,768]{2,1,0:T(8,128)(2,1)S(1)} %get-tuple-element.171), channel_id=1, source_target_pairs={{0,8},{1,9},{2,10},{3,11},{4,12},{5,13},{6,14},{7,15},{8,0},{9,1},... | collective-permute-start | bytes 884744 | tf_op jit(solution)/shard_map/ppermute | solution.py:56
  131.6 12.1 %collective-permute-start.37 = (bf16[2,96,768]{2,1,0:T(8,128)(2,1)S(1)}, bf16[2,96,768]{2,1,0:T(8,128)(2,1)S(1)}, u32[]{:S(2)}, u32[]{:S(2)}) collective-permute-start(bf16[2,96,768]{2,1,0:T(8,128)(2,1)S(1)} %get-tuple-element.168.refs_2_), channel_id=1, source_target_pairs={{0,16},{1,17},{2,18},{3,19},{4,20},{5,21},{6,22},{7,23},{8,24},{9,... | collective-permute-start | bytes 884744 | tf_op jit(solution)/shard_map/ppermute | solution.py:56
  136.8 9.7 %collective-permute-start.35 = (bf16[224,384]{1,0:T(8,128)(2,1)S(1)}, bf16[224,384]{1,0:T(8,128)(2,1)S(1)}, u32[]{:S(2)}, u32[]{:S(2)}) collective-permute-start(bf16[224,384]{1,0:T(8,128)(2,1)S(1)} %get-tuple-element.169.refs_6_), channel_id=1, source_target_pairs={{0,16},{1,17},{2,18},{3,19},{4,20},{5,21},{6,22},{7,23},{8,24},{9,... | collective-permute-start | bytes 516104 | tf_op jit(solution)/shard_map/ppermute | solution.py:56
  138.0 6.5 %collective-permute-start.39 = (bf16[96,768]{1,0:T(8,128)(2,1)S(1)}, bf16[96,768]{1,0:T(8,128)(2,1)S(1)}, u32[]{:S(2)}, u32[]{:S(2)}) collective-permute-start(bf16[96,768]{1,0:T(8,128)(2,1)S(1)} %far_back.1.refs_4_), channel_id=1, source_target_pairs={{0,2},{1,3},{2,0},{3,1},{4,6},{5,7},{6,4},{7,5},{8,10},{9,11},{10,... | collective-permute-start | bytes 442376 | tf_op jit(solution)/shard_map/ppermute | solution.py:56
  139.7 6.4 %collective-permute-start.36 = (bf16[192,384]{1,0:T(8,128)(2,1)S(1)}, bf16[192,384]{1,0:T(8,128)(2,1)S(1)}, u32[]{:S(2)}, u32[]{:S(2)}) collective-permute-start(bf16[192,384]{1,0:T(8,128)(2,1)S(1)} %get-tuple-element.170), channel_id=1, source_target_pairs={{0,8},{1,9},{2,10},{3,11},{4,12},{5,13},{6,14},{7,15},{8,0},{9,1},... | collective-permute-start | bytes 442376 | tf_op jit(solution)/shard_map/ppermute | solution.py:56
  143.0 23.4 %collective-permute-start.42 = (bf16[256,768]{1,0:T(8,128)(2,1)S(1)}, bf16[256,768]{1,0:T(8,128)(2,1)S(1)}, u32[]{:S(2)}, u32[]{:S(2)}) collective-permute-start(bf16[256,768]{1,0:T(8,128)(2,1)S(1)} %near.1.refs_2_), channel_id=1, source_target_pairs={{0,1},{1,0},{2,3},{3,2},{4,5},{5,4},{6,7},{7,6},{8,9},{9,8},{10,11... | collective-permute-start | bytes 1179656 | tf_op jit(solution)/shard_map/ppermute | solution.py:56
  146.6 19.7 %collective-permute-start.40 = (bf16[208,768]{1,0:T(8,128)(2,1)S(1)}, bf16[208,768]{1,0:T(8,128)(2,1)S(1)}, u32[]{:S(2)}, u32[]{:S(2)}) collective-permute-start(bf16[208,768]{1,0:T(8,128)(2,1)S(1)} %qkv_three.1.refs_2_.refs_0_), channel_id=1, source_target_pairs={{0,2},{1,3},{2,0},{3,1},{4,6},{5,7},{6,4},{7,5},{8,10},{9,11},{10,... | collective-permute-start | bytes 958472 | tf_op jit(solution)/shard_map/ppermute | solution.py:56
  148.5 17.7 %collective-permute-start.41 = (bf16[2,96,768]{2,1,0:T(8,128)(2,1)S(1)}, bf16[2,96,768]{2,1,0:T(8,128)(2,1)S(1)}, u32[]{:S(2)}, u32[]{:S(2)}) collective-permute-start(bf16[2,96,768]{2,1,0:T(8,128)(2,1)S(1)} %get-tuple-element.173), channel_id=1, source_target_pairs={{0,1},{1,0},{2,3},{3,2},{4,5},{5,4},{6,7},{7,6},{8,9},{9,8},{10,11... | collective-permute-start | bytes 884744 | tf_op jit(solution)/shard_map/ppermute | solution.py:56
  166.4 8.0 %collective-permute-start.43 = (bf16[208,768]{1,0:T(8,128)(2,1)S(1)}, bf16[208,768]{1,0:T(8,128)(2,1)S(1)}, u32[]{:S(2)}, u32[]{:S(2)}) collective-permute-start(bf16[208,768]{1,0:T(8,128)(2,1)S(1)} %qkv_four.1.refs_0_), channel_id=1, source_target_pairs={{0,1},{1,0},{2,3},{3,2},{4,5},{5,4},{6,7},{7,6},{8,9},{9,8},{10,11... | collective-permute-start | bytes 958472 | tf_op jit(solution)/shard_map/ppermute | solution.py:56
  166.5 6.0 %collective-permute-start.45 = (bf16[192,768]{1,0:T(8,128)(2,1)S(1)}, bf16[192,768]{1,0:T(8,128)(2,1)S(1)}, u32[]{:S(2)}, u32[]{:S(2)}) collective-permute-start(bf16[192,768]{1,0:T(8,128)(2,1)S(1)} %slice.14), channel_id=1, source_target_pairs={{0,16},{1,17},{2,18},{3,19},{4,20},{5,21},{6,22},{7,23},{8,24},{9,... | collective-permute-start | bytes 884744 | tf_op jit(solution)/shard_map/ppermute | solution.py:56
  168.5 5.9 %collective-permute-start.44 = (bf16[192,768]{1,0:T(8,128)(2,1)S(1)}, bf16[192,768]{1,0:T(8,128)(2,1)S(1)}, u32[]{:S(2)}, u32[]{:S(2)}) collective-permute-start(bf16[192,768]{1,0:T(8,128)(2,1)S(1)} %slice.14), channel_id=1, source_target_pairs={{0,8},{1,9},{2,10},{3,11},{4,12},{5,13},{6,14},{7,15},{8,0},{9,1},... | collective-permute-start | bytes 884744 | tf_op jit(solution)/shard_map/ppermute | solution.py:56
  168.6 5.9 %collective-permute-start.48 = (bf16[96,768]{1,0:T(8,128)(2,1)S(1)}, bf16[96,768]{1,0:T(8,128)(2,1)S(1)}, u32[]{:S(2)}, u32[]{:S(2)}) collective-permute-start(bf16[96,768]{1,0:T(8,128)(2,1)S(1)} %far_in.1.refs_2_), channel_id=1, source_target_pairs={{0,2},{1,3},{2,0},{3,1},{4,6},{5,7},{6,4},{7,5},{8,10},{9,11},{10,... | collective-permute-start | bytes 442376 | tf_op jit(solution)/shard_map/ppermute | solution.py:56
  174.6 12.8 %collective-permute-start.50 = (bf16[2,96,768]{2,1,0:T(8,128)(2,1)S(1)}, bf16[2,96,768]{2,1,0:T(8,128)(2,1)S(1)}, u32[]{:S(2)}, u32[]{:S(2)}) collective-permute-start(bf16[2,96,768]{2,1,0:T(8,128)(2,1)S(1)} %last.1.refs_0_.refs_5_), channel_id=1, source_target_pairs={{0,16},{1,17},{2,18},{3,19},{4,20},{5,21},{6,22},{7,23},{8,24},{9,... | collective-permute-start | bytes 884744 | tf_op jit(solution)/shard_map/ppermute | solution.py:56
  175.8 18.1 %collective-permute-start.47 = (bf16[288,768]{1,0:T(8,128)(2,1)S(1)}, bf16[288,768]{1,0:T(8,128)(2,1)S(1)}, u32[]{:S(2)}, u32[]{:S(2)}) collective-permute-start(bf16[288,768]{1,0:T(8,128)(2,1)S(1)} %get-tuple-element.175), channel_id=1, source_target_pairs={{0,16},{1,17},{2,18},{3,19},{4,20},{5,21},{6,22},{7,23},{8,24},{9,... | collective-permute-start | bytes 1327112 | tf_op jit(solution)/shard_map/ppermute | solution.py:56
  176.2 18.2 %collective-permute-start.46 = (bf16[288,768]{1,0:T(8,128)(2,1)S(1)}, bf16[288,768]{1,0:T(8,128)(2,1)S(1)}, u32[]{:S(2)}, u32[]{:S(2)}) collective-permute-start(bf16[288,768]{1,0:T(8,128)(2,1)S(1)} %get-tuple-element.174.refs_6_.refs_2_), channel_id=1, source_target_pairs={{0,8},{1,9},{2,10},{3,11},{4,12},{5,13},{6,14},{7,15},{8,0},{9,1},... | collective-permute-start | bytes 1327112 | tf_op jit(solution)/shard_map/ppermute | solution.py:56
  178.0 14.9 %collective-permute-start.49 = (bf16[2,96,768]{2,1,0:T(8,128)(2,1)S(1)}, bf16[2,96,768]{2,1,0:T(8,128)(2,1)S(1)}, u32[]{:S(2)}, u32[]{:S(2)}) collective-permute-start(bf16[2,96,768]{2,1,0:T(8,128)(2,1)S(1)} %last.1.refs_0_.refs_5_), channel_id=1, source_target_pairs={{0,8},{1,9},{2,10},{3,11},{4,12},{5,13},{6,14},{7,15},{8,0},{9,1},... | collective-permute-start | bytes 884744 | tf_op jit(solution)/shard_map/ppermute | solution.py:56
  178.2 23.1 %collective-permute-start.55 = (bf16[256,768]{1,0:T(8,128)(2,1)S(1)}, bf16[256,768]{1,0:T(8,128)(2,1)S(1)}, u32[]{:S(2)}, u32[]{:S(2)}) collective-permute-start(bf16[256,768]{1,0:T(8,128)(2,1)S(1)} %get-tuple-element.182), channel_id=1, source_target_pairs={{0,0},{1,1},{2,4},{3,5},{4,2},{5,3},{6,6},{7,7},{8,8},{9,9},{10,12... | collective-permute-start | bytes 1179656 | tf_op jit(solution)/shard_map/ppermute | solution.py:67
  187.4 18.1 %collective-permute-start.56 = (bf16[256,768]{1,0:T(8,128)(2,1)S(1)}, bf16[256,768]{1,0:T(8,128)(2,1)S(1)}, u32[]{:S(2)}, u32[]{:S(2)}) collective-permute-start(bf16[256,768]{1,0:T(8,128)(2,1)S(1)} %get-tuple-element.183), channel_id=1, source_target_pairs={{0,0},{1,1},{2,4},{3,5},{4,2},{5,3},{6,6},{7,7},{8,8},{9,9},{10,12... | collective-permute-start | bytes 1179656 | tf_op jit(solution)/shard_map/ppermute | solution.py:67
  194.4 11.1 %collective-permute-start.51 = (bf16[96,768]{1,0:T(8,128)(2,1)S(1)}, bf16[96,768]{1,0:T(8,128)(2,1)S(1)}, u32[]{:S(2)}, u32[]{:S(2)}) collective-permute-start(bf16[96,768]{1,0:T(8,128)(2,1)S(1)} %get-tuple-element.177), channel_id=1, source_target_pairs={{0,8},{1,9},{2,10},{3,11},{4,12},{5,13},{6,14},{7,15},{8,0},{9,1},... | collective-permute-start | bytes 442376 | tf_op jit(solution)/shard_map/ppermute | solution.py:56
  197.0 8.5 %collective-permute-start.52 = (bf16[96,768]{1,0:T(8,128)(2,1)S(1)}, bf16[96,768]{1,0:T(8,128)(2,1)S(1)}, u32[]{:S(2)}, u32[]{:S(2)}) collective-permute-start(bf16[96,768]{1,0:T(8,128)(2,1)S(1)} %get-tuple-element.178), channel_id=1, source_target_pairs={{0,16},{1,17},{2,18},{3,19},{4,20},{5,21},{6,22},{7,23},{8,24},{9,... | collective-permute-start | bytes 442376 | tf_op jit(solution)/shard_map/ppermute | solution.py:56
  205.6 6.4 %collective-permute-start.57 = (bf16[1552,768]{1,0:T(8,128)(2,1)S(1)}, bf16[1552,768]{1,0:T(8,128)(2,1)S(1)}, u32[]{:S(2)}, u32[]{:S(2)}) collective-permute-start(bf16[1552,768]{1,0:T(8,128)(2,1)S(1)} %join_l.1.c_ref), channel_id=1, source_target_pairs={{0,4},{1,5},{2,6},{3,7},{4,0},{5,1},{6,2},{7,3},{8,12},{9,13},{10,... | collective-permute-start | bytes 7151624 | tf_op jit(solution)/shard_map/ppermute | solution.py:56
  206.2 5.9 %collective-permute-start.58 = (bf16[8,96,768]{2,1,0:T(8,128)(2,1)S(1)}, bf16[8,96,768]{2,1,0:T(8,128)(2,1)S(1)}, u32[]{:S(2)}, u32[]{:S(2)}) collective-permute-start(bf16[8,96,768]{2,1,0:T(8,128)(2,1)S(1)} %join_f.1.refs_8_.f_ref), channel_id=1, source_target_pairs={{0,4},{1,5},{2,6},{3,7},{4,0},{5,1},{6,2},{7,3},{8,12},{9,13},{10,... | collective-permute-start | bytes 3538952 | tf_op jit(solution)/shard_map/ppermute | solution.py:56
  (29 other events, 137.7 us)
